TPU v7x, 32 devices: a whole 2x2x4 slice. The times are simulated.
32 devices in a mesh: wide: 4 (over y, core), narrow: 8 (over z, x).
Axes of the slice: x: 2, y: 2, z: 4, core: 2. Of those that a mesh axis runs over, the one named last changes fastest.
Arguments:
- tokens: bfloat16 [32768, 384], P(('wide', 'narrow')), may hold values from -6 to 6
- cotangent: bfloat16 [32768, 384], P(('wide', 'narrow')), may hold values from -6 to 6
- routes: int32 [32768, 1], P(('wide', 'narrow')), may hold values from 0 to 31
- images: int32 [32], P(('wide', 'narrow')), may hold values from 0 to 1, as said below
- dense_weight: float32 [384, 1568], P(('wide', 'narrow'))
- dense_moment: float32 [384, 1568], P(('wide', 'narrow'))
- dense_square: float32 [384, 1568], P(('wide', 'narrow'))
- small_params: float32 [10380], replicated
- small_moment: float32 [10380], replicated
- small_square: float32 [10380], replicated
- inner_weight: float32 [32, 384, 1536], P(('wide', 'narrow')), may hold values from -0.3125 to 0.3125
- inner_moment: float32 [32, 384, 1536], P(('wide', 'narrow'))
- inner_square: float32 [32, 384, 1536], P(('wide', 'narrow'))
- outer_weight: float32 [32, 1536, 384], P(('wide', 'narrow')), may hold values from -0.15625 to 0.15625
- outer_moment: float32 [32, 1536, 384], P(('wide', 'narrow'))
- outer_square: float32 [32, 1536, 384], P(('wide', 'narrow'))
- expert_bias: float32 [32, 1920], P(('wide', 'narrow'))
- bias_moment: float32 [32, 1920], P(('wide', 'narrow'))
- bias_square: float32 [32, 1920], P(('wide', 'narrow'))
Outputs:
- layer_out: bfloat16 [32768, 384], P(('wide', 'narrow'))
- input_grad: bfloat16 [32768, 384], P(('wide', 'narrow'))
- dense_next: float32 [384, 1568], P(('wide', 'narrow'))
- dense_first: float32 [384, 1568], P(('wide', 'narrow'))
- dense_second: float32 [384, 1568], P(('wide', 'narrow'))
- small_next: float32 [10380], replicated
- small_first: float32 [10380], replicated
- small_second: float32 [10380], replicated
- inner_next: float32 [32, 384, 1536], P(('wide', 'narrow'))
- inner_first: float32 [32, 384, 1536], P(('wide', 'narrow'))
- inner_second: float32 [32, 384, 1536], P(('wide', 'narrow'))
- inner_copy: bfloat16 [32, 384, 1536], P(('wide', 'narrow'))
- outer_next: float32 [32, 1536, 384], P(('wide', 'narrow'))
- outer_first: float32 [32, 1536, 384], P(('wide', 'narrow'))
- outer_second: float32 [32, 1536, 384], P(('wide', 'narrow'))
- outer_copy: bfloat16 [32, 1536, 384], P(('wide', 'narrow'))
- bias_next: float32 [32, 1920], P(('wide', 'narrow'))
- bias_first: float32 [32, 1920], P(('wide', 'narrow'))
- bias_second: float32 [32, 1920], P(('wide', 'narrow'))
Inputs may be any that keep to these rules, and one draw needn't show every extreme that they name: Device d's first images[d] image slots hold live images; in every draw some device holds 1 and some holds none.
All inputs are finite; a program needn't handle non-finite values.
Results may differ from a plain program's by a relative error of at most 0.013.
The roundings to bfloat16 on the way count: a program that leaves them out, or rounds other values in their place, can miss the bound.
Values may be sent and summed in bfloat16 or wider, within the bound.
No kernel may reach another device: no remote copies, remote signals or barrier semaphores. Data moves between devices by JAX's collectives and lax.ppermute only.
A program may use at most 192 MiB of HBM per device.

v0:
```python
import jax
import jax.numpy as jnp
from jax import lax
from jax.sharding import PartitionSpec as P

MODEL_WIDTH = 384
ATTENTION_HEADS = 12
HEAD_DIM = 32
BIAS_NET_HIDDEN = 512
EXPERTS = 32
SIDE = 8
IMG_TOK = 1024
STEP = 10
WIN = 64


highest = lax.Precision.HIGHEST
beta_one = 0.9
beta_two = 0.999
epsilon = 1e-08
dense_rate = 0.05
expert_rate = 0.05
small_rate = 0.3
weight_decay = 0.05
contract_rows = (((0,), (0,)), ((), ()))
contract_cols = (((1,), (1,)), ((), ()))


def pieces(small_params):
    length_list = (
        MODEL_WIDTH,
        MODEL_WIDTH,
        MODEL_WIDTH,
        MODEL_WIDTH,
        MODEL_WIDTH,
        MODEL_WIDTH,
        MODEL_WIDTH,
        ATTENTION_HEADS,
        BIAS_NET_HIDDEN,
        2 * BIAS_NET_HIDDEN,
        BIAS_NET_HIDDEN * ATTENTION_HEADS,
    )
    piece_collection = []
    offset = 0
    for length in length_list:
        piece_collection.append(small_params[offset : offset + length])
        offset = offset + length
    piece_collection[9] = piece_collection[9].reshape(2, BIAS_NET_HIDDEN)
    piece_collection[10] = piece_collection[10].reshape(BIAS_NET_HIDDEN, ATTENTION_HEADS)
    return piece_collection


def norm_rows(values, gain, shift):
    average = jnp.mean(values, axis=-1, keepdims=True)
    centred = values - average
    variance = jnp.mean(centred * centred, axis=-1, keepdims=True)
    return centred * lax.rsqrt(variance + 1e-05) * gain + shift


def position_bias(small_params):
    piece_collection = pieces(small_params)
    span = 2 * SIDE - 1
    offsets = jnp.arange(span, dtype=jnp.float32) - (SIDE - 1)
    coords = jnp.stack([jnp.repeat(offsets, span), jnp.tile(offsets, span)], axis=1) * (
        8.0 / (SIDE - 1)
    )
    coords = jnp.sign(coords) * jnp.log2(jnp.abs(coords) + 1.0) / 3.0
    hidden = jax.nn.gelu(
        jnp.dot(coords, piece_collection[9], precision=highest) + piece_collection[8]
    )
    table = 16.0 * jax.nn.sigmoid(jnp.dot(hidden, piece_collection[10], precision=highest))
    places = jnp.arange(WIN, dtype=jnp.int32)
    row_pos = places // SIDE
    col_pos = places % SIDE
    index = (row_pos[:, None] - row_pos[None, :] + SIDE - 1) * span + (
        col_pos[:, None] - col_pos[None, :] + SIDE - 1
    )
    lookup = (index.reshape(-1, 1) == jnp.arange(span * span, dtype=jnp.int32)[None, :]).astype(
        table.dtype
    )
    spread = jnp.dot(lookup, table, precision=highest)
    return spread.T.reshape(ATTENTION_HEADS, WIN, WIN)


def matmul_back(left_low, right_low, grad_low):
    grad_left = lax.dot_general(
        grad_low, right_low, contract_cols, preferred_element_type=jnp.float32
    )
    grad_right = lax.dot_general(
        left_low, grad_low, contract_rows, preferred_element_type=jnp.float32
    )
    return (grad_left, grad_right)


def add_joined_bias(raw, params):
    piece_collection = pieces(params)
    return raw + jnp.concatenate(
        [piece_collection[4], jnp.zeros_like(piece_collection[4]), piece_collection[5]]
    )


def add_out_bias(raw, params):
    return raw + pieces(params)[6]


def normalize_heads(projected):
    window_count = projected.shape[0] // WIN
    shaped = projected.reshape(window_count, WIN, 3, ATTENTION_HEADS, HEAD_DIM)
    queries = shaped[:, :, 0]
    key_vecs = shaped[:, :, 1]
    queries = queries * lax.rsqrt(jnp.sum(queries * queries, axis=-1, keepdims=True) + 1e-06)
    key_vecs = key_vecs * lax.rsqrt(jnp.sum(key_vecs * key_vecs, axis=-1, keepdims=True) + 1e-06)
    return (queries, key_vecs, shaped[:, :, 2])


def softmax_part(cosine, params):
    scale = jnp.exp(pieces(params)[7])[:, None, None]
    return jax.nn.softmax(cosine * scale + position_bias(params), axis=-1)


def front_forward(tokens_low, weights_low, params, route_ids):
    rows_here = tokens_low.shape[0]
    qkv_low = weights_low[:, : 3 * MODEL_WIDTH]
    out_low = weights_low[:, 3 * MODEL_WIDTH : 4 * MODEL_WIDTH]
    route_low = weights_low[:, 4 * MODEL_WIDTH :]
    raw_qkv = jnp.dot(tokens_low, qkv_low, preferred_element_type=jnp.float32)
    projected = add_joined_bias(raw_qkv, params)
    q_f, k_f, v_f = normalize_heads(projected)
    q_low = q_f.astype(jnp.bfloat16)
    k_low = k_f.astype(jnp.bfloat16)
    v_low = v_f.astype(jnp.bfloat16)
    cosine = jnp.einsum("wihd,wjhd->whij", q_low, k_low, preferred_element_type=jnp.float32)
    probs = softmax_part(cosine, params)
    probs_low = probs.astype(jnp.bfloat16)
    mixed_low = (
        jnp.einsum("whij,wjhd->wihd", probs_low, v_low, preferred_element_type=jnp.float32)
        .astype(jnp.bfloat16)
        .reshape(rows_here, MODEL_WIDTH)
    )
    attended = add_out_bias(jnp.dot(mixed_low, out_low, preferred_element_type=jnp.float32), params)
    piece_collection = pieces(params)
    section_one = tokens_low.astype(jnp.float32) + norm_rows(
        attended, piece_collection[0], piece_collection[1]
    )
    section_low = section_one.astype(jnp.bfloat16)
    logits = jnp.dot(section_low, route_low, preferred_element_type=jnp.float32)
    chosen_mask = (
        route_ids[:, None] == jnp.arange(logits.shape[1], dtype=jnp.int32)[None, :]
    ).astype(jnp.float32)
    gating = jax.nn.sigmoid(jnp.sum(logits * chosen_mask, axis=1))
    kept = (
        projected,
        q_low,
        k_low,
        v_low,
        cosine,
        probs_low,
        mixed_low,
        attended,
        section_low,
        logits,
        chosen_mask,
    )
    return (section_one, gating, section_low, kept)


def front_backward(tokens_low, weights_low, params, kept, grad_section, grad_gate, grad_feed):
    (
        projected,
        q_low,
        k_low,
        v_low,
        cosine,
        probs_low,
        mixed_low,
        attended,
        section_low,
        logits,
        chosen_mask,
    ) = kept
    rows_here = tokens_low.shape[0]
    window_count = rows_here // WIN
    qkv_low = weights_low[:, : 3 * MODEL_WIDTH]
    out_low = weights_low[:, 3 * MODEL_WIDTH : 4 * MODEL_WIDTH]
    route_low = weights_low[:, 4 * MODEL_WIDTH :]

    def gate_part(logit_values):
        return jax.nn.sigmoid(jnp.sum(logit_values * chosen_mask, axis=1))

    gate_back = jax.vjp(gate_part, logits)[1]
    grad_logits = gate_back(grad_gate)[0].astype(jnp.bfloat16)
    grad_from_route, grad_route = matmul_back(section_low, route_low, grad_logits)
    grad_total = grad_section + grad_feed + grad_from_route

    def section_part(attended_value, params_value):
        piece_collection = pieces(params_value)
        return norm_rows(attended_value, piece_collection[0], piece_collection[1])

    section_back = jax.vjp(section_part, attended, params)[1]
    grad_attended, grad_params_a = section_back(grad_total)
    grad_att_low = grad_attended.astype(jnp.bfloat16)
    grad_params_b = jax.vjp(add_out_bias, jnp.zeros_like(attended), params)[1](
        grad_att_low.astype(jnp.float32)
    )[1]
    grad_mixed, grad_out = matmul_back(mixed_low, out_low, grad_att_low)
    grad_mixed_low = grad_mixed.astype(jnp.bfloat16).reshape(
        window_count, WIN, ATTENTION_HEADS, HEAD_DIM
    )
    grad_probs = jnp.einsum(
        "wihd,wjhd->whij", grad_mixed_low, v_low, preferred_element_type=jnp.float32
    )
    grad_v = jnp.einsum(
        "whij,wihd->wjhd", probs_low, grad_mixed_low, preferred_element_type=jnp.float32
    )
    soft_back = jax.vjp(softmax_part, cosine, params)[1]
    grad_cosine, grad_params_c = soft_back(grad_probs)
    grad_cos_low = grad_cosine.astype(jnp.bfloat16)
    grad_q = jnp.einsum("whij,wjhd->wihd", grad_cos_low, k_low, preferred_element_type=jnp.float32)
    grad_k = jnp.einsum("whij,wihd->wjhd", grad_cos_low, q_low, preferred_element_type=jnp.float32)
    norm_back = jax.vjp(normalize_heads, projected)[1]
    grad_projected = norm_back((grad_q, grad_k, grad_v))[0]
    grad_proj_low = grad_projected.astype(jnp.bfloat16)
    grad_params_d = jax.vjp(add_joined_bias, jnp.zeros_like(projected), params)[1](
        grad_proj_low.astype(jnp.float32)
    )[1]
    grad_tokens, grad_qkv = matmul_back(tokens_low, qkv_low, grad_proj_low)
    grad_inputs = grad_total + grad_tokens
    grad_weights = jnp.concatenate([grad_qkv, grad_out, grad_route], axis=1)
    grad_params = grad_params_a + grad_params_b + grad_params_c + grad_params_d
    return (grad_inputs, grad_weights, grad_params)


def finish_block(section_one, gating, combined, kept_rows, live_rows, small_params):
    piece_collection = pieces(small_params)
    branch = (
        norm_rows(combined, piece_collection[2], piece_collection[3])
        * (gating * kept_rows)[:, None]
    )
    return (section_one + branch) * live_rows[:, None]


def assign(route_ids, count, experts, capacity):
    places = jnp.arange(route_ids.shape[0], dtype=jnp.int32)
    live_rows = places // IMG_TOK < count
    chosen = (
        (route_ids[:, None] == jnp.arange(experts, dtype=jnp.int32)[None, :]) & live_rows[:, None]
    ).astype(jnp.int32)
    before = jnp.cumsum(chosen, axis=0) - chosen
    slot = jnp.sum(before * chosen, axis=1)
    kept_rows = live_rows & (slot < capacity)
    dest_slot = jnp.where(kept_rows, route_ids * capacity + slot, experts * capacity)
    return (live_rows, kept_rows, dest_slot)


def adamw_step(weight, gradient, first, second, rate, decay):
    first_new = beta_one * first + (1.0 - beta_one) * gradient
    second_new = beta_two * second + (1.0 - beta_two) * gradient * gradient
    first_hat = first_new / (1.0 - beta_one**STEP)
    second_hat = second_new / (1.0 - beta_two**STEP)
    weight_new = weight - rate * (first_hat / (jnp.sqrt(second_hat) + epsilon) + decay * weight)
    return (weight_new, first_new, second_new)


def trade_rows(payload):
    arrived_rows = lax.all_to_all(
        payload, ("wide", "narrow"), split_axis=0, concat_axis=0, tiled=True
    )
    return arrived_rows


def per_device(
    tokens,
    cotangent,
    routes,
    images,
    dense_weight,
    dense_moment,
    dense_square,
    small_params,
    small_moment,
    small_square,
    inner_weight,
    inner_moment,
    inner_square,
    outer_weight,
    outer_moment,
    outer_square,
    expert_bias,
    bias_moment,
    bias_square,
):
    slices = lax.axis_size(("wide", "narrow"))
    split = slices // EXPERTS
    member = lax.axis_index(("wide", "narrow")) % split
    piece = MODEL_WIDTH // split
    ff_dev = inner_weight.shape[2]
    tok_rows = tokens.shape[0]
    capacity = (5 * tok_rows + 4 * EXPERTS - 1) // (4 * EXPERTS)
    slot_total = EXPERTS * capacity
    route_ids = routes[:, 0]
    live_rows, kept_rows, dest_slot = assign(route_ids, images[0], EXPERTS, capacity)
    live_f = live_rows.astype(jnp.float32)
    keep_f = kept_rows.astype(jnp.float32)
    clipped = jnp.minimum(dest_slot, slot_total - 1)
    gathered = lax.all_gather(
        dense_weight.astype(jnp.bfloat16), ("wide", "narrow"), axis=0, tiled=True
    )
    section_one, gating, expert_feed, kept = front_forward(
        tokens, gathered, small_params, route_ids
    )

    def fan_out(rows_value):
        placed_rows = (
            jnp.zeros((slot_total, MODEL_WIDTH), jnp.bfloat16)
            .at[dest_slot]
            .set(rows_value.astype(jnp.bfloat16), mode="drop")
        )
        copies = jnp.broadcast_to(
            placed_rows.reshape(EXPERTS, 1, capacity, MODEL_WIDTH),
            (EXPERTS, split, capacity, MODEL_WIDTH),
        )
        return trade_rows(copies.reshape(slices, capacity, MODEL_WIDTH)).reshape(
            slices * capacity, MODEL_WIDTH
        )

    def fan_in(partials):
        arrived = trade_rows(partials.reshape(slices, capacity, MODEL_WIDTH))
        summed = jnp.sum(
            arrived.reshape(EXPERTS, split, capacity, MODEL_WIDTH).astype(jnp.float32), axis=1
        ).reshape(slot_total, MODEL_WIDTH)
        return jnp.take(summed, clipped, axis=0) * keep_f[:, None]

    expert_rows = fan_out(expert_feed)
    first_matrix = inner_weight[0].astype(jnp.bfloat16)
    second_matrix = outer_weight[0].astype(jnp.bfloat16)
    pre_act = (
        jnp.dot(expert_rows, first_matrix, preferred_element_type=jnp.float32)
        + expert_bias[0, :ff_dev]
    )
    hidden = jax.nn.gelu(pre_act).astype(jnp.bfloat16)
    out_bias = lax.dynamic_update_slice(
        jnp.zeros((MODEL_WIDTH,), jnp.float32), expert_bias[0, ff_dev:], (member * piece,)
    )
    result = (jnp.dot(hidden, second_matrix, preferred_element_type=jnp.float32) + out_bias).astype(
        jnp.bfloat16
    )
    combined = fan_in(result)

    def tail_local(section_value, gate_value, combined_value, params):
        return finish_block(section_value, gate_value, combined_value, keep_f, live_f, params)

    layer_value, tail_back = jax.vjp(tail_local, section_one, gating, combined, small_params)
    grad_section, grad_gate, grad_combined, grad_small_tail = tail_back(
        cotangent.astype(jnp.float32)
    )
    grad_result = fan_out(grad_combined)
    grad_outer = lax.dot_general(
        hidden, grad_result, contract_rows, preferred_element_type=jnp.float32
    )
    grad_hidden = lax.dot_general(
        grad_result, second_matrix, contract_cols, preferred_element_type=jnp.float32
    )
    gelu_back = jax.vjp(jax.nn.gelu, pre_act)[1]
    grad_pre = gelu_back(grad_hidden)[0].astype(jnp.bfloat16)
    grad_inner = lax.dot_general(
        expert_rows, grad_pre, contract_rows, preferred_element_type=jnp.float32
    )
    column_total = jnp.sum(grad_result.astype(jnp.float32), axis=0)
    grad_bias = jnp.concatenate(
        [
            jnp.sum(grad_pre.astype(jnp.float32), axis=0),
            lax.dynamic_slice_in_dim(column_total, member * piece, piece, 0),
        ]
    )
    grad_rows = lax.dot_general(
        grad_pre, first_matrix, contract_cols, preferred_element_type=jnp.float32
    ).astype(jnp.bfloat16)
    grad_feed = fan_in(grad_rows)
    grad_inputs, grad_weights, grad_small_front = front_backward(
        tokens, gathered, small_params, kept, grad_section, grad_gate, grad_feed
    )
    grad_small = grad_small_front + grad_small_tail
    grad_whole, grad_small = lax.psum((grad_weights, grad_small), ("wide", "narrow"))
    share_rows = dense_weight.shape[0]
    grad_dense = lax.dynamic_slice_in_dim(
        grad_whole, lax.axis_index(("wide", "narrow")) * share_rows, share_rows, 0
    )
    dense_out = adamw_step(
        dense_weight, grad_dense, dense_moment, dense_square, dense_rate, weight_decay
    )
    small_out = adamw_step(small_params, grad_small, small_moment, small_square, small_rate, 0.0)
    inner_out = adamw_step(
        inner_weight, grad_inner[None], inner_moment, inner_square, expert_rate, weight_decay
    )
    outer_out = adamw_step(
        outer_weight, grad_outer[None], outer_moment, outer_square, expert_rate, weight_decay
    )
    bias_out = adamw_step(expert_bias, grad_bias[None], bias_moment, bias_square, expert_rate, 0.0)
    return (
        layer_value.astype(jnp.bfloat16),
        grad_inputs.astype(jnp.bfloat16),
        dense_out[0],
        dense_out[1],
        dense_out[2],
        small_out[0],
        small_out[1],
        small_out[2],
        inner_out[0],
        inner_out[1],
        inner_out[2],
        inner_out[0].astype(jnp.bfloat16),
        outer_out[0],
        outer_out[1],
        outer_out[2],
        outer_out[0].astype(jnp.bfloat16),
        bias_out[0],
        bias_out[1],
        bias_out[2],
    )


def solution(mesh):
    return jax.shard_map(
        per_device,
        mesh=mesh,
        in_specs=(
            P(("wide", "narrow"), None),
            P(("wide", "narrow"), None),
            P(("wide", "narrow"), None),
            P(("wide", "narrow")),
            P(("wide", "narrow"), None),
            P(("wide", "narrow"), None),
            P(("wide", "narrow"), None),
            P(),
            P(),
            P(),
            P(("wide", "narrow"), None, None),
            P(("wide", "narrow"), None, None),
            P(("wide", "narrow"), None, None),
            P(("wide", "narrow"), None, None),
            P(("wide", "narrow"), None, None),
            P(("wide", "narrow"), None, None),
            P(("wide", "narrow"), None),
            P(("wide", "narrow"), None),
            P(("wide", "narrow"), None),
        ),
        out_specs=(
            P(("wide", "narrow"), None),
            P(("wide", "narrow"), None),
            P(("wide", "narrow"), None),
            P(("wide", "narrow"), None),
            P(("wide", "narrow"), None),
            P(),
            P(),
            P(),
            P(("wide", "narrow"), None, None),
            P(("wide", "narrow"), None, None),
            P(("wide", "narrow"), None, None),
            P(("wide", "narrow"), None, None),
            P(("wide", "narrow"), None, None),
            P(("wide", "narrow"), None, None),
            P(("wide", "narrow"), None, None),
            P(("wide", "narrow"), None, None),
            P(("wide", "narrow"), None),
            P(("wide", "narrow"), None),
            P(("wide", "narrow"), None),
        ),
        check_vma=False,
    )
```

profile of v0, /device:TPU:0, one launch (start us, length us, event | category | flops | bytes accessed | tf_op | source)
XLA Modules:
  0.0 516.0 jit_solution(18043255246555057141)
XLA Ops:
  7.2 1.5 convert_bitcast_fusion
  13.0 9.0 %reduce-window.6 = s32[32,8,128]{2,1,0:T(8,128)S(1)} reduce-window(s32[32,8,128]{2,1,0:T(8,128)S(1)} %fusion.74, s32[]{:T(128)} %constant.214.clone.1), window={size=1x1x128 pad=0_0x0_0x127_0}, to_apply=%region_6.7 | reduce-window | flops 4161536 | bytes 262148 | tf_op jit(solution)/shard_map/reduce-window
  24.6 2.0 fusion.10
  27.2 1.7 fusion.126
  30.4 39.3 %all-gather.3.cloned.1.call-done = bf16[32,12,1568]{2,1,0:T(8,128)(2,1)} async-done(((bf16[1,12,1568]{2,1,0:T(8,128)(2,1)}), bf16[32,12,1568]{2,1,0:T(8,128)(2,1)}) %all-gather.3.cloned.1.call-update) | async-done | bytes 1204240 | tf_op jit(solution)/shard_map/all_gather | solution.py:305
  69.7 2.5 reshape.590
  72.2 3.6 convolution_add_fusion.1
  75.8 6.0 %copy.179 = f32[1024,1152]{0,1:T(8,128)} copy(f32[1024,1152]{1,0:T(8,128)} %convolution_add_fusion.1) | data formatting | bytes 9437184 | tf_op jit(solution)/shard_map/add | solution.py:97
  81.9 8.5 %reshape.533 = f32[16,64,3,12,32]{1,0,4,3,2:T(8,128)} reshape(f32[1024,1152]{0,1:T(8,128)} %copy.179) | data formatting | bytes 9437184 | tf_op jit(solution)/shard_map/reshape | solution.py:108
  90.4 2.1 slice.111
  92.6 4.0 fusion.125
  96.6 1.4 multiply_reduce_fusion.2
  99.2 1.4 multiply_reduce_fusion.3
  100.7 4.1 multiply_convert_fusion.2
  104.8 7.2 %fusion.127 = (f32[16,12,64]{2,1,0:T(8,128)S(1)}, f32[16,12,64,64]{2,3,1,0:T(8,128)}) fusion(f32[12,64,64]{1,2,0:T(8,128)S(1)} %copy.183, f32[12]{0:T(128)S(1)} %slice_exponential_fusion, bf16[16,64,12,32]{1,3,2,0:T(8,128)(2,1)} %get-tuple-element.183, bf16[16,64,12,32]{1,3,2,0:T(8,128)(2,1)} %get-tuple-element.182), kind=kOutput, calls=%fused_computation.262 | convolution fusion | flops 53477440 | bytes 4964400 | tf_op jit(solution)/shard_map/sub | solution.py:118
  112.0 3.9 divide_convert_fusion
  120.1 1.8 fusion.128
  123.0 6.1 %scatter_custom_fusion = bf16[1280,384]{1,0:T(8,128)(2,1)} fusion(s32[1024]{0:T(1024)} %bitcast.195, bf16[1024,384]{1,0:T(8,128)(2,1)S(1)} %copy.188, bf16[]{:T(256)} %constant.222.clone.1), kind=kCustom, calls=%fused_computation.129 | custom fusion | bytes 983552 | tf_op jit(solution)/shard_map/scatter | solution.py:316
  129.1 3.5 all-to-all-start
  132.7 26.1 %all-to-all-done = bf16[32,40,384]{2,1,0:T(8,128)(2,1)S(1)} async-done(((bf16[32,40,384]{2,1,0:T(8,128)(2,1)}), bf16[32,40,384]{2,1,0:T(8,128)(2,1)S(1)}, u32[]{:S(2)}, u32[]{:S(2)}) %all-to-all-start) | async-done | bytes 983072 | tf_op jit(solution)/shard_map/all_to_all | solution.py:265
  158.8 8.0 %multiply_convert_fusion = (bf16[1280,1536]{1,0:T(8,128)(2,1)S(1)}, f32[1280,1536]{1,0:T(8,128)}) fusion(f32[1536]{0:T(1024)S(1)} %slice_reduce_fusion, bf16[1280,384]{1,0:T(8,128)(2,1)S(1)} %bitcast.181, f32[1,384,1536]{2,1,0:T(8,128)} %param.31), kind=kOutput, calls=%fused_computation.18 | convolution fusion | flops 1530200064 | bytes 15144960 | tf_op jit(solution)/shard_map/dot_general | solution.py:337
  166.8 3.2 fusion.17
  170.0 3.7 all-to-all-start.1
  178.5 21.4 %all-to-all-done.1 = bf16[32,40,384]{2,1,0:T(8,128)(2,1)} async-done(((bf16[32,40,384]{2,1,0:T(8,128)(2,1)}), bf16[32,40,384]{2,1,0:T(8,128)(2,1)}, u32[]{:S(2)}, u32[]{:S(2)}) %all-to-all-start.1) | async-done | bytes 983072 | tf_op jit(solution)/shard_map/all_to_all | solution.py:265
  199.8 1.3 bitcast_convert_fusion.1
  201.2 5.0 gather_fusion
  206.2 1.9 copy.189
  208.4 2.7 multiply_reduce_fusion.8
  211.2 3.2 multiply_reduce_fusion.4
  214.4 1.6 add_convert_fusion.3
  216.0 1.5 copy.191
  217.6 6.3 %scatter_custom_fusion.1 = bf16[1280,384]{1,0:T(8,128)(2,1)} fusion(s32[1024]{0:T(1024)} %bitcast.196, bf16[1024,384]{1,0:T(8,128)(2,1)S(1)} %copy.191, bf16[]{:T(256)} %constant.222.clone.1), kind=kCustom, calls=%fused_computation.127 | custom fusion | bytes 983552 | tf_op jit(solution)/shard_map/scatter | solution.py:316
  223.9 3.0 all-to-all-start.2
  227.6 2.3 copy.207
  230.9 22.2 %all-to-all-done.2 = bf16[32,40,384]{2,1,0:T(8,128)(2,1)S(1)} async-done(((bf16[32,40,384]{2,1,0:T(8,128)(2,1)}), bf16[32,40,384]{2,1,0:T(8,128)(2,1)S(1)}, u32[]{:S(2)}, u32[]{:S(2)}) %all-to-all-start.2) | async-done | bytes 983072 | tf_op jit(solution)/shard_map/all_to_all | solution.py:265
  253.1 9.5 %convert_reduce_fusion.1 = (f32[1536]{0:T(1024)S(1)}, bf16[1280,1536]{1,0:T(8,128)(2,1)S(1)}) fusion(f32[1280,1536]{1,0:T(8,128)} %get-tuple-element.168, bf16[1280,384]{1,0:T(8,128)(2,1)S(1)} %bitcast.178, f32[1,1536,384]{2,1,0:T(8,128)} %param.34), kind=kOutput, calls=%fused_computation.17 | convolution fusion | flops 1553791488 | bytes 15144960 | tf_op jit(solution)/shard_map/dot_general | solution.py:360
  262.6 3.2 convolution_convert_fusion
  265.9 3.5 all-to-all-start.3
  270.3 11.3 %fusion.121 = (bf16[1,384,1536]{2,1,0:T(8,128)(2,1)}, f32[1,384,1536]{2,1,0:T(8,128)}, f32[1,384,1536]{2,1,0:T(8,128)}, f32[1,384,1536]{2,1,0:T(8,128)}) fusion(f32[1,384,1536]{2,1,0:T(8,128)} %param.31, f32[1,384,1536]{2,1,0:T(8,128)} %param.32, f32[1,384,1536]{2,1,0:T(8,128)} %param.33, bf16[1280,384]{1,0:T(8,128)(2,1)} %bitcast.182, ...), kind=kOutput, calls=%fused_computation.259 | convolution fusion | flops 1519386624 | bytes 20250624 | tf_op jit(solution)/shard_map/dot_general | solution.py:365
  281.7 7.1 %fusion.119 = (bf16[1,1536,384]{2,1,0:T(8,128)(2,1)}, f32[1,1536,384]{2,1,0:T(8,128)}, f32[1,1536,384]{2,1,0:T(8,128)}, f32[1,1536,384]{2,1,0:T(8,128)}) fusion(f32[1,1536,384]{2,1,0:T(8,128)S(1)} %copy-done.93, f32[1,1536,384]{2,1,0:T(8,128)S(1)} %copy-done.94, f32[1,1536,384]{2,1,0:T(8,128)S(1)} %copy-done.95, bf16[1280,1536]{1,0:T(8,128)(2,1)S(1)} %copy-done.98, ...), kind=kOutput, calls=%fused_computation.258 | convolution fusion | flops 1519386624 | bytes 20250624 | tf_op jit(solution)/shard_map/dot_general | solution.py:357
  288.8 6.8 %all-to-all-done.3 = bf16[32,40,384]{2,1,0:T(8,128)(2,1)} async-done(((bf16[32,40,384]{2,1,0:T(8,128)(2,1)}), bf16[32,40,384]{2,1,0:T(8,128)(2,1)}, u32[]{:S(2)}, u32[]{:S(2)}) %all-to-all-start.3) | async-done | bytes 983072 | tf_op jit(solution)/shard_map/all_to_all | solution.py:265
  296.9 5.2 %gather_fusion.1 = f32[1024,384]{1,0:T(8,128)} fusion(f32[1280,384]{1,0:T(8,128)S(1)} %bitcast_convert_fusion, s32[1024]{0:T(1024)} %broadcast_clamp_fusion), kind=kCustom, calls=%fused_computation.1.clone | custom fusion | bytes 3149824 | tf_op jit(solution)/shard_map/jit(_take)/gather | solution.py:331
  302.1 3.1 copy.192
  305.3 2.2 fusion.117
  309.3 1.4 fusion.130
  310.7 2.6 convolution_convert_fusion.2
  313.3 2.5 copy.194
  315.8 3.2 reshape.546
  319.0 3.3 convolution_bitcast_fusion.1
  322.4 7.6 %multiply_reduce_fusion.1 = (f32[16,12,64]{2,1,0:T(8,128)S(1)}, f32[16,12,64,64]{2,3,1,0:T(8,128)}) fusion(f32[16,12,64,64]{2,3,1,0:T(8,128)} %get-tuple-element.164, f32[16,12,64]{2,1,0:T(8,128)S(1)} %copy-done.42, bf16[16,64,1,12,32]{1,0,4,3,2:T(8,128)(2,1)S(1)} %copy-done.11, bf16[16,64,12,32]{1,0,3,2:T(8,128)(2,1)S(1)} %copy-done.12), kind=kOutput, calls=%fused_computation.22 | convolution fusion | flops 52678656 | bytes 7962624 | tf_op jit(solution)/shard_map/wihd,wjhd->whij/dot_general | solution.py:209
  330.1 6.0 %fusion.116 = (f32[12,64,64]{1,2,0:T(8,128)}, f32[12]{0:T(128)S(1)}, f32[16,12,64,64]{2,3,1,0:T(8,128)S(1)}) fusion(f32[16,12,64,64]{2,3,1,0:T(8,128)S(1)} %bitcast.177, f32[16,12,64]{2,1,0:T(8,128)S(1)} %neg.28, f32[16,12,64,64]{2,3,1,0:T(8,128)} %get-tuple-element.171, f32[16,12,64]{2,1,0:T(8,128)S(1)} %copy-done.41, ...), kind=kOutput, calls=%fused_computation.256 | convolution fusion | flops 55001076 | bytes 11305008 | tf_op jit(solution)/shard_map/wihd,wjhd->whij/dot_general | solution.py:132
  336.1 2.1 fusion.13
  338.2 2.0 fusion.14
  341.7 1.4 fusion.12
  343.2 1.7 convert_reduce_fusion
  344.9 7.6 %copy.200 = bf16[16,64,3,12,32]{1,0,4,3,2:T(8,128)(2,1)} copy(bf16[16,64,3,12,32]{1,4,3,0,2:T(8,128)(2,1)S(1)} %get-tuple-element.145) | data formatting | bytes 4718592 | tf_op jit(solution)/shard_map/convert_element_type | solution.py:222
  352.5 7.8 %convert_element_type.162 = bf16[1024,1152]{0,1:T(8,128)(2,1)} reshape(bf16[16,64,3,12,32]{1,0,4,3,2:T(8,128)(2,1)} %copy.200) | data formatting | bytes 4718592 | tf_op jit(solution)/shard_map/convert_element_type | solution.py:222
  360.4 3.9 add_convert_fusion.1
  366.7 2.4 fusion.42
  369.1 2.6 fusion.129
  371.6 1.7 pad_maximum_fusion
  376.6 38.6 %psum.15 = f32[10380]{0:T(1024)S(1)} all-reduce(f32[10380]{0:T(1024)S(1)} %add_add_fusion.5), channel_id=1, replica_groups=mesh['wide'=4,'narrow'=8] {'wide','narrow'}, use_global_device_ids=true, to_apply=%region_32.34 | all-reduce | flops 10380 | bytes 83040 | tf_op jit(solution)/shard_map/psum | solution.py:383
  415.8 91.1 %all-reduce.16.cloned.1.call-done = f32[384,1568]{1,0:T(8,128)} async-done(((f32[384,1568]{1,0:T(8,128)}), f32[384,1568]{1,0:T(8,128)}) %all-reduce.16.cloned.1.call-update) | async-done | bytes 2408464 | tf_op jit(solution)/shard_map/psum | solution.py:383
  507.0 1.7 multiply_subtract_fusion.2
  (297 shorter events, 32.8 us)
Async XLA Ops:
  7.2 62.5 %all-gather.3.cloned.1.call-start = ((), (), s32[]{:S(2)}) async-start(), calls=%async_computation.5 | async-start | bytes 1757184 | tf_op jit(solution)/shard_map/all_gather | solution.py:305
  12.0 11.9 %copy-start.80 = (f32[225,1]{0,1:T(1,128)}, f32[225,1]{0,1:T(1,128)S(1)}, u32[]{:S(2)}) copy-start(f32[225,1]{0,1:T(1,128)S(1)} %stack_tile.3) | copy-start | bytes 2704
  12.2 11.7 %copy-start.82 = (f32[225,1]{0,1:T(1,128)}, f32[225,1]{0,1:T(1,128)S(1)}, u32[]{:S(2)}) copy-start(f32[225,1]{0,1:T(1,128)S(1)} %stack_reshape.3) | copy-start | bytes 2704
  12.3 11.7 %copy-start.78 = (s32[4096]{0:T(1024)}, s32[4096]{0:T(1024)S(1)}, u32[]{:S(2)}) copy-start(s32[4096]{0:T(1024)S(1)} %add.422) | copy-start | bytes 49156
  22.3 4.6 copy-start.36
  22.6 4.6 copy-start.48
  23.3 3.9 copy-start.43
  24.6 4.5 copy-start.49
  27.2 94.9 %copy-start.17 = (bf16[1024,384]{0,1:T(8,128)(2,1)}, bf16[1024,384]{0,1:T(8,128)(2,1)S(1)}, u32[]{:S(2)}) copy-start(bf16[1024,384]{0,1:T(8,128)(2,1)S(1)} %copy.178) | copy-start | bytes 2359300
  28.9 93.3 %copy-start.55 = (f32[384]{0:T(512)}, f32[384]{0:T(512)S(1)}, u32[]{:S(2)}) copy-start(f32[384]{0:T(512)S(1)} %get-tuple-element.156) | copy-start | bytes 4612
  29.1 46.7 %copy-start.58 = (s32[1024]{0:T(1024)}, s32[1024]{0:T(1024)S(1)}, u32[]{:S(2)}) copy-start(s32[1024]{0:T(1024)S(1)} %fusion.71) | copy-start | bytes 12292
  29.8 75.0 %copy-start.89 = (f32[12]{0:T(128)}, f32[12]{0:T(128)S(1)}, u32[]{:S(2)}) copy-start(f32[12]{0:T(128)S(1)} %slice_exponential_fusion) | copy-start | bytes 148
  72.2 3.6 copy-start.21
  92.5 23.4 %copy-start.10 = (bf16[16,64,1,12,32]{1,0,4,3,2:T(8,128)(2,1)}, bf16[16,64,1,12,32]{1,0,4,3,2:T(8,128)(2,1)S(1)}, u32[]{:S(2)}) copy-start(bf16[16,64,1,12,32]{1,0,4,3,2:T(8,128)(2,1)S(1)} %slice.111) | copy-start | bytes 2359300
  96.6 4.0 copy-start
  96.6 4.0 copy-start.2
  98.1 6.7 %copy-start.27 = (f32[16,64,12]{1,2,0:T(8,128)}, f32[16,64,12]{1,2,0:T(8,128)S(1)}, u32[]{:S(2)}) copy-start(f32[16,64,12]{1,2,0:T(8,128)S(1)} %add_rsqrt_fusion) | copy-start | bytes 147460
  100.6 4.2 copy-start.31
  100.7 4.1 copy-start.25
  112.0 3.9 copy-start.39
  122.6 54.1 %copy-start.13 = (bf16[1024,384]{0,1:T(8,128)(2,1)}, bf16[1024,384]{0,1:T(8,128)(2,1)S(1)}, u32[]{:S(2)}) copy-start(bf16[1024,384]{0,1:T(8,128)(2,1)S(1)} %fusion.111) | copy-start | bytes 2359300
  122.6 10.0 %copy-start.70 = (f32[1,1920]{1,0:T(1,128)S(1)}, f32[1,1920]{1,0:T(1,128)}, u32[]{:S(2)}) copy-start(f32[1,1920]{1,0:T(1,128)} %param.37) | copy-start | bytes 23044
  129.1 29.7 %all-to-all-start = ((bf16[32,40,384]{2,1,0:T(8,128)(2,1)}), bf16[32,40,384]{2,1,0:T(8,128)(2,1)S(1)}, u32[]{:S(2)}, u32[]{:S(2)}) async-start(bf16[32,40,384]{2,1,0:T(8,128)(2,1)} %bitcast.12), calls=%async_computation | async-start | bytes 1966080 | tf_op jit(solution)/shard_map/all_to_all | solution.py:265
  158.8 8.0 %copy-start.33 = (bf16[32,40,384]{2,1,0:T(8,128)(2,1)}, bf16[32,40,384]{2,1,0:T(8,128)(2,1)S(1)}, u32[]{:S(2)}) copy-start(bf16[32,40,384]{2,1,0:T(8,128)(2,1)S(1)} %all-to-all-done) | copy-start | bytes 2949124
  158.8 8.0 %copy-start.92 = (f32[1,1536,384]{2,1,0:T(8,128)S(1)}, f32[1,1536,384]{2,1,0:T(8,128)}, u32[]{:S(2)}) copy-start(f32[1,1536,384]{2,1,0:T(8,128)} %param.34) | copy-start | bytes 7077892
  166.8 6.9 %copy-start.59 = (s32[1024]{0:T(1024)S(1)}, s32[1024]{0:T(1024)}, u32[]{:S(2)}) copy-start(s32[1024]{0:T(1024)} %copy-done.58) | copy-start | bytes 12292
  170.0 4.3 copy-start.35
  170.0 29.9 %all-to-all-start.1 = ((bf16[32,40,384]{2,1,0:T(8,128)(2,1)}), bf16[32,40,384]{2,1,0:T(8,128)(2,1)}, u32[]{:S(2)}, u32[]{:S(2)}) async-start(bf16[32,40,384]{2,1,0:T(8,128)(2,1)} %bitcast.16), calls=%async_computation.1 | async-start | bytes 1966080 | tf_op jit(solution)/shard_map/all_to_all | solution.py:265
  174.3 4.2 copy-start.72
  216.0 10.9 %copy-start.40 = (f32[16,12,64]{2,1,0:T(8,128)S(1)}, f32[16,12,64]{2,1,0:T(8,128)}, u32[]{:S(2)}) copy-start(f32[16,12,64]{2,1,0:T(8,128)} %copy-done.39) | copy-start | bytes 147460
  217.6 12.3 %copy-start.66 = (f32[1024]{0:T(1024)S(1)}, f32[1024]{0:T(1024)}, u32[]{:S(2)}) copy-start(f32[1024]{0:T(1024)} %copy-done.65) | copy-start | bytes 12292
  217.6 12.3 %copy-start.73 = (pred[1024]{0:T(1024)(128)(4,1)S(1)}, pred[1024]{0:T(1024)(128)(4,1)}, u32[]{:S(2)}) copy-start(pred[1024]{0:T(1024)(128)(4,1)} %copy-done.72) | copy-start | bytes 3076
  217.6 12.3 %copy-start.14 = (bf16[1024,384]{0,1:T(8,128)(2,1)S(1)}, bf16[1024,384]{0,1:T(8,128)(2,1)}, u32[]{:S(2)}) copy-start(bf16[1024,384]{0,1:T(8,128)(2,1)} %copy-done.13) | copy-start | bytes 2359300
  223.9 29.2 %all-to-all-start.2 = ((bf16[32,40,384]{2,1,0:T(8,128)(2,1)}), bf16[32,40,384]{2,1,0:T(8,128)(2,1)S(1)}, u32[]{:S(2)}, u32[]{:S(2)}) async-start(bf16[32,40,384]{2,1,0:T(8,128)(2,1)} %bitcast.180), calls=%async_computation.2 | async-start | bytes 1966080 | tf_op jit(solution)/shard_map/all_to_all | solution.py:265
  229.9 32.7 %copy-start.76 = (bf16[1024]{0:T(1024)(128)(2,1)}, bf16[1024]{0:T(1024)(128)(2,1)S(1)}, u32[]{:S(2)}) copy-start(bf16[1024]{0:T(1024)(128)(2,1)S(1)} %fusion.91) | copy-start | bytes 6148
  253.1 9.5 %copy-start.91 = (f32[1,384,1536]{2,1,0:T(8,128)S(1)}, f32[1,384,1536]{2,1,0:T(8,128)}, u32[]{:S(2)}) copy-start(f32[1,384,1536]{2,1,0:T(8,128)} %param.31) | copy-start | bytes 7077892
  265.8 3.8 copy-start.71
  265.9 3.8 copy-start.87
  265.9 3.8 copy-start.88
  265.9 29.7 %all-to-all-start.3 = ((bf16[32,40,384]{2,1,0:T(8,128)(2,1)}), bf16[32,40,384]{2,1,0:T(8,128)(2,1)}, u32[]{:S(2)}, u32[]{:S(2)}) async-start(bf16[32,40,384]{2,1,0:T(8,128)(2,1)} %bitcast.183), calls=%async_computation.3 | async-start | bytes 1966080 | tf_op jit(solution)/shard_map/all_to_all | solution.py:265
  269.4 237.6 %all-reduce.16.cloned.1.call-start = ((), (), s32[]{:S(2)}) async-start(), calls=%async_computation.4 | async-start | bytes 5111808 | tf_op jit(solution)/shard_map/psum | solution.py:383
  270.3 11.3 %copy-start.93 = (f32[1,1536,384]{2,1,0:T(8,128)S(1)}, f32[1,1536,384]{2,1,0:T(8,128)}, u32[]{:S(2)}) copy-start(f32[1,1536,384]{2,1,0:T(8,128)} %param.34) | copy-start | bytes 7077892
  270.3 11.3 %copy-start.94 = (f32[1,1536,384]{2,1,0:T(8,128)S(1)}, f32[1,1536,384]{2,1,0:T(8,128)}, u32[]{:S(2)}) copy-start(f32[1,1536,384]{2,1,0:T(8,128)} %param.35) | copy-start | bytes 7077892
  270.3 11.3 %copy-start.95 = (f32[1,1536,384]{2,1,0:T(8,128)S(1)}, f32[1,1536,384]{2,1,0:T(8,128)}, u32[]{:S(2)}) copy-start(f32[1,1536,384]{2,1,0:T(8,128)} %param.36) | copy-start | bytes 7077892
  270.3 11.3 %copy-start.98 = (bf16[1280,1536]{1,0:T(8,128)(2,1)S(1)}, bf16[1280,1536]{1,0:T(8,128)(2,1)}, u32[]{:S(2)}) copy-start(bf16[1280,1536]{1,0:T(8,128)(2,1)} %copy-done.97) | copy-start | bytes 11796484
  313.3 5.7 %copy-start.5 = (bf16[16,12,64,64]{2,3,1,0:T(8,128)(2,1)S(1)}, bf16[16,12,64,64]{2,3,1,0:T(8,128)(2,1)}, u32[]{:S(2)}) copy-start(bf16[16,12,64,64]{2,3,1,0:T(8,128)(2,1)} %copy-done.4) | copy-start | bytes 4718596
  319.0 11.0 %slice-start = ((s8[6291456]{0:T(1024)(128)(4,1)}), s8[4194304]{0:T(1024)(128)(4,1)S(1)}, s32[]{:S(2)}) async-start(s8[6291456]{0:T(1024)(128)(4,1)} %bitcast.176), calls=%async_computation.6 | async-start | bytes 8388608
  322.3 7.7 %slice-start.1 = ((s8[6291456]{0:T(1024)(128)(4,1)}), s8[2097152]{0:T(1024)(128)(4,1)S(1)}, s32[]{:S(2)}) async-start(s8[6291456]{0:T(1024)(128)(4,1)} %bitcast.176), calls=%async_computation.7 | async-start | bytes 4194304
  322.3 7.7 %copy-start.19 = (bf16[16,64,12,32]{1,3,2,0:T(8,128)(2,1)S(1)}, bf16[16,64,12,32]{1,3,2,0:T(8,128)(2,1)}, u32[]{:S(2)}) copy-start(bf16[16,64,12,32]{1,3,2,0:T(8,128)(2,1)} %get-tuple-element.183) | copy-start | bytes 2359300
  322.3 7.7 %copy-start.20 = (bf16[16,64,12,32]{1,3,2,0:T(8,128)(2,1)S(1)}, bf16[16,64,12,32]{1,3,2,0:T(8,128)(2,1)}, u32[]{:S(2)}) copy-start(bf16[16,64,12,32]{1,3,2,0:T(8,128)(2,1)} %get-tuple-element.182) | copy-start | bytes 2359300
  322.3 7.7 %copy-start.41 = (f32[16,12,64]{2,1,0:T(8,128)S(1)}, f32[16,12,64]{2,1,0:T(8,128)}, u32[]{:S(2)}) copy-start(f32[16,12,64]{2,1,0:T(8,128)} %copy-done.39) | copy-start | bytes 147460
  330.1 6.0 %copy-start.1 = (f32[16,64,1,12,32]{1,0,4,3,2:T(8,128)S(1)}, f32[16,64,1,12,32]{1,0,4,3,2:T(8,128)}, u32[]{:S(2)}) copy-start(f32[16,64,1,12,32]{1,0,4,3,2:T(8,128)} %copy-done) | copy-start | bytes 4718596
  330.1 6.0 %copy-start.90 = (f32[12]{0:T(128)S(1)}, f32[12]{0:T(128)}, u32[]{:S(2)}) copy-start(f32[12]{0:T(128)} %copy-done.89) | copy-start | bytes 148
  352.5 7.8 %copy-start.9 = (f32[1024,384]{0,1:T(8,128)S(1)}, f32[1024,384]{0,1:T(8,128)}, u32[]{:S(2)}) copy-start(f32[1024,384]{0,1:T(8,128)} %copy-done.8) | copy-start | bytes 4718596
  352.5 7.8 %copy-start.22 = (bf16[384,1568]{1,0:T(8,128)(2,1)S(1)}, bf16[384,1568]{1,0:T(8,128)(2,1)}, u32[]{:S(2)}) copy-start(bf16[384,1568]{1,0:T(8,128)(2,1)} %copy-done.21) | copy-start | bytes 3612676
  360.4 3.9 copy-start.23
  360.4 3.9 copy-start.37
  365.8 5.8 %copy-start.24 = (f32[384,384]{1,0:T(8,128)S(1)}, f32[384,384]{1,0:T(8,128)}, u32[]{:S(2)}) copy-start(f32[384,384]{1,0:T(8,128)} %fusion.130) | copy-start | bytes 1769476
  365.8 5.8 %copy-start.34 = (f32[384,32]{1,0:T(8,128)S(1)}, f32[384,32]{1,0:T(8,128)}, u32[]{:S(2)}) copy-start(f32[384,32]{1,0:T(8,128)} %fusion.78) | copy-start | bytes 147460
  373.4 41.7 %copy-start.61 = (f32[10380]{0:T(1024)S(1)}, f32[10380]{0:T(1024)}, u32[]{:S(2)}) copy-start(f32[10380]{0:T(1024)} %param.29) | copy-start | bytes 124564
  373.4 41.7 %copy-start.62 = (f32[10380]{0:T(1024)S(1)}, f32[10380]{0:T(1024)}, u32[]{:S(2)}) copy-start(f32[10380]{0:T(1024)} %param.30) | copy-start | bytes 124564
  373.4 133.5 %copy-start.46 = (f32[12,1568]{1,0:T(8,128)S(1)}, f32[12,1568]{1,0:T(8,128)}, u32[]{:S(2)}) copy-start(f32[12,1568]{1,0:T(8,128)} %param.25) | copy-start | bytes 225796
  373.5 133.5 %copy-start.51 = (f32[12,1568]{1,0:T(8,128)S(1)}, f32[12,1568]{1,0:T(8,128)}, u32[]{:S(2)}) copy-start(f32[12,1568]{1,0:T(8,128)} %param.26) | copy-start | bytes 225796
  373.5 133.5 %copy-start.52 = (f32[12,1568]{1,0:T(8,128)S(1)}, f32[12,1568]{1,0:T(8,128)}, u32[]{:S(2)}) copy-start(f32[12,1568]{1,0:T(8,128)} %param.27) | copy-start | bytes 225796
  (45 other events, 104.4 us)
Sparse Core Ops, SparseCore 0:
  11.4 58.1 all-gather.2
  373.5 133.4 all-reduce.15
where the time goes:
time: 523 us; the launch traced here: 516 us
  waiting for transfers between devices  207 us (40%)
  matrix products  100 us (19%)
  local copies, waits for them, and re-layouts  91.8 us (18%)
  other arithmetic  48 us (9%)
  blocking collectives  38.6 us (7%)
  between operations  16.8 us (3%)
  starting transfers between devices  13.8 us (3%)
    psum x1, waiting for transfers between devices, per_device(): lax.psum((grad_weights, grad_small), ('wide', 'narrow'))  91.1 us
    all_to_all x4, waiting for transfers between devices, trade_rows(): lax.all_to_all(payload, ('wide', 'narrow'), split_axis=0, concat_axis=0,...  76.4 us
    all_gather x1, waiting for transfers between devices, per_device(): lax.all_gather(dense_weight.astype(jnp.bfloat16), ('wide', 'narrow'), axi...  39.3 us
    psum x1, blocking collectives, per_device(): lax.psum((grad_weights, grad_small), ('wide', 'narrow'))  38.6 us
    convert_element_type x2, local copies, waits for them, and re-layouts, front_backward(): grad_proj_low = grad_projected.astype(jnp.bfloat16)  15.4 us
    gather x4, local copies, waits for them, and re-layouts, fan_in(): return jnp.take(summed, clipped, axis=0) * keep_f[:, None]  15.2 us
    all_to_all x4, starting transfers between devices, trade_rows(): lax.all_to_all(payload, ('wide', 'narrow'), split_axis=0, concat_axis=0,...  13.7 us
    scatter x2, local copies, waits for them, and re-layouts, fan_out(): placed_rows = jnp.zeros((slot_total, MODEL_WIDTH), jnp.bfloat16).at[dest_...  12.4 us
  transfers between devices with their start and end apart: 6, of which 6 were waited for; matrix products, arithmetic and copies ran while one was open for 10% of the time, Pallas kernels for 0%

commit v1 on v0

--- a/solution.py
+++ b/solution.py
@@ -1,6 +1,12 @@
+import functools
+import math
+
 import jax
 import jax.numpy as jnp
+import numpy as np
 from jax import lax
+from jax.experimental import pallas as pl
+from jax.experimental.pallas import tpu as pltpu
 from jax.sharding import PartitionSpec as P
 
 MODEL_WIDTH = 384
@@ -12,6 +18,18 @@
 IMG_TOK = 1024
 STEP = 10
 WIN = 64
+GROUP = 4
+GROUP_LANES = 128
+VMEM_BYTES = 48 * 2**20
+TABLE = 256
+TABLE_MID = 119
+STRIDE = 16
+SUM_LANES = BIAS_NET_HIDDEN
+SECOND_ROWS = 8
+SHIFT_ROW = 20
+FIRST_ROWS = 21
+SCALE_ROWS = 24
+ROUTE_ROWS = 32
 
 
 highest = lax.Precision.HIGHEST
@@ -118,7 +136,7 @@
     return jax.nn.softmax(cosine * scale + position_bias(params), axis=-1)
 
 
-def front_forward(tokens_low, weights_low, params, route_ids):
+def front_forward_split(tokens_low, weights_low, params, route_ids):
     rows_here = tokens_low.shape[0]
     qkv_low = weights_low[:, : 3 * MODEL_WIDTH]
     out_low = weights_low[:, 3 * MODEL_WIDTH : 4 * MODEL_WIDTH]
@@ -164,7 +182,7 @@
     return (section_one, gating, section_low, kept)
 
 
-def front_backward(tokens_low, weights_low, params, kept, grad_section, grad_gate, grad_feed):
+def front_backward_split(tokens_low, weights_low, params, kept, grad_section, grad_gate, grad_feed):
     (
         projected,
         q_low,
@@ -268,7 +286,753 @@
     return arrived_rows
 
 
-def per_device(
+def axis_bits(axis):
+    size = lax.axis_size(axis)
+    return [(axis, 1 << k) for k in range(size.bit_length() - 1)]
+
+
+def swap(value, step):
+    axis, offset = step
+    return lax.ppermute(value, axis, [(i, i ^ offset) for i in range(lax.axis_size(axis))])
+
+
+def upper(step):
+    axis, offset = step
+    return (lax.axis_index(axis) & offset) > 0
+
+
+def gather_rows(share):
+    steps = axis_bits("narrow") + axis_bits("wide")
+    first, rest = steps[0], steps[1:]
+    other = swap(share, first)
+    block = jnp.where(
+        upper(first), jnp.concatenate([other, share]), jnp.concatenate([share, other])
+    )
+    held = block
+    done = []
+    core = ("wide", 1)
+    for step in [s for s in rest if s != core] + [core]:
+        place = sum(1 for d in done if rest.index(d) > rest.index(step))
+        other = swap(held, step)
+        held = jnp.where(
+            upper(step), jnp.stack([other, held], place), jnp.stack([held, other], place)
+        )
+        done.append(step)
+    return held.reshape(-1, share.shape[1])
+
+
+def sum_grads(partial, small):
+    steps = axis_bits("narrow") + axis_bits("wide")
+    first, rest = steps[0], steps[1:]
+    core = ("wide", 1)
+    order = [core] + [s for s in rest[::-1] if s != core]
+    count = lax.axis_size(("wide", "narrow"))
+    share = partial.shape[0] // count
+    held = partial.reshape((2,) * len(rest) + (2 * share, partial.shape[1]))
+    left = rest[::-1]
+    for step in order:
+        place = left.index(step)
+        side = upper(step).astype(jnp.int32)
+        send = lax.dynamic_index_in_dim(held, 1 - side, place, keepdims=False)
+        keep = lax.dynamic_index_in_dim(held, side, place, keepdims=False)
+        other = swap(send.astype(jnp.bfloat16), step)
+        small = small + swap(small, step)
+        held = keep + other.astype(jnp.float32)
+        left = [s for s in left if s != step]
+    side = upper(first)
+    send = jnp.where(side, held[:share], held[share:])
+    keep = jnp.where(side, held[share:], held[:share])
+    other = swap(send.astype(jnp.bfloat16), first)
+    small = small + swap(small, first)
+    return keep + other.astype(jnp.float32), small
+
+
+def join(held, step, axis=None):
+    other = swap(held, step)
+    if axis is None or axis >= 0:
+        both = functools.partial(jnp.stack, axis=axis or 0)
+    else:
+        both = functools.partial(jnp.concatenate, axis=axis)
+    return jnp.where(upper(step), both([other, held]), both([held, other]))
+
+
+def sum_quads(small, steps):
+    axis, low = steps[0]
+    high = steps[1][1]
+    near = small + swap(small, (axis, low))
+    return near + (swap(small, (axis, high)) + swap(small, (axis, high + low)))
+
+
+def sum_chip(send, keep):
+    return (keep + swap(send, ("wide", 1)).astype(jnp.float32)).astype(jnp.bfloat16)
+
+
+def sum_shares(held):
+    wide, narrow = lax.axis_size("wide"), lax.axis_size("narrow")
+    groups = [
+        [w * narrow + n for w in range(core, wide, 2) for n in range(narrow)] for core in range(2)
+    ]
+    arrived = lax.all_to_all(held, ("wide", "narrow"), 0, 0, axis_index_groups=groups, tiled=True)
+    return jnp.sum(arrived.astype(jnp.float32), axis=0)
+
+
+def lane_masks(dtype):
+    lane = lax.broadcasted_iota(jnp.int32, (1, GROUP_LANES), 1) // HEAD_DIM
+    return [(lane == h).astype(jnp.float32).astype(dtype) for h in range(GROUP)]
+
+
+def dot(left, right):
+    return jnp.dot(left, right, preferred_element_type=jnp.float32)
+
+
+def dot_cols(left, right):
+    return lax.dot_general(left, right, contract_cols, preferred_element_type=jnp.float32)
+
+
+def dot_rows(left, right):
+    return lax.dot_general(left, right, contract_rows, preferred_element_type=jnp.float32)
+
+
+def stack_heads(rows, masks):
+    return jnp.concatenate([rows * m for m in masks], axis=0)
+
+
+def pick_heads(blocks, masks):
+    n = blocks.shape[0] // GROUP
+    return sum(blocks[n * h : n * h + n] * masks[h] for h in range(GROUP))
+
+
+def head_sums(values):
+    row = lax.broadcasted_iota(jnp.int32, (2 * GROUP_LANES, GROUP_LANES), 0) % GROUP_LANES
+    col = lax.broadcasted_iota(jnp.int32, (2 * GROUP_LANES, GROUP_LANES), 1)
+    ones = (row // HEAD_DIM == col // HEAD_DIM).astype(jnp.float32).astype(jnp.bfloat16)
+    high = values.astype(jnp.bfloat16)
+    rest = (values - high.astype(jnp.float32)).astype(jnp.bfloat16)
+    sums = []
+    for start in range(0, values.shape[1], GROUP_LANES):
+        cut = slice(start, start + GROUP_LANES)
+        sums.append(dot(jnp.concatenate([high[:, cut], rest[:, cut]], axis=1), ones))
+    return jnp.concatenate(sums, axis=1)
+
+
+def send_rows(dest_row, rows, out_ref):
+    total = out_ref.shape[0]
+    block = math.gcd(total, 256)
+    for start in range(0, total, block):
+        slot = lax.broadcasted_iota(jnp.int32, (block, rows.shape[0]), 0) + start
+        chosen = jnp.where(slot == dest_row, 1.0, 0.0).astype(jnp.bfloat16)
+        out_ref[pl.ds(start, block), :] = dot(chosen, rows).astype(jnp.bfloat16)
+
+
+def gelu_pair(pre):
+    inner = math.sqrt(2.0 / math.pi)
+    square = pre * pre
+    bend = jnp.tanh(pre * (inner + (inner * 0.044715) * square))
+    half = 0.5 + 0.5 * bend
+    slope = half + pre * (half * (1.0 - bend)) * (inner + (3.0 * inner * 0.044715) * square)
+    return pre * half, slope
+
+
+def take_rows(dest_row, rows):
+    count, total = dest_row.shape[1], rows.shape[0]
+    places = jnp.broadcast_to(dest_row.astype(jnp.float32), (GROUP_LANES, count)).T
+    lane = lax.broadcasted_iota(jnp.int32, (count, GROUP_LANES), 1).astype(jnp.float32)
+    chosen = jnp.concatenate(
+        [
+            jnp.where(places == lane + float(start), 1.0, 0.0).astype(jnp.bfloat16)
+            for start in range(0, total, GROUP_LANES)
+        ],
+        axis=1,
+    )
+    return dot(chosen, rows)
+
+
+def assign_kernel(capacity, count_ref, route_ref, cot_ref, dest_ref, out_ref):
+    tokens = route_ref.shape[1]
+    total = out_ref.shape[0]
+    span = GROUP_LANES
+    live_end = count_ref[0] * IMG_TOK
+    first = lax.broadcasted_iota(jnp.int32, (span, span), 0)
+    second = lax.broadcasted_iota(jnp.int32, (span, span), 1)
+    earlier = jnp.where(first < second, 1.0, 0.0).astype(jnp.bfloat16)
+    whole = jnp.ones((span, span), jnp.bfloat16)
+    carry = jnp.zeros((EXPERTS, span), jnp.float32)
+    for start in range(0, tokens, span):
+        route = route_ref[:, start : start + span]
+        place = lax.broadcasted_iota(jnp.int32, (1, span), 1) + start
+        expert = lax.broadcasted_iota(jnp.int32, (EXPERTS, span), 0)
+        chosen = jnp.where((expert == route) & (place < live_end), 1.0, 0.0)
+        low = chosen.astype(jnp.bfloat16)
+        before = dot(low, earlier) + carry
+        carry = carry + dot(low, whole)
+        slot = jnp.sum(before * chosen, axis=0, keepdims=True).astype(jnp.int32)
+        keep = (place < live_end) & (slot < capacity)
+        dest_ref[:, start : start + span] = jnp.where(keep, route * capacity + slot, total)
+    send_rows(dest_ref[...], cot_ref[...], out_ref)
+
+
+def call_assign(images, routes, cotangent, capacity):
+    tokens = routes.shape[0]
+    total = EXPERTS * capacity
+    return pl.pallas_call(
+        functools.partial(assign_kernel, capacity),
+        out_shape=(
+            jax.ShapeDtypeStruct((1, tokens), jnp.int32),
+            jax.ShapeDtypeStruct((total, MODEL_WIDTH), jnp.bfloat16),
+        ),
+        in_specs=[
+            pl.BlockSpec(memory_space=pltpu.SMEM),
+            pl.BlockSpec(memory_space=pltpu.VMEM),
+            pl.BlockSpec(memory_space=pltpu.VMEM),
+        ],
+        out_specs=(
+            pl.BlockSpec(memory_space=pltpu.VMEM),
+            pl.BlockSpec(memory_space=pltpu.VMEM),
+        ),
+        cost_estimate=pl.CostEstimate(
+            flops=2 * total * tokens * MODEL_WIDTH, bytes_accessed=4 * 10**6, transcendentals=0
+        ),
+        compiler_params=pltpu.CompilerParams(vmem_limit_bytes=VMEM_BYTES),
+        name="assign",
+    )(images, routes.reshape(1, tokens), cotangent)
+
+
+def front_kernel(
+    dest_ref,
+    tokens_ref,
+    weight_ref,
+    rows_ref,
+    scale_ref,
+    bias_ref,
+    placed_ref,
+    section_ref,
+    attended_ref,
+    mixed_ref,
+    raw_ref,
+    heads_ref,
+    probs_ref,
+    low_ref,
+):
+    step = pl.program_id(0)
+    block = tokens_ref.shape[0]
+    width = MODEL_WIDTH
+    tokens = tokens_ref[...]
+    masks_low = lane_masks(jnp.bfloat16)
+    masks = lane_masks(jnp.float32)
+    projected = dot(tokens, weight_ref[:, : 3 * width])
+    queries = projected[:, :width] + rows_ref[4:5, :]
+    keys = projected[:, width : 2 * width]
+    values = projected[:, 2 * width :] + rows_ref[5:6, :]
+    raw_ref[:, :width] = queries
+    raw_ref[:, width:] = keys
+    heads_ref[:, :width] = (queries * lax.rsqrt(head_sums(queries * queries) + 1e-06)).astype(
+        jnp.bfloat16
+    )
+    heads_ref[:, width : 2 * width] = (
+        keys * lax.rsqrt(head_sums(keys * keys) + 1e-06)
+    ).astype(jnp.bfloat16)
+    heads_ref[:, 2 * width :] = values.astype(jnp.bfloat16)
+    for window in range(block // WIN):
+        at = pl.ds(window * WIN, WIN)
+        for group in range(width // GROUP_LANES):
+            start = group * GROUP_LANES
+            query = heads_ref[at, start : start + GROUP_LANES]
+            key = heads_ref[at, width + start : width + start + GROUP_LANES]
+            value = heads_ref[at, 2 * width + start : 2 * width + start + GROUP_LANES]
+            cosine = dot_cols(key, stack_heads(query, masks_low))
+            scores = cosine * scale_ref[group] + bias_ref[group]
+            powers = jnp.exp(scores - jnp.max(scores, axis=0, keepdims=True))
+            probs = powers * (1.0 / jnp.sum(powers, axis=0, keepdims=True))
+            probs_ref[window, group] = probs
+            mixed = pick_heads(dot_rows(probs.astype(jnp.bfloat16), value), masks)
+            mixed_ref[at, start : start + GROUP_LANES] = mixed.astype(jnp.bfloat16)
+    attended = dot(mixed_ref[...], weight_ref[:, 3 * width : 4 * width]) + rows_ref[6:7, :]
+    attended_ref[...] = attended
+    section = tokens.astype(jnp.float32) + norm_rows(attended, rows_ref[0:1, :], rows_ref[1:2, :])
+    section_ref[...] = section
+    low_ref[pl.ds(pl.multiple_of(step * block, block), block), :] = section.astype(jnp.bfloat16)
+
+    @pl.when(step == pl.num_programs(0) - 1)
+    def _():
+        send_rows(dest_ref[...], low_ref[...], placed_ref)
+
+
+def token_block(tok_rows):
+    return math.gcd(tok_rows, 256)
+
+
+def whole(shape):
+    return pl.BlockSpec(shape, lambda i: (0,) * len(shape))
+
+
+def by_rows(block, width):
+    return pl.BlockSpec((block, width), lambda i: (i, 0))
+
+
+def call_front(dest, tokens, gathered, rows, scale, bias, capacity):
+    count, width = tokens.shape
+    total = EXPERTS * capacity
+    block = token_block(count)
+    groups = width // GROUP_LANES
+    probs_shape = (count // WIN, groups, WIN, GROUP * WIN)
+    return pl.pallas_call(
+        front_kernel,
+        grid=(count // block,),
+        out_shape=(
+            jax.ShapeDtypeStruct((total, width), jnp.bfloat16),
+            jax.ShapeDtypeStruct((count, width), jnp.float32),
+            jax.ShapeDtypeStruct((count, width), jnp.float32),
+            jax.ShapeDtypeStruct((count, width), jnp.bfloat16),
+            jax.ShapeDtypeStruct((count, 2 * width), jnp.float32),
+            jax.ShapeDtypeStruct((count, 3 * width), jnp.bfloat16),
+            jax.ShapeDtypeStruct(probs_shape, jnp.float32),
+        ),
+        in_specs=[
+            whole(dest.shape),
+            by_rows(block, width),
+            whole(gathered.shape),
+            whole(rows.shape),
+            whole(scale.shape),
+            whole(bias.shape),
+        ],
+        out_specs=(
+            whole((total, width)),
+            by_rows(block, width),
+            by_rows(block, width),
+            by_rows(block, width),
+            by_rows(block, 2 * width),
+            by_rows(block, 3 * width),
+            pl.BlockSpec((block // WIN,) + probs_shape[1:], lambda i: (i, 0, 0, 0)),
+        ),
+        scratch_shapes=[pltpu.VMEM((count, width), jnp.bfloat16)],
+        cost_estimate=pl.CostEstimate(
+            flops=2 * count * width * width * 8, bytes_accessed=20 * 10**6, transcendentals=0
+        ),
+        compiler_params=pltpu.CompilerParams(vmem_limit_bytes=VMEM_BYTES),
+        name="front",
+    )(dest, tokens, gathered, rows, scale, bias)
+
+
+def back_kernel(
+    narrow,
+    count_ref,
+    place_ref,
+    dest_ref,
+    arrived_ref,
+    cot_ref,
+    tokens_ref,
+    weight_ref,
+    rows_ref,
+    scale_ref,
+    attended_ref,
+    mixed_ref,
+    raw_ref,
+    heads_ref,
+    probs_ref,
+    expert_ref,
+    table_ref,
+    coords_ref,
+    net_ref,
+    inputs_ref,
+    send_ref,
+    keep_ref,
+    sums_ref,
+    grad_bias_ref,
+    grad_scale_ref,
+    grad_heads,
+    low_attended,
+    low_projected,
+):
+    step = pl.program_id(0)
+    block = cot_ref.shape[0]
+    width = MODEL_WIDTH
+    start_row = pl.multiple_of(step * block, block)
+    here = pl.ds(start_row, block)
+    masks_low = lane_masks(jnp.bfloat16)
+    masks = lane_masks(jnp.float32)
+
+    @pl.when(step == 0)
+    def _():
+        sums_ref[...] = jnp.zeros_like(sums_ref)
+        grad_bias_ref[...] = jnp.zeros_like(grad_bias_ref)
+        grad_scale_ref[...] = jnp.zeros_like(grad_scale_ref)
+
+    place = lax.broadcasted_iota(jnp.int32, (block, 1), 0) + start_row
+    live = jnp.where(place < count_ref[0] * IMG_TOK, 1.0, 0.0)
+    feed = take_rows(dest_ref[...], arrived_ref[...])
+    total = cot_ref[...].astype(jnp.float32) * live + feed
+    attended = attended_ref[...]
+    centred = attended - jnp.mean(attended, axis=-1, keepdims=True)
+    spread = lax.rsqrt(jnp.mean(centred * centred, axis=-1, keepdims=True) + 1e-05)
+    unit = centred * spread
+    grad_unit = total * rows_ref[0:1, :]
+    grad_attended = spread * (
+        grad_unit
+        - jnp.mean(grad_unit, axis=-1, keepdims=True)
+        - unit * jnp.mean(grad_unit * unit, axis=-1, keepdims=True)
+    )
+    grad_low = grad_attended.astype(jnp.bfloat16)
+    low_attended[here, :] = grad_low
+    sums_ref[0:1, :width] += jnp.sum(total * unit, axis=0, keepdims=True)
+    sums_ref[1:2, :width] += jnp.sum(total, axis=0, keepdims=True)
+    sums_ref[6:7, :width] += jnp.sum(grad_low.astype(jnp.float32), axis=0, keepdims=True)
+    grad_mixed = dot_cols(grad_low, weight_ref[:, 3 * width : 4 * width]).astype(jnp.bfloat16)
+    for window in range(block // WIN):
+        at = pl.ds(window * WIN, WIN)
+        for group in range(width // GROUP_LANES):
+            start = group * GROUP_LANES
+            cut_q = slice(start, start + GROUP_LANES)
+            cut_k = slice(width + start, width + start + GROUP_LANES)
+            cut_v = slice(2 * width + start, 2 * width + start + GROUP_LANES)
+            query = stack_heads(heads_ref[at, cut_q], masks_low)
+            key = heads_ref[at, cut_k]
+            value = heads_ref[at, cut_v]
+            grad_out = stack_heads(grad_mixed[window * WIN : window * WIN + WIN, cut_q], masks_low)
+            grad_probs = dot_cols(value, grad_out)
+            cosine = dot_cols(key, query)
+            probs = probs_ref[window, group]
+            grad_heads[at, cut_v] = dot(probs.astype(jnp.bfloat16), grad_out)
+            weighed = probs * grad_probs
+            grad_scores = weighed - probs * jnp.sum(weighed, axis=0, keepdims=True)
+            grad_bias_ref[group] += grad_scores
+            grad_scale_ref[group] += jnp.sum(grad_scores * cosine, axis=0, keepdims=True)
+            grad_cosine = (grad_scores * scale_ref[group]).astype(jnp.bfloat16)
+            grad_heads[at, cut_k] = dot(grad_cosine, query)
+            grad_heads[at, cut_q] = pick_heads(dot_rows(grad_cosine, key), masks)
+    for side in range(2):
+        cut = slice(side * width, side * width + width)
+        raw = raw_ref[:, cut]
+        inverse = lax.rsqrt(head_sums(raw * raw) + 1e-06)
+        unit = raw * inverse
+        grad = grad_heads[:, cut]
+        low_projected[here, cut] = (inverse * (grad - unit * head_sums(grad * unit))).astype(
+            jnp.bfloat16
+        )
+    low_projected[here, 2 * width :] = grad_heads[:, 2 * width :].astype(jnp.bfloat16)
+    grad_projected = low_projected[here, :]
+    sums_ref[4:5, :width] += jnp.sum(
+        grad_projected[:, :width].astype(jnp.float32), axis=0, keepdims=True
+    )
+    sums_ref[5:6, :width] += jnp.sum(
+        grad_projected[:, 2 * width :].astype(jnp.float32), axis=0, keepdims=True
+    )
+    inputs_ref[...] = (total + dot_cols(grad_projected, weight_ref[:, : 3 * width])).astype(
+        jnp.bfloat16
+    )
+
+    @pl.when(step == pl.num_programs(0) - 1)
+    def _():
+        grad_qkv = dot_rows(tokens_ref[...], low_projected[...])
+        grad_out = dot_rows(mixed_ref[...], low_attended[...])
+        grad_dense = jnp.concatenate([grad_qkv, grad_out], axis=1)
+        chips = keep_ref.shape[0]
+        on_first = place_ref[0] == 0
+        share = width // (2 * chips)
+        for chip in range(chips):
+            cuts = []
+            for core in range(2):
+                row = (chip // narrow * 2 * narrow + core * narrow + chip % narrow) * share
+                rows = grad_dense[row : row + share]
+                cuts.append(
+                    jnp.concatenate([rows[:, : 2 * width], rows[:, 2 * width :]], axis=0)
+                )
+            keep_ref[chip] = jnp.where(on_first, cuts[0], cuts[1])
+            send_ref[chip] = jnp.where(on_first, cuts[1], cuts[0]).astype(jnp.bfloat16)
+        sums_ref[2:4, :width] = expert_ref[1:3, :]
+        row = lax.broadcasted_iota(jnp.int32, (EXPERTS, width), 0)
+        sums_ref[ROUTE_ROWS:, :width] = jnp.where(row == place_ref[1], expert_ref[3:4, :], 0.0)
+        for group in range(grad_scale_ref.shape[0]):
+            at = SCALE_ROWS + group
+            sums_ref[at : at + 1, : GROUP * WIN] = grad_scale_ref[group]
+        net_back(
+            sum_offsets(grad_bias_ref), table_ref[...], coords_ref[...], net_ref, sums_ref
+        )
+
+
+def sum_offsets(grad_bias_ref):
+    row = lax.broadcasted_iota(jnp.int32, (GROUP * WIN, TABLE), 0)
+    lane = lax.broadcasted_iota(jnp.int32, (GROUP * WIN, TABLE), 1)
+    query = row % WIN
+    aim = TABLE_MID - STRIDE * (query // SIDE) - query % SIDE
+    spreads = [
+        jnp.where((lane == aim) & (row // WIN == h), 1.0, 0.0).astype(jnp.bfloat16)
+        for h in range(GROUP)
+    ]
+    sums = []
+    for group in range(grad_bias_ref.shape[0]):
+        grad = grad_bias_ref[group]
+        high = grad.astype(jnp.bfloat16)
+        rest = grad - high.astype(jnp.float32)
+        middle = rest.astype(jnp.bfloat16)
+        last = (rest - middle.astype(jnp.float32)).astype(jnp.bfloat16)
+        parts = jnp.concatenate([high, middle, last], axis=0)
+        for h in range(GROUP):
+            spread = dot(parts, spreads[h])
+            spread = spread[:WIN] + spread[WIN : 2 * WIN] + spread[2 * WIN :]
+            rows = spread[:SIDE]
+            for r in range(1, SIDE):
+                rows = rows + pltpu.roll(spread[SIDE * r : SIDE * r + SIDE], STRIDE * r, 1)
+            rows = pltpu.roll(rows, 0, 1, stride=1, stride_axis=0)
+            sums.append(jnp.sum(rows, axis=0, keepdims=True))
+    return jnp.concatenate(sums, axis=0)
+
+
+def net_back(grad, table, coords, net_ref, sums_ref):
+    heads = table.shape[0]
+    second, shift, first = net_ref[:heads], net_ref[heads : heads + 1], net_ref[heads + 1 : heads + 3]
+    pre = coords[:, 0:1] * first[0:1] + coords[:, 1:2] * first[1:2] + shift
+    hidden, slope = gelu_pair(pre)
+    grad_logits = grad * table * (1.0 - table * (1.0 / 16.0))
+    sums_ref[SECOND_ROWS : SECOND_ROWS + heads, :] = jnp.dot(
+        grad_logits, hidden, precision=highest, preferred_element_type=jnp.float32
+    )
+    grad_pre = slope * lax.dot_general(
+        grad_logits, second, contract_rows, precision=highest, preferred_element_type=jnp.float32
+    )
+    sums_ref[SHIFT_ROW : SHIFT_ROW + 1, :] = jnp.sum(grad_pre, axis=0, keepdims=True)
+    for k in range(2):
+        sums_ref[FIRST_ROWS + k : FIRST_ROWS + k + 1, :] = jnp.sum(
+            grad_pre * coords[:, k : k + 1], axis=0, keepdims=True
+        )
+
+
+def call_back(
+    images, dest, arrived, cotangent, tokens, gathered, rows, scale, attended, mixed, raw, heads, probs, sums_expert, table, net
+):
+    count, width = tokens.shape
+    narrow = lax.axis_size("narrow")
+    chips = narrow * lax.axis_size("wide") // 2
+    share = width // (2 * chips)
+    coords = jnp.asarray(offset_coords())
+    place = jnp.stack([lax.axis_index("wide") % 2, lax.axis_index(("wide", "narrow"))])
+    block = token_block(count)
+    groups = width // GROUP_LANES
+    return pl.pallas_call(
+        functools.partial(back_kernel, narrow),
+        grid=(count // block,),
+        out_shape=(
+            jax.ShapeDtypeStruct((count, width), jnp.bfloat16),
+            jax.ShapeDtypeStruct((chips, 2 * share, 2 * width), jnp.bfloat16),
+            jax.ShapeDtypeStruct((chips, 2 * share, 2 * width), jnp.float32),
+            jax.ShapeDtypeStruct((ROUTE_ROWS + EXPERTS, SUM_LANES), jnp.float32),
+        ),
+        in_specs=[
+            pl.BlockSpec(memory_space=pltpu.SMEM),
+            pl.BlockSpec(memory_space=pltpu.SMEM),
+            pl.BlockSpec((1, block), lambda i: (0, i)),
+            whole(arrived.shape),
+            by_rows(block, width),
+            whole(tokens.shape),
+            whole(gathered.shape),
+            whole(rows.shape),
+            whole(scale.shape),
+            by_rows(block, width),
+            whole(mixed.shape),
+            by_rows(block, 2 * width),
+            by_rows(block, 3 * width),
+            pl.BlockSpec((block // WIN,) + probs.shape[1:], lambda i: (i, 0, 0, 0)),
+            whole(sums_expert.shape),
+            whole(table.shape),
+            whole(coords.shape),
+            whole(net.shape),
+        ],
+        out_specs=(
+            by_rows(block, width),
+            whole((chips, 2 * share, 2 * width)),
+            whole((chips, 2 * share, 2 * width)),
+            whole((ROUTE_ROWS + EXPERTS, SUM_LANES)),
+        ),
+        scratch_shapes=[
+            pltpu.VMEM((groups, WIN, GROUP * WIN), jnp.float32),
+            pltpu.VMEM((groups, 1, GROUP * WIN), jnp.float32),
+            pltpu.VMEM((block, 3 * width), jnp.float32),
+            pltpu.VMEM((count, width), jnp.bfloat16),
+            pltpu.VMEM((count, 3 * width), jnp.bfloat16),
+        ],
+        cost_estimate=pl.CostEstimate(
+            flops=2 * count * width * width * 16, bytes_accessed=20 * 10**6, transcendentals=0
+        ),
+        compiler_params=pltpu.CompilerParams(vmem_limit_bytes=VMEM_BYTES),
+        name="back",
+    )(
+        images,
+        place.astype(jnp.int32),
+        dest,
+        arrived,
+        cotangent,
+        tokens,
+        gathered,
+        rows,
+        scale,
+        attended,
+        mixed,
+        raw,
+        heads,
+        probs,
+        sums_expert,
+        table,
+        coords,
+        net,
+    )
+
+
+def layer_kernel(count_ref, dest_ref, branch_ref, section_ref, out_ref):
+    block = out_ref.shape[0]
+    place = lax.broadcasted_iota(jnp.int32, (block, 1), 0) + pl.program_id(0) * block
+    live = jnp.where(place < count_ref[0] * IMG_TOK, 1.0, 0.0)
+    branch = take_rows(dest_ref[...], branch_ref[...])
+    out_ref[...] = ((section_ref[...] + branch) * live).astype(jnp.bfloat16)
+
+
+def call_layer(images, dest, branch, section):
+    count, width = section.shape
+    block = token_block(count)
+    return pl.pallas_call(
+        layer_kernel,
+        grid=(count // block,),
+        out_shape=jax.ShapeDtypeStruct((count, width), jnp.bfloat16),
+        in_specs=[
+            pl.BlockSpec(memory_space=pltpu.SMEM),
+            pl.BlockSpec((1, block), lambda i: (0, i)),
+            whole(branch.shape),
+            by_rows(block, width),
+        ],
+        out_specs=by_rows(block, width),
+        cost_estimate=pl.CostEstimate(
+            flops=2 * count * width * branch.shape[0], bytes_accessed=4 * 10**6, transcendentals=0
+        ),
+        compiler_params=pltpu.CompilerParams(vmem_limit_bytes=VMEM_BYTES),
+        name="layer",
+    )(images, dest, branch, section)
+
+
+def expert_kernel(
+    rows_ref,
+    cot_ref,
+    first_ref,
+    second_ref,
+    bias_one_ref,
+    vecs_ref,
+    branch_ref,
+    back_ref,
+    hidden_ref,
+    grad_pre_ref,
+    grad_result_ref,
+    sums_ref,
+    sum_pre_ref,
+):
+    @pl.when(pl.program_id(0) == 0)
+    def _():
+        sums_ref[...] = jnp.zeros_like(sums_ref)
+        sum_pre_ref[...] = jnp.zeros_like(sum_pre_ref)
+
+    low = rows_ref[...]
+    rows = low.astype(jnp.float32)
+    bias_two, gain, shift, route = (vecs_ref[i : i + 1, :] for i in range(4))
+    hidden, slope = gelu_pair(dot(low, first_ref[...]) + bias_one_ref[...])
+    hidden = hidden.astype(jnp.bfloat16)
+    hidden_ref[...] = hidden
+    result = (dot(hidden, second_ref[...]) + bias_two).astype(jnp.bfloat16).astype(jnp.float32)
+    gating = jax.nn.sigmoid(jnp.sum(rows * route, axis=-1, keepdims=True))
+    centred = result - jnp.mean(result, axis=-1, keepdims=True)
+    spread = lax.rsqrt(jnp.mean(centred * centred, axis=-1, keepdims=True) + 1e-05)
+    unit = centred * spread
+    normed = unit * gain + shift
+    branch_ref[...] = (normed * gating).astype(jnp.bfloat16)
+    cot = cot_ref[...].astype(jnp.float32)
+    grad_gate = jnp.sum(cot * normed, axis=-1, keepdims=True)
+    gated = cot * gating
+    grad_unit = gated * gain
+    grad_result = (
+        spread
+        * (
+            grad_unit
+            - jnp.mean(grad_unit, axis=-1, keepdims=True)
+            - unit * jnp.mean(grad_unit * unit, axis=-1, keepdims=True)
+        )
+    ).astype(jnp.bfloat16)
+    grad_result_ref[...] = grad_result
+    grad_logit = (
+        (grad_gate * gating * (1.0 - gating)).astype(jnp.bfloat16).astype(jnp.float32)
+    )
+    sums_ref[0:1, :] += jnp.sum(grad_result.astype(jnp.float32), axis=0, keepdims=True)
+    sums_ref[1:2, :] += jnp.sum(gated * unit, axis=0, keepdims=True)
+    sums_ref[2:3, :] += jnp.sum(gated, axis=0, keepdims=True)
+    sums_ref[3:4, :] += jnp.sum(rows * grad_logit, axis=0, keepdims=True)
+    grad_pre = (dot_cols(grad_result, second_ref[...]) * slope).astype(jnp.bfloat16)
+    grad_pre_ref[...] = grad_pre
+    sum_pre_ref[...] += jnp.sum(grad_pre.astype(jnp.float32), axis=0, keepdims=True)
+    back_ref[...] = (dot_cols(grad_pre, first_ref[...]) + grad_logit * route).astype(jnp.bfloat16)
+
+
+def call_expert(rows, cot, first, second, bias_one, vecs):
+    count, width = rows.shape
+    ff = first.shape[1]
+    block = math.gcd(count, 256)
+    return pl.pallas_call(
+        expert_kernel,
+        grid=(count // block,),
+        out_shape=(
+            jax.ShapeDtypeStruct((count, width), jnp.bfloat16),
+            jax.ShapeDtypeStruct((count, width), jnp.bfloat16),
+            jax.ShapeDtypeStruct((count, ff), jnp.bfloat16),
+            jax.ShapeDtypeStruct((count, ff), jnp.bfloat16),
+            jax.ShapeDtypeStruct((count, width), jnp.bfloat16),
+            jax.ShapeDtypeStruct((8, width), jnp.float32),
+            jax.ShapeDtypeStruct((1, ff), jnp.float32),
+        ),
+        in_specs=[
+            by_rows(block, width),
+            by_rows(block, width),
+            whole(first.shape),
+            whole(second.shape),
+            whole(bias_one.shape),
+            whole(vecs.shape),
+        ],
+        out_specs=(
+            by_rows(block, width),
+            by_rows(block, width),
+            by_rows(block, ff),
+            by_rows(block, ff),
+            by_rows(block, width),
+            whole((8, width)),
+            whole((1, ff)),
+        ),
+        cost_estimate=pl.CostEstimate(
+            flops=8 * count * width * ff, bytes_accessed=16 * 10**6, transcendentals=count * ff
+        ),
+        compiler_params=pltpu.CompilerParams(vmem_limit_bytes=VMEM_BYTES),
+        name="expert",
+    )(rows, cot, first, second, bias_one, vecs)
+
+
+def offset_coords():
+    place = TABLE_MID - np.arange(TABLE)
+    row = (place + STRIDE // 2 - 1) // STRIDE
+    coords = np.stack([row, place - STRIDE * row], axis=1) * (8.0 / (SIDE - 1))
+    return (np.sign(coords) * np.log2(np.abs(coords) + 1.0) / 3.0).astype(np.float32)
+
+
+def bias_table(params):
+    piece_collection = pieces(params)
+    hidden = jax.nn.gelu(
+        jnp.dot(offset_coords(), piece_collection[9], precision=highest) + piece_collection[8]
+    )
+    return 16.0 * jax.nn.sigmoid(jnp.dot(hidden, piece_collection[10], precision=highest)).T
+
+
+def spread_bias(table):
+    places = jnp.arange(WIN, dtype=jnp.int32)
+    coded = STRIDE * (places // SIDE) + places % SIDE
+    index = TABLE_MID + coded[:, None] - coded[None, :]
+    lookup = (index.reshape(1, -1) == jnp.arange(TABLE, dtype=jnp.int32)[:, None]).astype(
+        table.dtype
+    )
+    bias = jnp.dot(table, lookup, precision=highest).reshape(-1, GROUP, WIN, WIN)
+    return bias.transpose(0, 2, 1, 3).reshape(-1, WIN, GROUP * WIN)
+
+
+def per_device_split(
     tokens,
     cotangent,
     routes,
@@ -302,10 +1066,8 @@
     live_f = live_rows.astype(jnp.float32)
     keep_f = kept_rows.astype(jnp.float32)
     clipped = jnp.minimum(dest_slot, slot_total - 1)
-    gathered = lax.all_gather(
-        dense_weight.astype(jnp.bfloat16), ("wide", "narrow"), axis=0, tiled=True
-    )
-    section_one, gating, expert_feed, kept = front_forward(
+    gathered = gather_rows(dense_weight.astype(jnp.bfloat16))
+    section_one, gating, expert_feed, kept = front_forward_split(
         tokens, gathered, small_params, route_ids
     )
 
@@ -376,15 +1138,11 @@
         grad_pre, first_matrix, contract_cols, preferred_element_type=jnp.float32
     ).astype(jnp.bfloat16)
     grad_feed = fan_in(grad_rows)
-    grad_inputs, grad_weights, grad_small_front = front_backward(
+    grad_inputs, grad_weights, grad_small_front = front_backward_split(
         tokens, gathered, small_params, kept, grad_section, grad_gate, grad_feed
     )
     grad_small = grad_small_front + grad_small_tail
-    grad_whole, grad_small = lax.psum((grad_weights, grad_small), ("wide", "narrow"))
-    share_rows = dense_weight.shape[0]
-    grad_dense = lax.dynamic_slice_in_dim(
-        grad_whole, lax.axis_index(("wide", "narrow")) * share_rows, share_rows, 0
-    )
+    grad_dense, grad_small = sum_grads(grad_weights, grad_small)
     dense_out = adamw_step(
         dense_weight, grad_dense, dense_moment, dense_square, dense_rate, weight_decay
     )
@@ -419,6 +1177,184 @@
     )
 
 
+def per_device(
+    tokens,
+    cotangent,
+    routes,
+    images,
+    dense_weight,
+    dense_moment,
+    dense_square,
+    small_params,
+    small_moment,
+    small_square,
+    inner_weight,
+    inner_moment,
+    inner_square,
+    outer_weight,
+    outer_moment,
+    outer_square,
+    expert_bias,
+    bias_moment,
+    bias_square,
+):
+    slices = lax.axis_size(("wide", "narrow"))
+    if slices != EXPERTS:
+        return per_device_split(
+            tokens,
+            cotangent,
+            routes,
+            images,
+            dense_weight,
+            dense_moment,
+            dense_square,
+            small_params,
+            small_moment,
+            small_square,
+            inner_weight,
+            inner_moment,
+            inner_square,
+            outer_weight,
+            outer_moment,
+            outer_square,
+            expert_bias,
+            bias_moment,
+            bias_square,
+        )
+    expert = lax.axis_index(("wide", "narrow"))
+    ff_dev = inner_weight.shape[2]
+    tok_rows = tokens.shape[0]
+    capacity = (5 * tok_rows + 4 * EXPERTS - 1) // (4 * EXPERTS)
+    slot_total = EXPERTS * capacity
+
+    def trade(rows):
+        traded = trade_rows(rows.reshape(slices, capacity, MODEL_WIDTH))
+        return traded.reshape(slot_total, MODEL_WIDTH)
+
+    scale_at = 7 * MODEL_WIDTH
+    share = dense_weight.astype(jnp.bfloat16)
+    (pair, depth), across = axis_bits("narrow")[1:], axis_bits("narrow")[0]
+    held = join(share, pair)
+    held, params = lax.optimization_barrier((held, small_params))
+    table = bias_table(params)
+    net_pieces = pieces(params)
+    net = jnp.concatenate([net_pieces[10].T, net_pieces[8][None, :], net_pieces[9]])
+    vectors = params[:scale_at].reshape(7, MODEL_WIDTH)
+    scale_heads = jnp.exp(params[scale_at : scale_at + ATTENTION_HEADS])
+    scale = jnp.repeat(scale_heads, WIN).reshape(-1, 1, GROUP * WIN)
+    held = join(held, depth)
+    held, table, vectors, scale, route_ids, cot = lax.optimization_barrier(
+        (held, table, vectors, scale, routes, cotangent)
+    )
+    dest, placed_cot = call_assign(images, route_ids, cot, capacity)
+    held = join(held, across, -2)
+    held, table, placed_cot, dest = lax.optimization_barrier((held, table, placed_cot, dest))
+    bias = spread_bias(table)
+    core, *rest = axis_bits("wide")
+    for step in rest:
+        held = join(held, step)
+    held, bias = lax.optimization_barrier((held, bias))
+    gathered = join(held, core, len(rest)).reshape(-1, held.shape[-1])
+    gathered, placed_cot = lax.optimization_barrier((gathered, placed_cot))
+    cot_rows = trade(placed_cot)
+    placed, section, attended, mixed, raw, heads, probs = call_front(
+        dest, tokens, gathered, vectors, scale, bias, capacity
+    )
+    placed, cot_rows = lax.optimization_barrier((placed, cot_rows))
+    expert_rows = trade(placed)
+    first_matrix = inner_weight[0].astype(jnp.bfloat16)
+    second_matrix = outer_weight[0].astype(jnp.bfloat16)
+    route_row = lax.dynamic_slice_in_dim(gathered, 4 * MODEL_WIDTH + expert, 1, 1)
+    vecs = jnp.concatenate(
+        [expert_bias[:, ff_dev:], vectors[2:4], route_row.astype(jnp.float32).reshape(1, -1)]
+    )
+    branch, grad_rows, hidden, grad_pre, grad_result, sums_expert, sum_pre = call_expert(
+        expert_rows, cot_rows, first_matrix, second_matrix, expert_bias[:, :ff_dev], vecs
+    )
+    arrived = trade(grad_rows)
+    grad_outer = dot_rows(hidden, grad_result)
+    grad_inner = dot_rows(expert_rows, grad_pre)
+    grad_bias = jnp.concatenate([sum_pre, sums_expert[0:1]], axis=1)[0]
+    inner_out = adamw_step(
+        inner_weight, grad_inner[None], inner_moment, inner_square, expert_rate, weight_decay
+    )
+    outer_out = adamw_step(
+        outer_weight, grad_outer[None], outer_moment, outer_square, expert_rate, weight_decay
+    )
+    inner_out += (inner_out[0].astype(jnp.bfloat16),)
+    outer_out += (outer_out[0].astype(jnp.bfloat16),)
+    branch, arrived, inner_out, outer_out = lax.optimization_barrier(
+        (branch, arrived, inner_out, outer_out)
+    )
+    branch_rows = trade(branch)
+    grad_inputs, send, keep, sums = call_back(
+        images,
+        dest,
+        arrived,
+        cotangent,
+        tokens,
+        gathered,
+        vectors,
+        scale,
+        attended,
+        mixed,
+        raw,
+        heads,
+        probs,
+        sums_expert,
+        table,
+        net,
+    )
+    held = sum_chip(send, keep)
+    sums = sum_quads(sums, axis_bits("wide"))
+    held, sums, branch_rows = lax.optimization_barrier((held, sums, branch_rows))
+    grad_dense = sum_shares(held)
+    layer_out = call_layer(images, dest, branch_rows, section)
+    share_rows = dense_weight.shape[0]
+    grad_dense = jnp.concatenate([grad_dense[:share_rows], grad_dense[share_rows:]], axis=1)
+    sums = sum_quads(sums, axis_bits("narrow")[1:])
+    sums = sums + swap(sums, across)
+    grad_scale = sums[SCALE_ROWS : SCALE_ROWS + ATTENTION_HEADS // GROUP, : GROUP * WIN]
+    grad_small = jnp.concatenate(
+        [
+            sums[:7, :MODEL_WIDTH].reshape(-1),
+            jnp.sum(grad_scale.reshape(ATTENTION_HEADS, WIN), axis=1) * scale_heads,
+            sums[SHIFT_ROW : FIRST_ROWS + 2].reshape(-1),
+            sums[SECOND_ROWS : SECOND_ROWS + ATTENTION_HEADS].T.reshape(-1),
+        ]
+    )
+    grad_route = lax.dynamic_slice_in_dim(
+        sums[ROUTE_ROWS:, :MODEL_WIDTH], expert * share_rows, share_rows, 1
+    ).T
+    grad_dense = jnp.concatenate([grad_dense, grad_route], axis=1)
+    dense_out = adamw_step(
+        dense_weight, grad_dense, dense_moment, dense_square, dense_rate, weight_decay
+    )
+    small_out = adamw_step(small_params, grad_small, small_moment, small_square, small_rate, 0.0)
+    bias_out = adamw_step(expert_bias, grad_bias[None], bias_moment, bias_square, expert_rate, 0.0)
+    return (
+        layer_out,
+        grad_inputs,
+        dense_out[0],
+        dense_out[1],
+        dense_out[2],
+        small_out[0],
+        small_out[1],
+        small_out[2],
+        inner_out[0],
+        inner_out[1],
+        inner_out[2],
+        inner_out[3],
+        outer_out[0],
+        outer_out[1],
+        outer_out[2],
+        outer_out[3],
+        bias_out[0],
+        bias_out[1],
+        bias_out[2],
+    )
+
+
 def solution(mesh):
     return jax.shard_map(
         per_device,

time: 523 us -> 215 us (0.41); the launches traced: 516 us -> 214 us
  waiting for transfers between devices: 207 us -> 71 us
  local copies, waits for them, and re-layouts: 91.8 us -> 10.4 us
  matrix products: 100 us -> 22.1 us
  Pallas kernels: 0 us -> 58.9 us
  blocking collectives: 38.6 us -> 0 us
  other arithmetic: 48 us -> 11.1 us
  starting transfers between devices: 13.8 us -> 39.2 us
  between operations: 16.8 us -> 1.9 us
    psum x1 -> x0, waiting for transfers between devices: 91.1 us -> none  [per_device(): lax.psum((grad_weights, grad_small), ('wide', 'narrow'))]
    dot_general x28 -> x5, matrix products: 93 us -> 22.1 us  [the longest x2 18.4 us: dot_rows(): lax.dot_general(left, right, contract_rows, preferred_element_type=jnp.fl...]
    pallas_call x0 -> x5, Pallas kernels: none -> 58.9 us  [the longest x1 22.6 us: call_back(): pl.pallas_call(functools.partial(back_kernel, narrow), grid=(count // blo...]
    all_gather x1 -> x0, waiting for transfers between devices: 39.3 us -> none  [per_device(): lax.all_gather(dense_weight.astype(jnp.bfloat16), ('wide', 'narrow'), axi...]
    psum x1 -> x0, blocking collectives: 38.6 us -> none  [per_device(): lax.psum((grad_weights, grad_small), ('wide', 'narrow'))]
    all_to_all x4, waiting for transfers between devices: 76.4 us -> 39.4 us  [trade_rows(): lax.all_to_all(payload, ('wide', 'narrow'), split_axis=0, concat_axis=0,...]
    ppermute x0 -> x13, waiting for transfers between devices: none -> 23.1 us  [swap(): lax.ppermute(value, axis, [(i, i ^ offset) for i in range(lax.axis_size(a...]
    convert_element_type x6 -> x0, local copies, waits for them, and re-layouts: 21 us -> none  [the longest x2 15.4 us: front_backward(): grad_proj_low = grad_projected.astype(jnp.bfloat16)]
  transfers between devices with their start and end apart: 6 -> 18, of which waited for: 6 -> 13; matrix products, arithmetic and copies ran while one was open for 10% -> 15% of each run, Pallas kernels for 0% -> 20%
where the time goes in v1:
time: 215 us; the launch traced here: 214 us
  waiting for transfers between devices  71 us (33%)
  Pallas kernels  58.9 us (27%)
  starting transfers between devices  39.2 us (18%)
  matrix products  22.1 us (10%)
  other arithmetic  11.1 us (5%)
  local copies, waits for them, and re-layouts  10.4 us (5%)
    all_to_all x4, waiting for transfers between devices, trade_rows(): lax.all_to_all(payload, ('wide', 'narrow'), split_axis=0, concat_axis=0,...  39.4 us
    ppermute x13, waiting for transfers between devices, swap(): lax.ppermute(value, axis, [(i, i ^ offset) for i in range(lax.axis_size(a...  23.1 us
    pallas_call x1, Pallas kernels, call_back(): pl.pallas_call(functools.partial(back_kernel, narrow), grid=(count // blo...  22.6 us
    ppermute x13, starting transfers between devices, swap(): lax.ppermute(value, axis, [(i, i ^ offset) for i in range(lax.axis_size(a...  19.2 us
    dot_general x2, matrix products, dot_rows(): lax.dot_general(left, right, contract_rows, preferred_element_type=jnp.fl...  18.4 us
    pallas_call x1, Pallas kernels, call_expert(): pl.pallas_call(expert_kernel, grid=(count // block,), out_shape=(jax.Shap...  15.7 us
    all_to_all x4, starting transfers between devices, trade_rows(): lax.all_to_all(payload, ('wide', 'narrow'), split_axis=0, concat_axis=0,...  15.3 us
    pallas_call x1, Pallas kernels, call_front(): pl.pallas_call(front_kernel, grid=(count // block,), out_shape=(jax.Shape...  14.6 us
  transfers between devices with their start and end apart: 18, of which 13 were waited for; matrix products, arithmetic and copies ran while one was open for 15% of the time, Pallas kernels for 20%

profile of v1, /device:TPU:0, one launch (start us, length us, event | category | flops | bytes accessed | tf_op | source)
XLA Modules:
  0.0 214.5 jit_solution(16842995482608747633)
XLA Ops:
  0.7 1.0 convert_element_type.30
  1.7 3.0 %collective-permute-start = (bf16[12,1568]{1,0:T(8,128)(2,1)S(1)}, bf16[12,1568]{1,0:T(8,128)(2,1)S(1)}, u32[]{:S(2)}, u32[]{:S(2)}) collective-permute-start(bf16[12,1568]{1,0:T(8,128)(2,1)S(1)} %convert_element_type.30), channel_id=1, source_target_pairs={{0,2},{1,3},{2,0},{3,1},{4,6},{5,7},{6,4},{7,5},{8,10},{9,11},{10,... | collective-permute-start | bytes 112904 | tf_op jit(solution)/shard_map/ppermute | solution.py:296
  4.7 0.9 convert_bitcast_fusion.2
  5.6 1.2 collective-permute-done
  6.9 0.8 slice.67
  7.6 0.8 slice.66
  8.4 0.8 slice.65
  9.2 3.1 %collective-permute-start.1 = (bf16[2,12,1568]{2,1,0:T(8,128)(2,1)S(1)}, bf16[2,12,1568]{2,1,0:T(8,128)(2,1)S(1)}, u32[]{:S(2)}, u32[]{:S(2)}) collective-permute-start(bf16[2,12,1568]{2,1,0:T(8,128)(2,1)S(1)} %maximum_select_fusion.4), channel_id=1, source_target_pairs={{0,4},{1,5},{2,6},{3,7},{4,0},{5,1},{6,2},{7,3},{8,12},{9,13},{10,... | collective-permute-start | bytes 225800 | tf_op jit(solution)/shard_map/ppermute | solution.py:296
  12.3 0.3 reshape.281
  12.6 1.8 fusion.17
  14.3 0.6 fusion.10.table_ref
  15.3 2.7 %collective-permute-start.2 = (bf16[2,2,12,1568]{3,2,1,0:T(8,128)(2,1)S(1)}, bf16[2,2,12,1568]{3,2,1,0:T(8,128)(2,1)S(1)}, u32[]{:S(2)}, u32[]{:S(2)}) collective-permute-start(bf16[2,2,12,1568]{3,2,1,0:T(8,128)(2,1)S(1)} %maximum_select_fusion.3), channel_id=1, source_target_pairs={{0,1},{1,0},{2,3},{3,2},{4,5},{5,4},{6,7},{7,6},{8,9},{9,8},{10,11... | collective-permute-start | bytes 451592 | tf_op jit(solution)/shard_map/ppermute | solution.py:296
  18.8 2.8 %assign.1 = (s32[1,1024]{1,0:T(1,128)S(1)}, bf16[1280,384]{1,0:T(8,128)(2,1)}) custom-call(s32[1]{0:T(128)S(6)} %copy.50.count_ref, s32[1,1024]{1,0:T(1,128)S(1)} %bitcast.69, bf16[1024,384]{1,0:T(8,128)(2,1)S(1)} %copy-done.1), custom_call_target="tpu_custom_call" | custom-call | flops 1006632960 | bytes 4000000 | tf_op jit(solution)/shard_map/assign/pallas_call | solution.py:477
  21.5 0.4 collective-permute-done.2
  21.9 0.2 maximum_select_fusion.2
  22.1 2.1 collective-permute-start.3
  24.3 1.4 fusion
  25.7 0.2 reshape.285
  25.9 0.3 copy.49
  26.2 0.3 reshape.286.bias_ref
  26.4 2.7 %collective-permute-done.3 = bf16[2,2,24,1568]{3,2,1,0:T(8,128)(2,1)S(1)} collective-permute-done((bf16[2,2,24,1568]{3,2,1,0:T(8,128)(2,1)S(1)}, bf16[2,2,24,1568]{3,2,1,0:T(8,128)(2,1)S(1)}, u32[]{:S(2)}, u32[]{:S(2)}) %collective-permute-start.3) | collective-permute-done | bytes 301088 | tf_op jit(solution)/shard_map/ppermute | solution.py:296
  29.2 0.1 maximum_select_fusion.1
  29.4 2.1 collective-permute-done.4
  31.4 0.2 maximum_select_fusion
  31.8 6.2 %all-to-all-start = ((bf16[32,40,384]{2,1,0:T(8,128)(2,1)}), bf16[32,40,384]{2,1,0:T(8,128)(2,1)S(1)}, u32[]{:S(2)}, u32[]{:S(2)}) async-start(bf16[32,40,384]{2,1,0:T(8,128)(2,1)} %bitcast.14), calls=%async_computation | async-start | bytes 1966080 | tf_op jit(solution)/shard_map/all_to_all | solution.py:283
  38.1 14.6 %front.1 = (bf16[1280,384]{1,0:T(8,128)(2,1)}, f32[1024,384]{1,0:T(8,128)S(1)}, f32[1024,384]{1,0:T(8,128)}, bf16[1024,384]{1,0:T(8,128)(2,1)S(1)}, f32[1024,768...) custom-call(s32[1,1024]{1,0:T(1,128)S(1)} %get-tuple-element.78.dest_ref, ...), custom_call_target="tpu_custom_call" | custom-call | flops 2415919104 | bytes 20000000 | tf_op jit(solution)/shard_map/front/pallas_call | solution.py:578
  52.7 1.2 copy-done.7
  53.9 0.9 copy-done.9
  54.8 9.5 %all-to-all-done = bf16[32,40,384]{2,1,0:T(8,128)(2,1)S(1)} async-done(((bf16[32,40,384]{2,1,0:T(8,128)(2,1)}), bf16[32,40,384]{2,1,0:T(8,128)(2,1)S(1)}, u32[]{:S(2)}, u32[]{:S(2)}) %all-to-all-start) | async-done | bytes 983072 | tf_op jit(solution)/shard_map/all_to_all | solution.py:283
  64.2 3.5 %all-to-all-start.1 = ((bf16[32,40,384]{2,1,0:T(8,128)(2,1)}), bf16[32,40,384]{2,1,0:T(8,128)(2,1)}, u32[]{:S(2)}, u32[]{:S(2)}) async-start(bf16[32,40,384]{2,1,0:T(8,128)(2,1)} %bitcast.16), calls=%async_computation.1 | async-start | bytes 1966080 | tf_op jit(solution)/shard_map/all_to_all | solution.py:283
  67.8 1.9 convert_bitcast_fusion.1.first_ref
  69.8 0.4 copy-done.15
  70.2 1.1 convert_bitcast_fusion.second_ref
  71.4 0.2 convert_reduce_fusion.1
  71.6 22.2 %all-to-all-done.1 = bf16[32,40,384]{2,1,0:T(8,128)(2,1)} async-done(((bf16[32,40,384]{2,1,0:T(8,128)(2,1)}), bf16[32,40,384]{2,1,0:T(8,128)(2,1)}, u32[]{:S(2)}, u32[]{:S(2)}) %all-to-all-start.1) | async-done | bytes 983072 | tf_op jit(solution)/shard_map/all_to_all | solution.py:283
  93.8 15.7 %expert.1 = (bf16[1280,384]{1,0:T(8,128)(2,1)}, bf16[1280,384]{1,0:T(8,128)(2,1)}, bf16[1280,1536]{1,0:T(8,128)(2,1)}, bf16[1280,1536]{1,0:T(8,128)(2,1)}, bf16[...) custom-call(bf16[1280,384]{1,0:T(8,128)(2,1)} %bitcast.17.rows_ref, ...), custom_call_target="tpu_custom_call" | custom-call | flops 6039797760 | bytes 16000000 | tf_op jit(solution)/shard_map/expert/pallas_call | solution.py:972
  109.5 0.9 copy-done.11
  110.4 2.6 %all-to-all-start.2 = ((bf16[32,40,384]{2,1,0:T(8,128)(2,1)}), bf16[32,40,384]{2,1,0:T(8,128)(2,1)S(1)}, u32[]{:S(2)}, u32[]{:S(2)}) async-start(bf16[32,40,384]{2,1,0:T(8,128)(2,1)} %bitcast.20), calls=%async_computation.2 | async-start | bytes 1966080 | tf_op jit(solution)/shard_map/all_to_all | solution.py:283
  113.2 11.3 %fusion.29 = (bf16[1,384,1536]{2,1,0:T(8,128)(2,1)}, f32[1,384,1536]{2,1,0:T(8,128)}, f32[1,384,1536]{2,1,0:T(8,128)}, f32[1,384,1536]{2,1,0:T(8,128)}) fusion(f32[1,384,1536]{2,1,0:T(8,128)} %param.31, f32[1,384,1536]{2,1,0:T(8,128)} %param.32, f32[1,384,1536]{2,1,0:T(8,128)} %param.33, bf16[1280,384]{1,0:T(8,128)(2,1)} %bitcast.17.rows_ref, ...), kind=kOutput, calls=%fused_computation.72 | convolution fusion | flops 1519386624 | bytes 20250624 | tf_op jit(solution)/shard_map/dot_general | solution.py:393
  124.5 7.0 %fusion.27 = (bf16[1,1536,384]{2,1,0:T(8,128)(2,1)}, f32[1,1536,384]{2,1,0:T(8,128)}, f32[1,1536,384]{2,1,0:T(8,128)}, f32[1,1536,384]{2,1,0:T(8,128)}) fusion(f32[1,1536,384]{2,1,0:T(8,128)S(1)} %copy-done.16, f32[1,1536,384]{2,1,0:T(8,128)S(1)} %copy-done.26, f32[1,1536,384]{2,1,0:T(8,128)S(1)} %copy-done.27, bf16[1280,1536]{1,0:T(8,128)(2,1)S(1)} %copy-done.28, ...), kind=kOutput, calls=%fused_computation.71 | convolution fusion | flops 1519386624 | bytes 20250624 | tf_op jit(solution)/shard_map/dot_general | solution.py:393
  131.6 7.7 %all-to-all-done.2 = bf16[32,40,384]{2,1,0:T(8,128)(2,1)S(1)} async-done(((bf16[32,40,384]{2,1,0:T(8,128)(2,1)}), bf16[32,40,384]{2,1,0:T(8,128)(2,1)S(1)}, u32[]{:S(2)}, u32[]{:S(2)}) %all-to-all-start.2) | async-done | bytes 983072 | tf_op jit(solution)/shard_map/all_to_all | solution.py:283
  139.3 2.9 %all-to-all-start.3 = ((bf16[32,40,384]{2,1,0:T(8,128)(2,1)}), bf16[32,40,384]{2,1,0:T(8,128)(2,1)S(1)}, u32[]{:S(2)}, u32[]{:S(2)}) async-start(bf16[32,40,384]{2,1,0:T(8,128)(2,1)} %bitcast.28), calls=%async_computation.3 | async-start | bytes 1966080 | tf_op jit(solution)/shard_map/all_to_all | solution.py:283
  142.4 1.1 copy-done.4
  143.5 1.1 copy-done.10
  144.7 22.6 %back.1 = (bf16[1024,384]{1,0:T(8,128)(2,1)}, bf16[16,24,768]{2,1,0:T(8,128)(2,1)S(1)}, f32[16,24,768]{2,1,0:T(8,128)S(1)}, f32[64,512]{1,0:T(8,128)S(1)}) custom-call(s32[1]{0:T(128)S(6)} %copy.50.count_ref, s32[2]{0:T(128)S(1)} %pad_add_fusion.place_ref, s32[1,1024]{1,0:T(1,128)S(1)} %get-tuple-element.78.dest_ref, bf16[1280,384]{1,0:T(8,128)(2,1)S(1)} %bitcast.67, ...), custom_call_target="tpu_custom_call" | custom-call | flops 4831838208 | bytes 20000000 | tf_op jit(solution)/shard_map/back/pallas_call | solution.py:810
  167.4 1.5 collective-permute-start.8
  168.9 0.6 collective-permute-start.7
  169.5 3.2 %collective-permute-done.8 = f32[64,512]{1,0:T(8,128)S(1)} collective-permute-done((f32[64,512]{1,0:T(8,128)S(1)}, f32[64,512]{1,0:T(8,128)S(1)}, u32[]{:S(2)}, u32[]{:S(2)}) %collective-permute-start.8) | collective-permute-done | bytes 131104 | tf_op jit(solution)/shard_map/ppermute | solution.py:296
  172.8 3.3 %collective-permute-done.7 = f32[64,512]{1,0:T(8,128)S(1)} collective-permute-done((f32[64,512]{1,0:T(8,128)S(1)}, f32[64,512]{1,0:T(8,128)S(1)}, u32[]{:S(2)}, u32[]{:S(2)}) %collective-permute-start.7) | collective-permute-done | bytes 131104 | tf_op jit(solution)/shard_map/ppermute | solution.py:296
  176.1 0.9 add_convert_fusion
  177.1 3.5 %collective-permute-start.11 = (f32[64,512]{1,0:T(8,128)S(1)}, f32[64,512]{1,0:T(8,128)S(1)}, u32[]{:S(2)}, u32[]{:S(2)}) collective-permute-start(f32[64,512]{1,0:T(8,128)S(1)} %add_add_fusion.1), channel_id=1, source_target_pairs={{0,6},{1,7},{2,4},{3,5},{4,2},{5,3},{6,0},{7,1},{8,14},{9,15},{10,... | collective-permute-start | bytes 393224 | tf_op jit(solution)/shard_map/ppermute | solution.py:296
  180.6 0.9 collective-permute-start.9
  181.5 3.9 %collective-permute-done.11 = f32[64,512]{1,0:T(8,128)S(1)} collective-permute-done((f32[64,512]{1,0:T(8,128)S(1)}, f32[64,512]{1,0:T(8,128)S(1)}, u32[]{:S(2)}, u32[]{:S(2)}) %collective-permute-start.11) | collective-permute-done | bytes 131104 | tf_op jit(solution)/shard_map/ppermute | solution.py:296
  185.4 6.2 %collective-permute-done.10 = f32[64,512]{1,0:T(8,128)S(1)} collective-permute-done((f32[64,512]{1,0:T(8,128)S(1)}, f32[64,512]{1,0:T(8,128)S(1)}, u32[]{:S(2)}, u32[]{:S(2)}) %collective-permute-start.10) | collective-permute-done | bytes 131104 | tf_op jit(solution)/shard_map/ppermute | solution.py:296
  191.6 1.5 collective-permute-start.12
  193.1 0.7 multiply_subtract_fusion.4
  193.8 4.7 %all-to-all-start.4 = ((bf16[16,24,768]{2,1,0:T(8,128)(2,1)}), bf16[16,24,768]{2,1,0:T(8,128)(2,1)S(1)}, u32[]{:S(2)}, u32[]{:S(2)}) async-start(bf16[16,24,768]{2,1,0:T(8,128)(2,1)} %add_convert_fusion), calls=%async_computation.4 | async-start | bytes 1179648 | tf_op jit(solution)/shard_map/all_to_all | solution.py:375
  198.6 3.2 %layer.1 = bf16[1024,384]{1,0:T(8,128)(2,1)} custom-call(s32[1]{0:T(128)S(6)} %copy.50.count_ref, s32[1,1024]{1,0:T(1,128)S(1)} %get-tuple-element.78.dest_ref, bf16[1280,384]{1,0:T(8,128)(2,1)S(1)} %bitcast.66, f32[1024,384]{1,0:T(8,128)S(1)} %copy-done.8), custom_call_target="tpu_custom_call" | custom-call | flops 1006632960 | bytes 4000000 | tf_op jit(solution)/shard_map/layer/pallas_call | solution.py:890
  201.8 1.0 add.215
  203.0 0.1 copy.47
  203.2 0.2 reshape.300
  203.6 1.5 multiply_subtract_fusion.3
  205.0 8.5 %all-to-all-done.4 = bf16[16,24,768]{2,1,0:T(8,128)(2,1)S(1)} async-done(((bf16[16,24,768]{2,1,0:T(8,128)(2,1)}), bf16[16,24,768]{2,1,0:T(8,128)(2,1)S(1)}, u32[]{:S(2)}, u32[]{:S(2)}) %all-to-all-start.4) | async-done | bytes 589856 | tf_op jit(solution)/shard_map/all_to_all | solution.py:375
  213.7 0.8 multiply_subtract_fusion.2
  (103 shorter events, 1.9 us)
Async XLA Ops:
  0.7 14.3 %copy-start.18 = (f32[10380]{0:T(1024)S(1)}, f32[10380]{0:T(1024)}, u32[]{:S(2)}) copy-start(f32[10380]{0:T(1024)} %param.28) | copy-start | bytes 124564
  0.7 14.5 %slice-start = ((f32[10380]{0:T(1024)}), f32[2688]{0:T(1024)S(1)}, s32[]{:S(2)}) async-start(f32[10380]{0:T(1024)} %param.28), calls=%async_computation.5 | async-start | bytes 24576 | tf_op jit(solution)/shard_map/slice | solution.py:1242
  0.7 18.1 %copy-start.1 = (bf16[1024,384]{1,0:T(8,128)(2,1)S(1)}, bf16[1024,384]{1,0:T(8,128)(2,1)}, u32[]{:S(2)}) copy-start(bf16[1024,384]{1,0:T(8,128)(2,1)} %cot_ref.2) | copy-start | bytes 2359300
  0.7 18.1 %copy-start.5 = (s32[1024,1]{0,1:T(1,128)S(1)}, s32[1024,1]{0,1:T(1,128)}, u32[]{:S(2)}) copy-start(s32[1024,1]{0,1:T(1,128)} %param.23) | copy-start | bytes 12292
  1.7 5.1 %collective-permute-start = (bf16[12,1568]{1,0:T(8,128)(2,1)S(1)}, bf16[12,1568]{1,0:T(8,128)(2,1)S(1)}, u32[]{:S(2)}, u32[]{:S(2)}) collective-permute-start(bf16[12,1568]{1,0:T(8,128)(2,1)S(1)} %convert_element_type.30), channel_id=1, source_target_pairs={{0,2},{1,3},{2,0},{3,1},{4,6},{5,7},{6,4},{7,5},{8,10},{9,11},{10,... | collective-permute-start | bytes 112904 | tf_op jit(solution)/shard_map/ppermute | solution.py:296
  9.2 6.1 %collective-permute-start.1 = (bf16[2,12,1568]{2,1,0:T(8,128)(2,1)S(1)}, bf16[2,12,1568]{2,1,0:T(8,128)(2,1)S(1)}, u32[]{:S(2)}, u32[]{:S(2)}) collective-permute-start(bf16[2,12,1568]{2,1,0:T(8,128)(2,1)S(1)} %maximum_select_fusion.4), channel_id=1, source_target_pairs={{0,4},{1,5},{2,6},{3,7},{4,0},{5,1},{6,2},{7,3},{8,12},{9,13},{10,... | collective-permute-start | bytes 225800 | tf_op jit(solution)/shard_map/ppermute | solution.py:296
  12.6 8.9 %copy-start.13 = (f32[512,12]{1,0:T(8,128)}, f32[512,12]{1,0:T(8,128)S(1)}, u32[]{:S(2)}) copy-start(f32[512,12]{1,0:T(8,128)S(1)} %reshape.281) | copy-start | bytes 73732
  15.3 6.6 %collective-permute-start.2 = (bf16[2,2,12,1568]{3,2,1,0:T(8,128)(2,1)S(1)}, bf16[2,2,12,1568]{3,2,1,0:T(8,128)(2,1)S(1)}, u32[]{:S(2)}, u32[]{:S(2)}) collective-permute-start(bf16[2,2,12,1568]{3,2,1,0:T(8,128)(2,1)S(1)} %maximum_select_fusion.3), channel_id=1, source_target_pairs={{0,1},{1,0},{2,3},{3,2},{4,5},{5,4},{6,7},{7,6},{8,9},{9,8},{10,11... | collective-permute-start | bytes 451592 | tf_op jit(solution)/shard_map/ppermute | solution.py:296
  22.1 7.1 %collective-permute-start.3 = (bf16[2,2,24,1568]{3,2,1,0:T(8,128)(2,1)S(1)}, bf16[2,2,24,1568]{3,2,1,0:T(8,128)(2,1)S(1)}, u32[]{:S(2)}, u32[]{:S(2)}) collective-permute-start(bf16[2,2,24,1568]{3,2,1,0:T(8,128)(2,1)S(1)} %maximum_select_fusion.2), channel_id=1, source_target_pairs={{0,16},{8,24},{16,0},{24,8},{1,17},{9,25},{17,1},{25,9},{2,18},{10... | collective-permute-start | bytes 903176 | tf_op jit(solution)/shard_map/ppermute | solution.py:296
  29.3 2.1 collective-permute-start.4
  31.7 6.4 %copy-start.3 = (bf16[1024,384]{1,0:T(8,128)(2,1)S(1)}, bf16[1024,384]{1,0:T(8,128)(2,1)}, u32[]{:S(2)}) copy-start(bf16[1024,384]{1,0:T(8,128)(2,1)} %tokens_ref.3) | copy-start | bytes 2359300
  31.8 39.6 %copy-start = (bf16[2,2,2,2,24,1568]{5,4,3,2,1,0:T(8,128)(2,1)}, bf16[2,2,2,2,24,1568]{5,4,3,2,1,0:T(8,128)(2,1)S(1)}, u32[]{:S(2)}) copy-start(bf16[2,2,2,2,24,1568]{5,4,3,2,1,0:T(8,128)(2,1)S(1)} %copy.44) | copy-start | bytes 3612676
  31.8 32.4 %all-to-all-start = ((bf16[32,40,384]{2,1,0:T(8,128)(2,1)}), bf16[32,40,384]{2,1,0:T(8,128)(2,1)S(1)}, u32[]{:S(2)}, u32[]{:S(2)}) async-start(bf16[32,40,384]{2,1,0:T(8,128)(2,1)} %bitcast.14), calls=%async_computation | async-start | bytes 1966080 | tf_op jit(solution)/shard_map/all_to_all | solution.py:283
  38.1 29.7 %copy-start.22 = (f32[1,1920]{1,0:T(1,128)S(1)}, f32[1,1920]{1,0:T(1,128)}, u32[]{:S(2)}) copy-start(f32[1,1920]{1,0:T(1,128)} %param.37) | copy-start | bytes 23044
  52.7 1.2 copy-start.7
  53.9 0.9 copy-start.9
  64.2 29.5 %all-to-all-start.1 = ((bf16[32,40,384]{2,1,0:T(8,128)(2,1)}), bf16[32,40,384]{2,1,0:T(8,128)(2,1)}, u32[]{:S(2)}, u32[]{:S(2)}) async-start(bf16[32,40,384]{2,1,0:T(8,128)(2,1)} %bitcast.16), calls=%async_computation.1 | async-start | bytes 1966080 | tf_op jit(solution)/shard_map/all_to_all | solution.py:283
  67.8 2.4 %copy-start.15 = (f32[1,1536,384]{2,1,0:T(8,128)S(1)}, f32[1,1536,384]{2,1,0:T(8,128)}, u32[]{:S(2)}) copy-start(f32[1,1536,384]{2,1,0:T(8,128)} %param.34) | copy-start | bytes 7077892
  70.2 1.4 slice-start.1
  109.5 0.9 copy-start.11
  110.4 28.8 %all-to-all-start.2 = ((bf16[32,40,384]{2,1,0:T(8,128)(2,1)}), bf16[32,40,384]{2,1,0:T(8,128)(2,1)S(1)}, u32[]{:S(2)}, u32[]{:S(2)}) async-start(bf16[32,40,384]{2,1,0:T(8,128)(2,1)} %bitcast.20), calls=%async_computation.2 | async-start | bytes 1966080 | tf_op jit(solution)/shard_map/all_to_all | solution.py:283
  113.1 11.4 %copy-start.12 = (bf16[1280,384]{1,0:T(8,128)(2,1)S(1)}, bf16[1280,384]{1,0:T(8,128)(2,1)}, u32[]{:S(2)}) copy-start(bf16[1280,384]{1,0:T(8,128)(2,1)} %copy-done.11) | copy-start | bytes 2949124
  113.1 11.4 %copy-start.16 = (f32[1,1536,384]{2,1,0:T(8,128)S(1)}, f32[1,1536,384]{2,1,0:T(8,128)}, u32[]{:S(2)}) copy-start(f32[1,1536,384]{2,1,0:T(8,128)} %param.34) | copy-start | bytes 7077892
  113.1 11.4 %copy-start.26 = (f32[1,1536,384]{2,1,0:T(8,128)S(1)}, f32[1,1536,384]{2,1,0:T(8,128)}, u32[]{:S(2)}) copy-start(f32[1,1536,384]{2,1,0:T(8,128)} %param.35) | copy-start | bytes 7077892
  113.1 11.3 %copy-start.27 = (f32[1,1536,384]{2,1,0:T(8,128)S(1)}, f32[1,1536,384]{2,1,0:T(8,128)}, u32[]{:S(2)}) copy-start(f32[1,1536,384]{2,1,0:T(8,128)} %param.36) | copy-start | bytes 7077892
  113.1 11.3 %copy-start.28 = (bf16[1280,1536]{1,0:T(8,128)(2,1)S(1)}, bf16[1280,1536]{1,0:T(8,128)(2,1)}, u32[]{:S(2)}) copy-start(bf16[1280,1536]{1,0:T(8,128)(2,1)} %get-tuple-element.94) | copy-start | bytes 11796484
  124.5 17.7 %copy-start.14 = (f32[512,12]{1,0:T(8,128)S(1)}, f32[512,12]{1,0:T(8,128)}, u32[]{:S(2)}) copy-start(f32[512,12]{1,0:T(8,128)} %copy-done.13) | copy-start | bytes 73732
  131.6 10.8 %copy-start.2 = (bf16[1024,384]{1,0:T(8,128)(2,1)S(1)}, bf16[1024,384]{1,0:T(8,128)(2,1)}, u32[]{:S(2)}) copy-start(bf16[1024,384]{1,0:T(8,128)(2,1)} %cot_ref.2) | copy-start | bytes 2359300
  131.6 10.8 %copy-start.6 = (f32[256,2]{1,0:T(8,128)S(1)}, f32[256,2]{1,0:T(8,128)}, u32[]{:S(2)}) copy-start(f32[256,2]{1,0:T(8,128)} %constant.148.clone.coords_ref) | copy-start | bytes 6148
  139.3 37.8 %all-to-all-start.3 = ((bf16[32,40,384]{2,1,0:T(8,128)(2,1)}), bf16[32,40,384]{2,1,0:T(8,128)(2,1)S(1)}, u32[]{:S(2)}, u32[]{:S(2)}) async-start(bf16[32,40,384]{2,1,0:T(8,128)(2,1)} %bitcast.28), calls=%async_computation.3 | async-start | bytes 1966080 | tf_op jit(solution)/shard_map/all_to_all | solution.py:283
  142.4 1.1 copy-start.4
  143.5 1.1 copy-start.10
  167.3 25.8 %copy-start.23 = (f32[1,1920]{1,0:T(1,128)S(1)}, f32[1,1920]{1,0:T(1,128)}, u32[]{:S(2)}) copy-start(f32[1,1920]{1,0:T(1,128)} %param.37) | copy-start | bytes 23044
  167.3 25.8 %copy-start.24 = (f32[1,1920]{1,0:T(1,128)S(1)}, f32[1,1920]{1,0:T(1,128)}, u32[]{:S(2)}) copy-start(f32[1,1920]{1,0:T(1,128)} %param.38) | copy-start | bytes 23044
  167.3 25.8 %copy-start.25 = (f32[1,1920]{1,0:T(1,128)S(1)}, f32[1,1920]{1,0:T(1,128)}, u32[]{:S(2)}) copy-start(f32[1,1920]{1,0:T(1,128)} %param.39) | copy-start | bytes 23044
  167.3 8.8 %collective-permute-start.5 = (bf16[16,24,768]{2,1,0:T(8,128)(2,1)S(1)}, bf16[16,24,768]{2,1,0:T(8,128)(2,1)S(1)}, u32[]{:S(2)}, u32[]{:S(2)}) collective-permute-start(bf16[16,24,768]{2,1,0:T(8,128)(2,1)S(1)} %get-tuple-element.104), channel_id=1, source_target_pairs={{0,8},{8,0},{16,24},{24,16},{1,9},{9,1},{17,25},{25,17},{2,10},{10... | collective-permute-start | bytes 1769480 | tf_op jit(solution)/shard_map/ppermute | solution.py:296
  167.4 31.1 %copy-start.8 = (f32[1024,384]{1,0:T(8,128)S(1)}, f32[1024,384]{1,0:T(8,128)}, u32[]{:S(2)}) copy-start(f32[1024,384]{1,0:T(8,128)} %copy-done.7) | copy-start | bytes 4718596
  167.4 5.4 %collective-permute-start.8 = (f32[64,512]{1,0:T(8,128)S(1)}, f32[64,512]{1,0:T(8,128)S(1)}, u32[]{:S(2)}, u32[]{:S(2)}) collective-permute-start(f32[64,512]{1,0:T(8,128)S(1)} %get-tuple-element.105), channel_id=1, source_target_pairs={{0,24},{8,16},{16,8},{24,0},{1,25},{9,17},{17,9},{25,1},{2,26},{10... | collective-permute-start | bytes 393224 | tf_op jit(solution)/shard_map/ppermute | solution.py:296
  168.9 7.1 %collective-permute-start.7 = (f32[64,512]{1,0:T(8,128)S(1)}, f32[64,512]{1,0:T(8,128)S(1)}, u32[]{:S(2)}, u32[]{:S(2)}) collective-permute-start(f32[64,512]{1,0:T(8,128)S(1)} %get-tuple-element.105), channel_id=1, source_target_pairs={{0,16},{8,24},{16,0},{24,8},{1,17},{9,25},{17,1},{25,9},{2,18},{10... | collective-permute-start | bytes 393224 | tf_op jit(solution)/shard_map/ppermute | solution.py:296
  169.5 6.5 %collective-permute-start.6 = (f32[64,512]{1,0:T(8,128)S(1)}, f32[64,512]{1,0:T(8,128)S(1)}, u32[]{:S(2)}, u32[]{:S(2)}) collective-permute-start(f32[64,512]{1,0:T(8,128)S(1)} %get-tuple-element.105), channel_id=1, source_target_pairs={{0,8},{8,0},{16,24},{24,16},{1,9},{9,1},{17,25},{25,17},{2,10},{10... | collective-permute-start | bytes 393224 | tf_op jit(solution)/shard_map/ppermute | solution.py:296
  177.1 8.3 %collective-permute-start.11 = (f32[64,512]{1,0:T(8,128)S(1)}, f32[64,512]{1,0:T(8,128)S(1)}, u32[]{:S(2)}, u32[]{:S(2)}) collective-permute-start(f32[64,512]{1,0:T(8,128)S(1)} %add_add_fusion.1), channel_id=1, source_target_pairs={{0,6},{1,7},{2,4},{3,5},{4,2},{5,3},{6,0},{7,1},{8,14},{9,15},{10,... | collective-permute-start | bytes 393224 | tf_op jit(solution)/shard_map/ppermute | solution.py:296
  180.6 11.0 %collective-permute-start.10 = (f32[64,512]{1,0:T(8,128)S(1)}, f32[64,512]{1,0:T(8,128)S(1)}, u32[]{:S(2)}, u32[]{:S(2)}) collective-permute-start(f32[64,512]{1,0:T(8,128)S(1)} %add_add_fusion.1), channel_id=1, source_target_pairs={{0,4},{1,5},{2,6},{3,7},{4,0},{5,1},{6,2},{7,3},{8,12},{9,13},{10,... | collective-permute-start | bytes 393224 | tf_op jit(solution)/shard_map/ppermute | solution.py:296
  180.6 11.0 %collective-permute-start.9 = (f32[64,512]{1,0:T(8,128)S(1)}, f32[64,512]{1,0:T(8,128)S(1)}, u32[]{:S(2)}, u32[]{:S(2)}) collective-permute-start(f32[64,512]{1,0:T(8,128)S(1)} %add_add_fusion.1), channel_id=1, source_target_pairs={{0,2},{1,3},{2,0},{3,1},{4,6},{5,7},{6,4},{7,5},{8,10},{9,11},{10,... | collective-permute-start | bytes 393224 | tf_op jit(solution)/shard_map/ppermute | solution.py:296
  191.6 10.2 %collective-permute-start.12 = (f32[64,512]{1,0:T(8,128)S(1)}, f32[64,512]{1,0:T(8,128)}, u32[]{:S(2)}, u32[]{:S(2)}) collective-permute-start(f32[64,512]{1,0:T(8,128)S(1)} %add_add_fusion), channel_id=1, source_target_pairs={{0,1},{1,0},{2,3},{3,2},{4,5},{5,4},{6,7},{7,6},{8,9},{9,8},{10,11... | collective-permute-start | bytes 393224 | tf_op jit(solution)/shard_map/ppermute | solution.py:296
  193.8 19.8 %all-to-all-start.4 = ((bf16[16,24,768]{2,1,0:T(8,128)(2,1)}), bf16[16,24,768]{2,1,0:T(8,128)(2,1)S(1)}, u32[]{:S(2)}, u32[]{:S(2)}) async-start(bf16[16,24,768]{2,1,0:T(8,128)(2,1)} %add_convert_fusion), calls=%async_computation.4 | async-start | bytes 1179648 | tf_op jit(solution)/shard_map/all_to_all | solution.py:375
  198.6 5.0 %copy-start.21 = (f32[10380]{0:T(1024)S(1)}, f32[10380]{0:T(1024)}, u32[]{:S(2)}) copy-start(f32[10380]{0:T(1024)} %param.29) | copy-start | bytes 124564
  198.6 15.1 %copy-start.17 = (f32[12,1568]{1,0:T(8,128)S(1)}, f32[12,1568]{1,0:T(8,128)}, u32[]{:S(2)}) copy-start(f32[12,1568]{1,0:T(8,128)} %param.25) | copy-start | bytes 225796
  201.7 12.0 %copy-start.19 = (f32[12,1568]{1,0:T(8,128)S(1)}, f32[12,1568]{1,0:T(8,128)}, u32[]{:S(2)}) copy-start(f32[12,1568]{1,0:T(8,128)} %param.26) | copy-start | bytes 225796
  201.7 12.0 %copy-start.20 = (f32[12,1568]{1,0:T(8,128)S(1)}, f32[12,1568]{1,0:T(8,128)}, u32[]{:S(2)}) copy-start(f32[12,1568]{1,0:T(8,128)} %param.27) | copy-start | bytes 225796

commit v2 on v1

--- a/solution.py
+++ b/solution.py
@@ -21,6 +21,8 @@
 GROUP = 4
 GROUP_LANES = 128
 VMEM_BYTES = 48 * 2**20
+VMEM_MOST = 62 * 2**20
+EXPERT_PARTS = 2
 TABLE = 256
 TABLE_MID = 119
 STRIDE = 16
@@ -29,7 +31,7 @@
 SHIFT_ROW = 20
 FIRST_ROWS = 21
 SCALE_ROWS = 24
-ROUTE_ROWS = 32
+SUM_ROWS = 32
 
 
 highest = lax.Precision.HIGHEST
@@ -356,11 +358,30 @@
     return jnp.where(upper(step), both([other, held]), both([held, other]))
 
 
-def sum_quads(small, steps):
+def join_quad(held, steps):
     axis, low = steps[0]
     high = steps[1][1]
-    near = small + swap(small, (axis, low))
-    return near + (swap(small, (axis, high)) + swap(small, (axis, high + low)))
+    near, far, last = (swap(held, (axis, offset)) for offset in (low, high, low + high))
+    ahead = upper(steps[1])
+    blocks = [
+        jnp.where(ahead, second, first)
+        for first, second in ((held, far), (near, last), (far, held), (last, near))
+    ]
+    return jnp.where(
+        upper(steps[0]),
+        jnp.stack([blocks[1], blocks[0], blocks[3], blocks[2]]),
+        jnp.stack(blocks),
+    )
+
+
+def swap_flat(value, offset):
+    axes = ("wide", "narrow")
+    return lax.ppermute(value, axes, [(i, i ^ offset) for i in range(lax.axis_size(axes))])
+
+
+def sum_quads(small, low, high):
+    near = small + swap_flat(small, low)
+    return near + (swap_flat(small, high) + swap_flat(small, low + high))
 
 
 def sum_chip(send, keep):
@@ -532,20 +553,30 @@
         keys * lax.rsqrt(head_sums(keys * keys) + 1e-06)
     ).astype(jnp.bfloat16)
     heads_ref[:, 2 * width :] = values.astype(jnp.bfloat16)
-    for window in range(block // WIN):
-        at = pl.ds(window * WIN, WIN)
-        for group in range(width // GROUP_LANES):
-            start = group * GROUP_LANES
-            query = heads_ref[at, start : start + GROUP_LANES]
-            key = heads_ref[at, width + start : width + start + GROUP_LANES]
-            value = heads_ref[at, 2 * width + start : 2 * width + start + GROUP_LANES]
-            cosine = dot_cols(key, stack_heads(query, masks_low))
-            scores = cosine * scale_ref[group] + bias_ref[group]
-            powers = jnp.exp(scores - jnp.max(scores, axis=0, keepdims=True))
-            probs = powers * (1.0 / jnp.sum(powers, axis=0, keepdims=True))
-            probs_ref[window, group] = probs
-            mixed = pick_heads(dot_rows(probs.astype(jnp.bfloat16), value), masks)
-            mixed_ref[at, start : start + GROUP_LANES] = mixed.astype(jnp.bfloat16)
+    units = [
+        (window, group)
+        for window in range(block // WIN)
+        for group in range(width // GROUP_LANES)
+    ]
+
+    def part(window, group, side):
+        start = side * width + group * GROUP_LANES
+        return heads_ref[window * WIN : window * WIN + WIN, start : start + GROUP_LANES]
+
+    cosines = [dot_cols(part(w, g, 1), stack_heads(part(w, g, 0), masks_low)) for w, g in units]
+    all_probs = []
+    for (window, group), cosine in zip(units, cosines):
+        scores = cosine * scale_ref[group] + bias_ref[group]
+        powers = jnp.exp(scores - jnp.max(scores, axis=0, keepdims=True))
+        probs = powers * (1.0 / jnp.sum(powers, axis=0, keepdims=True))
+        probs_ref[window, group] = probs
+        all_probs.append(probs.astype(jnp.bfloat16))
+    mixes = [pick_heads(dot_rows(p, part(w, g, 2)), masks) for (w, g), p in zip(units, all_probs)]
+    for (window, group), mixed in zip(units, mixes):
+        mixed_ref[
+            window * WIN : window * WIN + WIN,
+            group * GROUP_LANES : group * GROUP_LANES + GROUP_LANES,
+        ] = mixed.astype(jnp.bfloat16)
     attended = dot(mixed_ref[...], weight_ref[:, 3 * width : 4 * width]) + rows_ref[6:7, :]
     attended_ref[...] = attended
     section = tokens.astype(jnp.float32) + norm_rows(attended, rows_ref[0:1, :], rows_ref[1:2, :])
@@ -614,18 +645,14 @@
 
 
 def back_kernel(
-    narrow,
     count_ref,
-    place_ref,
     dest_ref,
     arrived_ref,
     cot_ref,
-    tokens_ref,
     weight_ref,
     rows_ref,
     scale_ref,
     attended_ref,
-    mixed_ref,
     raw_ref,
     heads_ref,
     probs_ref,
@@ -633,21 +660,18 @@
     table_ref,
     coords_ref,
     net_ref,
-    inputs_ref,
-    send_ref,
-    keep_ref,
+    total_ref,
+    low_attended,
+    low_projected,
     sums_ref,
     grad_bias_ref,
     grad_scale_ref,
     grad_heads,
-    low_attended,
-    low_projected,
 ):
     step = pl.program_id(0)
     block = cot_ref.shape[0]
     width = MODEL_WIDTH
     start_row = pl.multiple_of(step * block, block)
-    here = pl.ds(start_row, block)
     masks_low = lane_masks(jnp.bfloat16)
     masks = lane_masks(jnp.float32)
 
@@ -672,75 +696,65 @@
         - unit * jnp.mean(grad_unit * unit, axis=-1, keepdims=True)
     )
     grad_low = grad_attended.astype(jnp.bfloat16)
-    low_attended[here, :] = grad_low
+    total_ref[...] = total
+    low_attended[...] = grad_low
     sums_ref[0:1, :width] += jnp.sum(total * unit, axis=0, keepdims=True)
     sums_ref[1:2, :width] += jnp.sum(total, axis=0, keepdims=True)
     sums_ref[6:7, :width] += jnp.sum(grad_low.astype(jnp.float32), axis=0, keepdims=True)
     grad_mixed = dot_cols(grad_low, weight_ref[:, 3 * width : 4 * width]).astype(jnp.bfloat16)
-    for window in range(block // WIN):
-        at = pl.ds(window * WIN, WIN)
-        for group in range(width // GROUP_LANES):
-            start = group * GROUP_LANES
-            cut_q = slice(start, start + GROUP_LANES)
-            cut_k = slice(width + start, width + start + GROUP_LANES)
-            cut_v = slice(2 * width + start, 2 * width + start + GROUP_LANES)
-            query = stack_heads(heads_ref[at, cut_q], masks_low)
-            key = heads_ref[at, cut_k]
-            value = heads_ref[at, cut_v]
-            grad_out = stack_heads(grad_mixed[window * WIN : window * WIN + WIN, cut_q], masks_low)
-            grad_probs = dot_cols(value, grad_out)
-            cosine = dot_cols(key, query)
-            probs = probs_ref[window, group]
-            grad_heads[at, cut_v] = dot(probs.astype(jnp.bfloat16), grad_out)
-            weighed = probs * grad_probs
-            grad_scores = weighed - probs * jnp.sum(weighed, axis=0, keepdims=True)
-            grad_bias_ref[group] += grad_scores
-            grad_scale_ref[group] += jnp.sum(grad_scores * cosine, axis=0, keepdims=True)
-            grad_cosine = (grad_scores * scale_ref[group]).astype(jnp.bfloat16)
-            grad_heads[at, cut_k] = dot(grad_cosine, query)
-            grad_heads[at, cut_q] = pick_heads(dot_rows(grad_cosine, key), masks)
+    units = [
+        (window, group)
+        for window in range(block // WIN)
+        for group in range(width // GROUP_LANES)
+    ]
+
+    def cut(window, group, side):
+        start = side * width + group * GROUP_LANES
+        return slice(window * WIN, window * WIN + WIN), slice(start, start + GROUP_LANES)
+
+    queries = [stack_heads(heads_ref[cut(w, g, 0)], masks_low) for w, g in units]
+    grad_outs = [stack_heads(grad_mixed[cut(w, g, 0)], masks_low) for w, g in units]
+    all_grad_probs = [
+        dot_cols(heads_ref[cut(w, g, 2)], grad_out) for (w, g), grad_out in zip(units, grad_outs)
+    ]
+    cosines = [dot_cols(heads_ref[cut(w, g, 1)], query) for (w, g), query in zip(units, queries)]
+    all_probs, grad_cosines = [], []
+    for (window, group), grad_probs, cosine in zip(units, all_grad_probs, cosines):
+        probs = probs_ref[window, group]
+        all_probs.append(probs.astype(jnp.bfloat16))
+        weighed = probs * grad_probs
+        grad_scores = weighed - probs * jnp.sum(weighed, axis=0, keepdims=True)
+        grad_bias_ref[group] += grad_scores
+        grad_scale_ref[group] += jnp.sum(grad_scores * cosine, axis=0, keepdims=True)
+        grad_cosines.append((grad_scores * scale_ref[group]).astype(jnp.bfloat16))
+    for (w, g), probs, grad_out in zip(units, all_probs, grad_outs):
+        grad_heads[cut(w, g, 2)] = dot(probs, grad_out)
+    for (w, g), grad_cosine, query in zip(units, grad_cosines, queries):
+        grad_heads[cut(w, g, 1)] = dot(grad_cosine, query)
+    for (w, g), grad_cosine in zip(units, grad_cosines):
+        grad_heads[cut(w, g, 0)] = pick_heads(
+            dot_rows(grad_cosine, heads_ref[cut(w, g, 1)]), masks
+        )
     for side in range(2):
         cut = slice(side * width, side * width + width)
         raw = raw_ref[:, cut]
         inverse = lax.rsqrt(head_sums(raw * raw) + 1e-06)
         unit = raw * inverse
         grad = grad_heads[:, cut]
-        low_projected[here, cut] = (inverse * (grad - unit * head_sums(grad * unit))).astype(
+        low_projected[:, cut] = (inverse * (grad - unit * head_sums(grad * unit))).astype(
             jnp.bfloat16
         )
-    low_projected[here, 2 * width :] = grad_heads[:, 2 * width :].astype(jnp.bfloat16)
-    grad_projected = low_projected[here, :]
+    low_projected[:, 2 * width :] = grad_heads[:, 2 * width :].astype(jnp.bfloat16)
+    grad_projected = low_projected[...]
     sums_ref[4:5, :width] += jnp.sum(
         grad_projected[:, :width].astype(jnp.float32), axis=0, keepdims=True
     )
     sums_ref[5:6, :width] += jnp.sum(
         grad_projected[:, 2 * width :].astype(jnp.float32), axis=0, keepdims=True
     )
-    inputs_ref[...] = (total + dot_cols(grad_projected, weight_ref[:, : 3 * width])).astype(
-        jnp.bfloat16
-    )
-
     @pl.when(step == pl.num_programs(0) - 1)
     def _():
-        grad_qkv = dot_rows(tokens_ref[...], low_projected[...])
-        grad_out = dot_rows(mixed_ref[...], low_attended[...])
-        grad_dense = jnp.concatenate([grad_qkv, grad_out], axis=1)
-        chips = keep_ref.shape[0]
-        on_first = place_ref[0] == 0
-        share = width // (2 * chips)
-        for chip in range(chips):
-            cuts = []
-            for core in range(2):
-                row = (chip // narrow * 2 * narrow + core * narrow + chip % narrow) * share
-                rows = grad_dense[row : row + share]
-                cuts.append(
-                    jnp.concatenate([rows[:, : 2 * width], rows[:, 2 * width :]], axis=0)
-                )
-            keep_ref[chip] = jnp.where(on_first, cuts[0], cuts[1])
-            send_ref[chip] = jnp.where(on_first, cuts[1], cuts[0]).astype(jnp.bfloat16)
         sums_ref[2:4, :width] = expert_ref[1:3, :]
-        row = lax.broadcasted_iota(jnp.int32, (EXPERTS, width), 0)
-        sums_ref[ROUTE_ROWS:, :width] = jnp.where(row == place_ref[1], expert_ref[3:4, :], 0.0)
         for group in range(grad_scale_ref.shape[0]):
             at = SCALE_ROWS + group
             sums_ref[at : at + 1, : GROUP * WIN] = grad_scale_ref[group]
@@ -797,37 +811,31 @@
 
 
 def call_back(
-    images, dest, arrived, cotangent, tokens, gathered, rows, scale, attended, mixed, raw, heads, probs, sums_expert, table, net
+    images, dest, arrived, cotangent, gathered, rows, scale, attended, raw, heads, probs,
+    sums_expert, table, net,
 ):
-    count, width = tokens.shape
-    narrow = lax.axis_size("narrow")
-    chips = narrow * lax.axis_size("wide") // 2
-    share = width // (2 * chips)
-    coords = jnp.asarray(offset_coords())
-    place = jnp.stack([lax.axis_index("wide") % 2, lax.axis_index(("wide", "narrow"))])
+    count, width = cotangent.shape
     block = token_block(count)
     groups = width // GROUP_LANES
+    coords = jnp.asarray(offset_coords())
     return pl.pallas_call(
-        functools.partial(back_kernel, narrow),
+        back_kernel,
         grid=(count // block,),
         out_shape=(
+            jax.ShapeDtypeStruct((count, width), jnp.float32),
             jax.ShapeDtypeStruct((count, width), jnp.bfloat16),
-            jax.ShapeDtypeStruct((chips, 2 * share, 2 * width), jnp.bfloat16),
-            jax.ShapeDtypeStruct((chips, 2 * share, 2 * width), jnp.float32),
-            jax.ShapeDtypeStruct((ROUTE_ROWS + EXPERTS, SUM_LANES), jnp.float32),
+            jax.ShapeDtypeStruct((count, 3 * width), jnp.bfloat16),
+            jax.ShapeDtypeStruct((SUM_ROWS, SUM_LANES), jnp.float32),
         ),
         in_specs=[
-            pl.BlockSpec(memory_space=pltpu.SMEM),
             pl.BlockSpec(memory_space=pltpu.SMEM),
             pl.BlockSpec((1, block), lambda i: (0, i)),
             whole(arrived.shape),
             by_rows(block, width),
-            whole(tokens.shape),
             whole(gathered.shape),
             whole(rows.shape),
             whole(scale.shape),
             by_rows(block, width),
-            whole(mixed.shape),
             by_rows(block, 2 * width),
             by_rows(block, 3 * width),
             pl.BlockSpec((block // WIN,) + probs.shape[1:], lambda i: (i, 0, 0, 0)),
@@ -838,42 +846,111 @@
         ],
         out_specs=(
             by_rows(block, width),
-            whole((chips, 2 * share, 2 * width)),
-            whole((chips, 2 * share, 2 * width)),
-            whole((ROUTE_ROWS + EXPERTS, SUM_LANES)),
+            by_rows(block, width),
+            by_rows(block, 3 * width),
+            whole((SUM_ROWS, SUM_LANES)),
         ),
         scratch_shapes=[
             pltpu.VMEM((groups, WIN, GROUP * WIN), jnp.float32),
             pltpu.VMEM((groups, 1, GROUP * WIN), jnp.float32),
             pltpu.VMEM((block, 3 * width), jnp.float32),
-            pltpu.VMEM((count, width), jnp.bfloat16),
-            pltpu.VMEM((count, 3 * width), jnp.bfloat16),
         ],
         cost_estimate=pl.CostEstimate(
-            flops=2 * count * width * width * 16, bytes_accessed=20 * 10**6, transcendentals=0
-        ),
-        compiler_params=pltpu.CompilerParams(vmem_limit_bytes=VMEM_BYTES),
+            flops=2 * count * width * width * 10, bytes_accessed=20 * 10**6, transcendentals=0
+        ),
+        compiler_params=pltpu.CompilerParams(vmem_limit_bytes=VMEM_MOST),
         name="back",
     )(
-        images,
-        place.astype(jnp.int32),
-        dest,
-        arrived,
-        cotangent,
-        tokens,
-        gathered,
-        rows,
-        scale,
-        attended,
-        mixed,
-        raw,
-        heads,
-        probs,
-        sums_expert,
-        table,
-        coords,
-        net,
-    )
+        images, dest, arrived, cotangent, gathered, rows, scale, attended, raw, heads, probs,
+        sums_expert, table, coords, net,
+    )
+
+
+def dense_kernel(
+    narrow,
+    place_ref,
+    tokens_ref,
+    mixed_ref,
+    attended_ref,
+    projected_ref,
+    expert_ref,
+    send_ref,
+    keep_ref,
+):
+    width = tokens_ref.shape[1]
+    grad_dense = jnp.concatenate(
+        [
+            dot_rows(tokens_ref[...], projected_ref[...]),
+            dot_rows(mixed_ref[...], attended_ref[...]),
+        ],
+        axis=1,
+    )
+    chips = keep_ref.shape[0]
+    on_first = place_ref[0] == 0
+    row = lax.broadcasted_iota(jnp.int32, (GROUP_LANES, width), 0)
+    grad_route = jnp.where(row == place_ref[1], expert_ref[3:4, :], 0.0).T
+    share = width // (2 * chips)
+    for chip in range(chips):
+        cuts = []
+        for core in range(2):
+            row = (chip // narrow * 2 * narrow + core * narrow + chip % narrow) * share
+            rows, route = grad_dense[row : row + share], grad_route[row : row + share]
+            halves = jnp.concatenate([rows[:, : 2 * width], rows[:, 2 * width :]], axis=0)
+            route = jnp.concatenate([route, jnp.zeros_like(route)], axis=0)
+            cuts.append(jnp.concatenate([halves, route], axis=1))
+        keep_ref[chip] = jnp.where(on_first, cuts[0], cuts[1])
+        send_ref[chip] = jnp.where(on_first, cuts[1], cuts[0]).astype(jnp.bfloat16)
+
+
+def call_dense(tokens, mixed, attended, projected, sums_expert):
+    count, width = tokens.shape
+    narrow = lax.axis_size("narrow")
+    chips = narrow * lax.axis_size("wide") // 2
+    shape = (chips, width // chips, 2 * width + GROUP_LANES)
+    place = jnp.stack([lax.axis_index("wide") % 2, lax.axis_index(("wide", "narrow"))])
+    return pl.pallas_call(
+        functools.partial(dense_kernel, narrow),
+        out_shape=(
+            jax.ShapeDtypeStruct(shape, jnp.bfloat16),
+            jax.ShapeDtypeStruct(shape, jnp.float32),
+        ),
+        in_specs=[pl.BlockSpec(memory_space=pltpu.SMEM)]
+        + [pl.BlockSpec(memory_space=pltpu.VMEM)] * 5,
+        out_specs=(pl.BlockSpec(memory_space=pltpu.VMEM),) * 2,
+        cost_estimate=pl.CostEstimate(
+            flops=8 * count * width * width, bytes_accessed=7 * 10**6, transcendentals=0
+        ),
+        compiler_params=pltpu.CompilerParams(vmem_limit_bytes=VMEM_BYTES),
+        name="dense",
+    )(place.astype(jnp.int32), tokens, mixed, attended, projected, sums_expert)
+
+
+def inputs_kernel(total_ref, projected_ref, weight_ref, out_ref):
+    wide = projected_ref.shape[1]
+    out_ref[...] = (
+        total_ref[...] + dot_cols(projected_ref[...], weight_ref[:, :wide])
+    ).astype(jnp.bfloat16)
+
+
+def call_inputs(total, projected, gathered):
+    count, width = total.shape
+    block = token_block(count)
+    return pl.pallas_call(
+        inputs_kernel,
+        grid=(count // block,),
+        out_shape=jax.ShapeDtypeStruct((count, width), jnp.bfloat16),
+        in_specs=[
+            by_rows(block, width),
+            by_rows(block, 3 * width),
+            whole(gathered.shape),
+        ],
+        out_specs=by_rows(block, width),
+        cost_estimate=pl.CostEstimate(
+            flops=0, bytes_accessed=0, transcendentals=0
+        ),
+        compiler_params=pltpu.CompilerParams(vmem_limit_bytes=VMEM_BYTES),
+        name="inputs",
+    )(total, projected, gathered)
 
 
 def layer_kernel(count_ref, dest_ref, branch_ref, section_ref, out_ref):
@@ -899,7 +976,7 @@
         ],
         out_specs=by_rows(block, width),
         cost_estimate=pl.CostEstimate(
-            flops=2 * count * width * branch.shape[0], bytes_accessed=4 * 10**6, transcendentals=0
+            flops=0, bytes_accessed=0, transcendentals=0
         ),
         compiler_params=pltpu.CompilerParams(vmem_limit_bytes=VMEM_BYTES),
         name="layer",
@@ -926,49 +1003,62 @@
         sums_ref[...] = jnp.zeros_like(sums_ref)
         sum_pre_ref[...] = jnp.zeros_like(sum_pre_ref)
 
-    low = rows_ref[...]
-    rows = low.astype(jnp.float32)
     bias_two, gain, shift, route = (vecs_ref[i : i + 1, :] for i in range(4))
-    hidden, slope = gelu_pair(dot(low, first_ref[...]) + bias_one_ref[...])
-    hidden = hidden.astype(jnp.bfloat16)
-    hidden_ref[...] = hidden
-    result = (dot(hidden, second_ref[...]) + bias_two).astype(jnp.bfloat16).astype(jnp.float32)
-    gating = jax.nn.sigmoid(jnp.sum(rows * route, axis=-1, keepdims=True))
-    centred = result - jnp.mean(result, axis=-1, keepdims=True)
-    spread = lax.rsqrt(jnp.mean(centred * centred, axis=-1, keepdims=True) + 1e-05)
-    unit = centred * spread
-    normed = unit * gain + shift
-    branch_ref[...] = (normed * gating).astype(jnp.bfloat16)
-    cot = cot_ref[...].astype(jnp.float32)
-    grad_gate = jnp.sum(cot * normed, axis=-1, keepdims=True)
-    gated = cot * gating
-    grad_unit = gated * gain
-    grad_result = (
-        spread
-        * (
-            grad_unit
-            - jnp.mean(grad_unit, axis=-1, keepdims=True)
-            - unit * jnp.mean(grad_unit * unit, axis=-1, keepdims=True)
+    count = rows_ref.shape[0]
+    size = count // EXPERT_PARTS
+    cuts = [slice(start, start + size) for start in range(0, count, size)]
+    pres = [dot(rows_ref[cut, :], first_ref[...]) + bias_one_ref[...] for cut in cuts]
+    pairs = [gelu_pair(pre) for pre in pres]
+    hiddens = [hidden.astype(jnp.bfloat16) for hidden, _ in pairs]
+    raws = [dot(hidden, second_ref[...]) + bias_two for hidden in hiddens]
+    grads = []
+    for cut, hidden, raw in zip(cuts, hiddens, raws):
+        hidden_ref[cut, :] = hidden
+        rows = rows_ref[cut, :].astype(jnp.float32)
+        result = raw.astype(jnp.bfloat16).astype(jnp.float32)
+        gating = jax.nn.sigmoid(jnp.sum(rows * route, axis=-1, keepdims=True))
+        centred = result - jnp.mean(result, axis=-1, keepdims=True)
+        spread = lax.rsqrt(jnp.mean(centred * centred, axis=-1, keepdims=True) + 1e-05)
+        unit = centred * spread
+        normed = unit * gain + shift
+        branch_ref[cut, :] = (normed * gating).astype(jnp.bfloat16)
+        cot = cot_ref[cut, :].astype(jnp.float32)
+        grad_gate = jnp.sum(cot * normed, axis=-1, keepdims=True)
+        gated = cot * gating
+        grad_unit = gated * gain
+        grad_result = (
+            spread
+            * (
+                grad_unit
+                - jnp.mean(grad_unit, axis=-1, keepdims=True)
+                - unit * jnp.mean(grad_unit * unit, axis=-1, keepdims=True)
+            )
+        ).astype(jnp.bfloat16)
+        grad_result_ref[cut, :] = grad_result
+        grad_logit = (
+            (grad_gate * gating * (1.0 - gating)).astype(jnp.bfloat16).astype(jnp.float32)
         )
-    ).astype(jnp.bfloat16)
-    grad_result_ref[...] = grad_result
-    grad_logit = (
-        (grad_gate * gating * (1.0 - gating)).astype(jnp.bfloat16).astype(jnp.float32)
-    )
-    sums_ref[0:1, :] += jnp.sum(grad_result.astype(jnp.float32), axis=0, keepdims=True)
-    sums_ref[1:2, :] += jnp.sum(gated * unit, axis=0, keepdims=True)
-    sums_ref[2:3, :] += jnp.sum(gated, axis=0, keepdims=True)
-    sums_ref[3:4, :] += jnp.sum(rows * grad_logit, axis=0, keepdims=True)
-    grad_pre = (dot_cols(grad_result, second_ref[...]) * slope).astype(jnp.bfloat16)
-    grad_pre_ref[...] = grad_pre
-    sum_pre_ref[...] += jnp.sum(grad_pre.astype(jnp.float32), axis=0, keepdims=True)
-    back_ref[...] = (dot_cols(grad_pre, first_ref[...]) + grad_logit * route).astype(jnp.bfloat16)
+        sums_ref[0:1, :] += jnp.sum(grad_result.astype(jnp.float32), axis=0, keepdims=True)
+        sums_ref[1:2, :] += jnp.sum(gated * unit, axis=0, keepdims=True)
+        sums_ref[2:3, :] += jnp.sum(gated, axis=0, keepdims=True)
+        sums_ref[3:4, :] += jnp.sum(rows * grad_logit, axis=0, keepdims=True)
+        grads.append((grad_result, grad_logit))
+    grad_hiddens = [dot_cols(grad, second_ref[...]) for grad, _ in grads]
+    grad_pres = [
+        (grad * slope).astype(jnp.bfloat16) for grad, (_, slope) in zip(grad_hiddens, pairs)
+    ]
+    for cut, grad_pre, (_, grad_logit) in zip(cuts, grad_pres, grads):
+        grad_pre_ref[cut, :] = grad_pre
+        sum_pre_ref[...] += jnp.sum(grad_pre.astype(jnp.float32), axis=0, keepdims=True)
+        back_ref[cut, :] = (dot_cols(grad_pre, first_ref[...]) + grad_logit * route).astype(
+            jnp.bfloat16
+        )
 
 
 def call_expert(rows, cot, first, second, bias_one, vecs):
     count, width = rows.shape
     ff = first.shape[1]
-    block = math.gcd(count, 256)
+    block = math.gcd(count, 640)
     return pl.pallas_call(
         expert_kernel,
         grid=(count // block,),
@@ -1001,7 +1091,7 @@
         cost_estimate=pl.CostEstimate(
             flops=8 * count * width * ff, bytes_accessed=16 * 10**6, transcendentals=count * ff
         ),
-        compiler_params=pltpu.CompilerParams(vmem_limit_bytes=VMEM_BYTES),
+        compiler_params=pltpu.CompilerParams(vmem_limit_bytes=VMEM_MOST),
         name="expert",
     )(rows, cot, first, second, bias_one, vecs)
 
@@ -1233,30 +1323,25 @@
 
     scale_at = 7 * MODEL_WIDTH
     share = dense_weight.astype(jnp.bfloat16)
-    (pair, depth), across = axis_bits("narrow")[1:], axis_bits("narrow")[0]
-    held = join(share, pair)
-    held, params = lax.optimization_barrier((held, small_params))
+    across, *deep = axis_bits("narrow")
+    held = join_quad(share, deep)
+    held, route_ids, cot = lax.optimization_barrier((held, routes, cotangent))
+    dest, placed_cot = call_assign(images, route_ids, cot, capacity)
+    held = join(held, across, -2)
+    held, placed_cot, dest = lax.optimization_barrier((held, placed_cot, dest))
+    core, *rest = axis_bits("wide")
+    for step in rest:
+        held = join(held, step)
+    gathered = join(held, core, len(rest)).reshape(-1, share.shape[-1])
+    gathered, placed_cot, params = lax.optimization_barrier((gathered, placed_cot, small_params))
+    cot_rows = trade(placed_cot)
     table = bias_table(params)
     net_pieces = pieces(params)
     net = jnp.concatenate([net_pieces[10].T, net_pieces[8][None, :], net_pieces[9]])
     vectors = params[:scale_at].reshape(7, MODEL_WIDTH)
     scale_heads = jnp.exp(params[scale_at : scale_at + ATTENTION_HEADS])
     scale = jnp.repeat(scale_heads, WIN).reshape(-1, 1, GROUP * WIN)
-    held = join(held, depth)
-    held, table, vectors, scale, route_ids, cot = lax.optimization_barrier(
-        (held, table, vectors, scale, routes, cotangent)
-    )
-    dest, placed_cot = call_assign(images, route_ids, cot, capacity)
-    held = join(held, across, -2)
-    held, table, placed_cot, dest = lax.optimization_barrier((held, table, placed_cot, dest))
     bias = spread_bias(table)
-    core, *rest = axis_bits("wide")
-    for step in rest:
-        held = join(held, step)
-    held, bias = lax.optimization_barrier((held, bias))
-    gathered = join(held, core, len(rest)).reshape(-1, held.shape[-1])
-    gathered, placed_cot = lax.optimization_barrier((gathered, placed_cot))
-    cot_rows = trade(placed_cot)
     placed, section, attended, mixed, raw, heads, probs = call_front(
         dest, tokens, gathered, vectors, scale, bias, capacity
     )
@@ -1287,17 +1372,15 @@
         (branch, arrived, inner_out, outer_out)
     )
     branch_rows = trade(branch)
-    grad_inputs, send, keep, sums = call_back(
+    total, low_attended, low_projected, sums = call_back(
         images,
         dest,
         arrived,
         cotangent,
-        tokens,
         gathered,
         vectors,
         scale,
         attended,
-        mixed,
         raw,
         heads,
         probs,
@@ -1305,15 +1388,27 @@
         table,
         net,
     )
+    send, keep = call_dense(tokens, mixed, low_attended, low_projected, sums_expert)
+    grad_inputs = call_inputs(total, low_projected, gathered)
     held = sum_chip(send, keep)
-    sums = sum_quads(sums, axis_bits("wide"))
-    held, sums, branch_rows = lax.optimization_barrier((held, sums, branch_rows))
+    narrow = lax.axis_size("narrow")
+    sums = sums + swap_flat(sums, narrow)
+    held, sums, branch_rows, grad_inputs = lax.optimization_barrier(
+        (held, sums, branch_rows, grad_inputs)
+    )
     grad_dense = sum_shares(held)
+    sums = sum_quads(sum_quads(sums, 2, 4), 1, 2 * narrow)
     layer_out = call_layer(images, dest, branch_rows, section)
     share_rows = dense_weight.shape[0]
-    grad_dense = jnp.concatenate([grad_dense[:share_rows], grad_dense[share_rows:]], axis=1)
-    sums = sum_quads(sums, axis_bits("narrow")[1:])
-    sums = sums + swap(sums, across)
+    half = 2 * MODEL_WIDTH
+    grad_dense = jnp.concatenate(
+        [
+            grad_dense[:share_rows, :half],
+            grad_dense[share_rows:, :half],
+            grad_dense[:share_rows, half : half + EXPERTS],
+        ],
+        axis=1,
+    )
     grad_scale = sums[SCALE_ROWS : SCALE_ROWS + ATTENTION_HEADS // GROUP, : GROUP * WIN]
     grad_small = jnp.concatenate(
         [
@@ -1323,10 +1418,6 @@
             sums[SECOND_ROWS : SECOND_ROWS + ATTENTION_HEADS].T.reshape(-1),
         ]
     )
-    grad_route = lax.dynamic_slice_in_dim(
-        sums[ROUTE_ROWS:, :MODEL_WIDTH], expert * share_rows, share_rows, 1
-    ).T
-    grad_dense = jnp.concatenate([grad_dense, grad_route], axis=1)
     dense_out = adamw_step(
         dense_weight, grad_dense, dense_moment, dense_square, dense_rate, weight_decay
     )

time: 215 us -> 198 us (0.921)
  waiting for transfers between devices: 71 us -> 55.7 us
  Pallas kernels: 58.9 us -> 53.8 us
  local copies, waits for them, and re-layouts: 10.4 us -> 14.4 us
  starting transfers between devices: 39.2 us -> 36.6 us
    ppermute x13 -> x7, starting transfers between devices: 19.2 us -> 8.9 us  [swap(): lax.ppermute(value, axis, [(i, i ^ offset) for i in range(lax.axis_size(a...]
    ppermute x13 -> x7, waiting for transfers between devices: 23.1 us -> 12.8 us  [swap(): lax.ppermute(value, axis, [(i, i ^ offset) for i in range(lax.axis_size(a...]
    ppermute x0 -> x7, starting transfers between devices: none -> 8.43 us  [swap_flat(): lax.ppermute(value, axes, [(i, i ^ offset) for i in range(lax.axis_size(a...]
    pallas_call x1, Pallas kernels: 14.6 us -> 10.5 us  [call_front(): pl.pallas_call(front_kernel, grid=(count // block,), out_shape=(jax.Shape...]
    unnamed x58 -> x78, local copies, waits for them, and re-layouts: 5.8 us -> 9.92 us
    all_to_all x4, waiting for transfers between devices: 39.4 us -> 35.3 us  [trade_rows(): lax.all_to_all(payload, ('wide', 'narrow'), split_axis=0, concat_axis=0,...]
    all_to_all x4, starting transfers between devices: 15.3 us -> 12.7 us  [trade_rows(): lax.all_to_all(payload, ('wide', 'narrow'), split_axis=0, concat_axis=0,...]
    all_to_all x1, waiting for transfers between devices: 8.55 us -> 6.26 us  [sum_shares(): lax.all_to_all(held, ('wide', 'narrow'), 0, 0, axis_index_groups=groups,...]
  transfers between devices with their start and end apart: 18 -> 19, of which waited for: 13 -> 10; matrix products, arithmetic and copies ran while one was open for 15% -> 18% of each run, Pallas kernels for 20% -> 20%
where the time goes in v2:
time: 198 us; the launch traced here: 197 us
  waiting for transfers between devices  55.7 us (28%)
  Pallas kernels  53.8 us (27%)
  starting transfers between devices  36.6 us (18%)
  matrix products  21.1 us (11%)
  local copies, waits for them, and re-layouts  14.4 us (7%)
  other arithmetic  13.2 us (7%)
    all_to_all x4, waiting for transfers between devices, trade_rows(): lax.all_to_all(payload, ('wide', 'narrow'), split_axis=0, concat_axis=0,...  35.3 us
    dot_general x2, matrix products, dot_rows(): lax.dot_general(left, right, contract_rows, preferred_element_type=jnp.fl...  18.4 us
    pallas_call x1, Pallas kernels, call_back(): pl.pallas_call(back_kernel, grid=(count // block,), out_shape=(jax.ShapeD...  15.9 us
    pallas_call x1, Pallas kernels, call_expert(): pl.pallas_call(expert_kernel, grid=(count // block,), out_shape=(jax.Shap...  15.3 us
    ppermute x7, waiting for transfers between devices, swap(): lax.ppermute(value, axis, [(i, i ^ offset) for i in range(lax.axis_size(a...  12.8 us
    all_to_all x4, starting transfers between devices, trade_rows(): lax.all_to_all(payload, ('wide', 'narrow'), split_axis=0, concat_axis=0,...  12.7 us
    pallas_call x1, Pallas kernels, call_front(): pl.pallas_call(front_kernel, grid=(count // block,), out_shape=(jax.Shape...  10.5 us
    unnamed x78, local copies, waits for them, and re-layouts  9.92 us
  transfers between devices with their start and end apart: 19, of which 10 were waited for; matrix products, arithmetic and copies ran while one was open for 18% of the time, Pallas kernels for 20%

profile of v2, /device:TPU:0, one launch (start us, length us, event | category | flops | bytes accessed | tf_op | source)
XLA Modules:
  0.0 196.9 jit_solution(18039357799345126009)
XLA Ops:
  0.7 0.9 convert_element_type.30
  1.6 4.0 %collective-permute-start.2 = (bf16[12,1568]{1,0:T(8,128)(2,1)S(1)}, bf16[12,1568]{1,0:T(8,128)(2,1)S(1)}, u32[]{:S(2)}, u32[]{:S(2)}) collective-permute-start(bf16[12,1568]{1,0:T(8,128)(2,1)S(1)} %convert_element_type.30), channel_id=1, source_target_pairs={{0,4},{1,5},{2,6},{3,7},{4,0},{5,1},{6,2},{7,3},{8,12},{9,13},{10,... | collective-permute-start | bytes 112904 | tf_op jit(solution)/shard_map/ppermute | solution.py:298
  5.6 1.6 collective-permute-start.1
  7.2 1.2 collective-permute-done.2
  8.4 0.9 select_bitcast_fusion.2
  9.3 0.4 collective-permute-done.1
  9.7 3.4 %collective-permute-done = bf16[12,1568]{1,0:T(8,128)(2,1)S(1)} collective-permute-done((bf16[12,1568]{1,0:T(8,128)(2,1)S(1)}, bf16[12,1568]{1,0:T(8,128)(2,1)S(1)}, u32[]{:S(2)}, u32[]{:S(2)}) %collective-permute-start) | collective-permute-done | bytes 37664 | tf_op jit(solution)/shard_map/ppermute | solution.py:298
  13.2 1.6 collective-permute-start.3
  15.4 1.1 copy-done.6
  16.6 0.7 copy-done.17
  17.2 2.8 %assign.1 = (s32[1,1024]{1,0:T(1,128)S(1)}, bf16[1280,384]{1,0:T(8,128)(2,1)}) custom-call(s32[1]{0:T(128)S(6)} %copy.46.count_ref, s32[1,1024]{1,0:T(1,128)S(1)} %bitcast.70, bf16[1024,384]{1,0:T(8,128)(2,1)S(1)} %copy-done.6), custom_call_target="tpu_custom_call" | custom-call | flops 1006632960 | bytes 4000000 | tf_op jit(solution)/shard_map/assign/pallas_call | solution.py:498
  20.0 0.2 maximum_select_fusion.3
  20.2 1.6 collective-permute-start.4
  21.7 5.9 %collective-permute-done.4 = bf16[4,24,1568]{2,1,0:T(8,128)(2,1)S(1)} collective-permute-done((bf16[4,24,1568]{2,1,0:T(8,128)(2,1)S(1)}, bf16[4,24,1568]{2,1,0:T(8,128)(2,1)S(1)}, u32[]{:S(2)}, u32[]{:S(2)}) %collective-permute-start.4) | collective-permute-done | bytes 301088 | tf_op jit(solution)/shard_map/ppermute | solution.py:298
  28.0 1.9 collective-permute-done.5
  29.9 0.8 copy-done.22
  30.7 1.8 maximum_select_fusion
  32.5 3.4 %all-to-all-start = ((bf16[32,40,384]{2,1,0:T(8,128)(2,1)}), bf16[32,40,384]{2,1,0:T(8,128)(2,1)}, u32[]{:S(2)}, u32[]{:S(2)}) async-start(bf16[32,40,384]{2,1,0:T(8,128)(2,1)} %bitcast.15), calls=%async_computation | async-start | bytes 1966080 | tf_op jit(solution)/shard_map/all_to_all | solution.py:285
  36.6 0.3 reshape.345
  36.9 0.7 fusion.17
  37.6 0.6 fusion.10.table_ref
  38.2 1.4 fusion
  39.6 0.2 reshape.347
  39.8 1.0 copy.45
  40.8 1.3 reshape.348.bias_ref
  42.1 10.5 %front.1 = (bf16[1280,384]{1,0:T(8,128)(2,1)}, f32[1024,384]{1,0:T(8,128)S(1)}, f32[1024,384]{1,0:T(8,128)}, bf16[1024,384]{1,0:T(8,128)(2,1)S(1)}, f32[1024,768...) custom-call(s32[1,1024]{1,0:T(1,128)S(1)} %get-tuple-element.71.dest_ref, ...), custom_call_target="tpu_custom_call" | custom-call | flops 2415919104 | bytes 20000000 | tf_op jit(solution)/shard_map/front/pallas_call | solution.py:609
  52.6 1.2 copy-done.3
  53.8 0.9 copy-done.9
  54.6 7.4 %all-to-all-done = bf16[32,40,384]{2,1,0:T(8,128)(2,1)} async-done(((bf16[32,40,384]{2,1,0:T(8,128)(2,1)}), bf16[32,40,384]{2,1,0:T(8,128)(2,1)}, u32[]{:S(2)}, u32[]{:S(2)}) %all-to-all-start) | async-done | bytes 983072 | tf_op jit(solution)/shard_map/all_to_all | solution.py:285
  62.1 3.6 %all-to-all-start.1 = ((bf16[32,40,384]{2,1,0:T(8,128)(2,1)}), bf16[32,40,384]{2,1,0:T(8,128)(2,1)}, u32[]{:S(2)}, u32[]{:S(2)}) async-start(bf16[32,40,384]{2,1,0:T(8,128)(2,1)} %bitcast.17), calls=%async_computation.1 | async-start | bytes 1966080 | tf_op jit(solution)/shard_map/all_to_all | solution.py:285
  65.7 0.6 slice.76.bias_one_ref
  66.3 3.0 %convert_bitcast_fusion.1.first_ref = bf16[384,1536]{1,0:T(8,128)(2,1)} fusion(f32[1,384,1536]{2,1,0:T(8,128)} %param.31), kind=kLoop, calls=%fused_computation.19 | loop fusion | flops 589824 | bytes 3538944 | tf_op jit(solution)/shard_map/convert_element_type | solution.py:1350
  69.2 1.1 convert_bitcast_fusion.second_ref
  70.4 0.2 convert_reduce_fusion.1
  70.6 0.6 pad_maximum_fusion.3.vecs_ref
  71.2 20.4 %all-to-all-done.1 = bf16[32,40,384]{2,1,0:T(8,128)(2,1)} async-done(((bf16[32,40,384]{2,1,0:T(8,128)(2,1)}), bf16[32,40,384]{2,1,0:T(8,128)(2,1)}, u32[]{:S(2)}, u32[]{:S(2)}) %all-to-all-start.1) | async-done | bytes 983072 | tf_op jit(solution)/shard_map/all_to_all | solution.py:285
  91.6 15.3 %expert.1 = (bf16[1280,384]{1,0:T(8,128)(2,1)}, bf16[1280,384]{1,0:T(8,128)(2,1)}, bf16[1280,1536]{1,0:T(8,128)(2,1)}, bf16[1280,1536]{1,0:T(8,128)(2,1)}, bf16[...) custom-call(bf16[1280,384]{1,0:T(8,128)(2,1)} %bitcast.18.rows_ref, bf16[1280,384]{1,0:T(8,128)(2,1)} %bitcast.16.cot_ref, ...), custom_call_target="tpu_custom_call" | custom-call | flops 6039797760 | bytes 16000000 | tf_op jit(solution)/shard_map/expert/pallas_call | solution.py:1062
  106.9 2.9 %all-to-all-start.2 = ((bf16[32,40,384]{2,1,0:T(8,128)(2,1)}), bf16[32,40,384]{2,1,0:T(8,128)(2,1)S(1)}, u32[]{:S(2)}, u32[]{:S(2)}) async-start(bf16[32,40,384]{2,1,0:T(8,128)(2,1)} %bitcast.78), calls=%async_computation.2 | async-start | bytes 1966080 | tf_op jit(solution)/shard_map/all_to_all | solution.py:285
  109.9 11.3 %fusion.29 = (bf16[1,384,1536]{2,1,0:T(8,128)(2,1)}, f32[1,384,1536]{2,1,0:T(8,128)}, f32[1,384,1536]{2,1,0:T(8,128)}, f32[1,384,1536]{2,1,0:T(8,128)}) fusion(f32[1,384,1536]{2,1,0:T(8,128)} %param.31, f32[1,384,1536]{2,1,0:T(8,128)} %param.32, f32[1,384,1536]{2,1,0:T(8,128)} %param.33, bf16[1280,384]{1,0:T(8,128)(2,1)} %bitcast.18.rows_ref, ...), kind=kOutput, calls=%fused_computation.75 | convolution fusion | flops 1519386624 | bytes 20250624 | tf_op jit(solution)/shard_map/dot_general | solution.py:414
  121.2 7.1 %fusion.27 = (bf16[1,1536,384]{2,1,0:T(8,128)(2,1)}, f32[1,1536,384]{2,1,0:T(8,128)}, f32[1,1536,384]{2,1,0:T(8,128)}, f32[1,1536,384]{2,1,0:T(8,128)}) fusion(f32[1,1536,384]{2,1,0:T(8,128)S(1)} %copy-done.20, f32[1,1536,384]{2,1,0:T(8,128)S(1)} %copy-done.35, f32[1,1536,384]{2,1,0:T(8,128)S(1)} %copy-done.36, bf16[1280,1536]{1,0:T(8,128)(2,1)S(1)} %copy-done.37, ...), kind=kOutput, calls=%fused_computation.74 | convolution fusion | flops 1519386624 | bytes 20250624 | tf_op jit(solution)/shard_map/dot_general | solution.py:414
  128.3 7.4 %all-to-all-done.2 = bf16[32,40,384]{2,1,0:T(8,128)(2,1)S(1)} async-done(((bf16[32,40,384]{2,1,0:T(8,128)(2,1)}), bf16[32,40,384]{2,1,0:T(8,128)(2,1)S(1)}, u32[]{:S(2)}, u32[]{:S(2)}) %all-to-all-start.2) | async-done | bytes 983072 | tf_op jit(solution)/shard_map/all_to_all | solution.py:285
  135.8 2.9 %all-to-all-start.3 = ((bf16[32,40,384]{2,1,0:T(8,128)(2,1)}), bf16[32,40,384]{2,1,0:T(8,128)(2,1)S(1)}, u32[]{:S(2)}, u32[]{:S(2)}) async-start(bf16[32,40,384]{2,1,0:T(8,128)(2,1)} %bitcast.77), calls=%async_computation.3 | async-start | bytes 1966080 | tf_op jit(solution)/shard_map/all_to_all | solution.py:285
  138.9 0.6 pad_maximum_fusion.1.net_ref
  139.5 15.9 %back.1 = (f32[1024,384]{1,0:T(8,128)}, bf16[1024,384]{1,0:T(8,128)(2,1)}, bf16[1024,1152]{1,0:T(8,128)(2,1)}, f32[32,512]{1,0:T(8,128)}) custom-call(s32[1]{0:T(128)S(6)} %copy.46.count_ref, s32[1,1024]{1,0:T(1,128)} %copy-done.14, bf16[1280,384]{1,0:T(8,128)(2,1)} %bitcast.71, bf16[1024,384]{1,0:T(8,128)(2,1)} %cot_ref.2, bf16[384,1568]{1,0:T(8,128)(2,1)} %bitcast.67, ...), custom_call_target="tpu_custom_call" | custom-call | flops 3019898880 | bytes 20000000 | tf_op jit(solution)/shard_map/back/pallas_call | solution.py:821
  155.5 1.1 copy-done.10
  156.6 1.1 copy-done.11
  157.8 3.5 %dense.1 = (bf16[16,24,896]{2,1,0:T(8,128)(2,1)S(1)}, f32[16,24,896]{2,1,0:T(8,128)S(1)}) custom-call(s32[2]{0:T(128)S(1)} %pad_add_fusion.place_ref, bf16[1024,384]{1,0:T(8,128)(2,1)S(1)} %copy-done.8, bf16[1024,384]{1,0:T(8,128)(2,1)S(1)} %copy-done.10, bf16[1024,384]{1,0:T(8,128)(2,1)S(1)} %copy-done.11, ...), custom_call_target="tpu_custom_call" | custom-call | flops 1207959552 | bytes 7000000 | tf_op jit(solution)/shard_map/dense/pallas_call | solution.py:911
  161.3 0.5 collective-permute-start.7
  161.8 1.4 copy-done.5
  163.2 2.8 %inputs.1 = bf16[1024,384]{1,0:T(8,128)(2,1)} custom-call(f32[1024,384]{1,0:T(8,128)S(1)} %copy-done.5, bf16[1024,1152]{1,0:T(8,128)(2,1)S(1)} %copy-done.2, bf16[384,1568]{1,0:T(8,128)(2,1)S(1)} %bitcast.68), custom_call_target="tpu_custom_call" | custom-call | tf_op jit(solution)/shard_map/inputs/pallas_call | solution.py:938
  166.1 1.0 add_convert_fusion
  167.1 3.4 %collective-permute-start.10 = (f32[32,512]{1,0:T(8,128)S(1)}, f32[32,512]{1,0:T(8,128)S(1)}, u32[]{:S(2)}, u32[]{:S(2)}) collective-permute-start(f32[32,512]{1,0:T(8,128)S(1)} %add.206), channel_id=1, source_target_pairs={{0,6},{1,7},{2,4},{3,5},{4,2},{5,3},{6,0},{7,1},{8,14},{9,15},{10,... | collective-permute-start | bytes 196616 | tf_op jit(solution)/shard_map/ppermute | solution.py:379
  170.5 1.0 collective-permute-start.8
  171.5 6.6 %all-to-all-start.4 = ((bf16[16,24,896]{2,1,0:T(8,128)(2,1)}), bf16[16,24,896]{2,1,0:T(8,128)(2,1)S(1)}, u32[]{:S(2)}, u32[]{:S(2)}) async-start(bf16[16,24,896]{2,1,0:T(8,128)(2,1)} %add_convert_fusion), calls=%async_computation.4 | async-start | bytes 1376256 | tf_op jit(solution)/shard_map/all_to_all | solution.py:396
  178.2 2.9 %collective-permute-start.13 = (f32[32,512]{1,0:T(8,128)S(1)}, f32[32,512]{1,0:T(8,128)S(1)}, u32[]{:S(2)}, u32[]{:S(2)}) collective-permute-start(f32[32,512]{1,0:T(8,128)S(1)} %add_add_fusion.1), channel_id=1, source_target_pairs={{0,17},{1,16},{2,19},{3,18},{4,21},{5,20},{6,23},{7,22},{8,25},{9,... | collective-permute-start | bytes 196616 | tf_op jit(solution)/shard_map/ppermute | solution.py:379
  181.1 0.6 collective-permute-start.12
  181.8 0.7 multiply_subtract_fusion.4
  182.4 1.4 copy-done.4
  183.9 3.1 %layer.1 = bf16[1024,384]{1,0:T(8,128)(2,1)} custom-call(s32[1]{0:T(128)S(6)} %copy.46.count_ref, s32[1,1024]{1,0:T(1,128)S(1)} %copy-done.15, bf16[1280,384]{1,0:T(8,128)(2,1)S(1)} %bitcast.69, f32[1024,384]{1,0:T(8,128)S(1)} %copy-done.4), custom_call_target="tpu_custom_call" | custom-call | tf_op jit(solution)/shard_map/layer/pallas_call | solution.py:967
  187.0 1.3 collective-permute-done.12
  188.6 0.2 reshape.362
  189.0 0.7 multiply_subtract_fusion.3
  189.7 6.3 %all-to-all-done.4 = bf16[16,24,896]{2,1,0:T(8,128)(2,1)S(1)} async-done(((bf16[16,24,896]{2,1,0:T(8,128)(2,1)}), bf16[16,24,896]{2,1,0:T(8,128)(2,1)S(1)}, u32[]{:S(2)}, u32[]{:S(2)}) %all-to-all-start.4) | async-done | bytes 688160 | tf_op jit(solution)/shard_map/all_to_all | solution.py:396
  196.1 0.8 multiply_subtract_fusion.2
  (126 shorter events, 2.3 us)
Async XLA Ops:
  1.6 6.8 %collective-permute-start.2 = (bf16[12,1568]{1,0:T(8,128)(2,1)S(1)}, bf16[12,1568]{1,0:T(8,128)(2,1)S(1)}, u32[]{:S(2)}, u32[]{:S(2)}) collective-permute-start(bf16[12,1568]{1,0:T(8,128)(2,1)S(1)} %convert_element_type.30), channel_id=1, source_target_pairs={{0,4},{1,5},{2,6},{3,7},{4,0},{5,1},{6,2},{7,3},{8,12},{9,13},{10,... | collective-permute-start | bytes 112904 | tf_op jit(solution)/shard_map/ppermute | solution.py:298
  5.6 4.1 %collective-permute-start.1 = (bf16[12,1568]{1,0:T(8,128)(2,1)S(1)}, bf16[12,1568]{1,0:T(8,128)(2,1)S(1)}, u32[]{:S(2)}, u32[]{:S(2)}) collective-permute-start(bf16[12,1568]{1,0:T(8,128)(2,1)S(1)} %convert_element_type.30), channel_id=1, source_target_pairs={{0,2},{1,3},{2,0},{3,1},{4,6},{5,7},{6,4},{7,5},{8,10},{9,11},{10,... | collective-permute-start | bytes 112904 | tf_op jit(solution)/shard_map/ppermute | solution.py:298
  7.2 5.9 %collective-permute-start = (bf16[12,1568]{1,0:T(8,128)(2,1)S(1)}, bf16[12,1568]{1,0:T(8,128)(2,1)S(1)}, u32[]{:S(2)}, u32[]{:S(2)}) collective-permute-start(bf16[12,1568]{1,0:T(8,128)(2,1)S(1)} %convert_element_type.30), channel_id=1, source_target_pairs={{0,6},{1,7},{2,4},{3,5},{4,2},{5,3},{6,0},{7,1},{8,14},{9,15},{10,... | collective-permute-start | bytes 112904 | tf_op jit(solution)/shard_map/ppermute | solution.py:298
  13.2 6.8 %collective-permute-start.3 = (bf16[4,12,1568]{2,1,0:T(8,128)(2,1)S(1)}, bf16[4,12,1568]{2,1,0:T(8,128)(2,1)S(1)}, u32[]{:S(2)}, u32[]{:S(2)}) collective-permute-start(bf16[4,12,1568]{2,1,0:T(8,128)(2,1)S(1)} %maximum_select_fusion.4), channel_id=1, source_target_pairs={{0,1},{1,0},{2,3},{3,2},{4,5},{5,4},{6,7},{7,6},{8,9},{9,8},{10,11... | collective-permute-start | bytes 451592 | tf_op jit(solution)/shard_map/ppermute | solution.py:298
  15.4 1.1 copy-start.6
  16.5 0.7 copy-start.17
  20.0 22.1 %copy-start.14 = (s32[1,1024]{1,0:T(1,128)}, s32[1,1024]{1,0:T(1,128)S(1)}, u32[]{:S(2)}) copy-start(s32[1,1024]{1,0:T(1,128)S(1)} %get-tuple-element.71.dest_ref) | copy-start | bytes 12292
  20.2 7.5 %collective-permute-start.4 = (bf16[4,24,1568]{2,1,0:T(8,128)(2,1)S(1)}, bf16[4,24,1568]{2,1,0:T(8,128)(2,1)S(1)}, u32[]{:S(2)}, u32[]{:S(2)}) collective-permute-start(bf16[4,24,1568]{2,1,0:T(8,128)(2,1)S(1)} %maximum_select_fusion.3), channel_id=1, source_target_pairs={{0,16},{8,24},{16,0},{24,8},{1,17},{9,25},{17,1},{25,9},{2,18},{10... | collective-permute-start | bytes 903176 | tf_op jit(solution)/shard_map/ppermute | solution.py:298
  27.8 2.1 %collective-permute-start.5 = (bf16[2,4,24,1568]{3,2,1,0:T(8,128)(2,1)S(1)}, bf16[2,4,24,1568]{3,2,1,0:T(8,128)(2,1)S(1)}, u32[]{:S(2)}, u32[]{:S(2)}) collective-permute-start(bf16[2,4,24,1568]{3,2,1,0:T(8,128)(2,1)S(1)} %maximum_select_fusion.1), channel_id=1, source_target_pairs={{0,8},{8,0},{16,24},{24,16},{1,9},{9,1},{17,25},{25,17},{2,10},{10... | collective-permute-start | bytes 1806344 | tf_op jit(solution)/shard_map/ppermute | solution.py:298
  28.0 8.1 %copy-start.23 = (f32[10380]{0:T(1024)S(1)}, f32[10380]{0:T(1024)}, u32[]{:S(2)}) copy-start(f32[10380]{0:T(1024)} %param.28) | copy-start | bytes 124564
  29.9 0.8 copy-start.22
  30.7 5.8 %slice-start = ((f32[10380]{0:T(1024)}), f32[2688]{0:T(1024)S(1)}, s32[]{:S(2)}) async-start(f32[10380]{0:T(1024)} %param.28), calls=%async_computation.5 | async-start | bytes 24576 | tf_op jit(solution)/shard_map/slice | solution.py:1341
  30.7 6.1 %copy-start.24 = (f32[256,2]{1,0:T(8,128)S(1)}, f32[256,2]{1,0:T(8,128)}, u32[]{:S(2)}) copy-start(f32[256,2]{1,0:T(8,128)} %constant.144.clone.coords_ref) | copy-start | bytes 6148
  32.5 37.8 %copy-start = (bf16[2,2,4,24,1568]{4,3,2,1,0:T(8,128)(2,1)}, bf16[2,2,4,24,1568]{4,3,2,1,0:T(8,128)(2,1)S(1)}, u32[]{:S(2)}) copy-start(bf16[2,2,4,24,1568]{4,3,2,1,0:T(8,128)(2,1)S(1)} %maximum_select_fusion) | copy-start | bytes 3612676
  32.5 29.6 %all-to-all-start = ((bf16[32,40,384]{2,1,0:T(8,128)(2,1)}), bf16[32,40,384]{2,1,0:T(8,128)(2,1)}, u32[]{:S(2)}, u32[]{:S(2)}) async-start(bf16[32,40,384]{2,1,0:T(8,128)(2,1)} %bitcast.15), calls=%async_computation | async-start | bytes 1966080 | tf_op jit(solution)/shard_map/all_to_all | solution.py:285
  36.6 5.5 %copy-start.16 = (f32[3,1,256]{2,1,0:T(1,128)}, f32[3,1,256]{2,1,0:T(1,128)S(1)}, u32[]{:S(2)}) copy-start(f32[3,1,256]{2,1,0:T(1,128)S(1)} %broadcast_in_dim.7.scale_ref) | copy-start | bytes 9220
  36.6 5.5 %copy-start.13 = (f32[7,384]{1,0:T(8,128)}, f32[7,384]{1,0:T(8,128)S(1)}, u32[]{:S(2)}) copy-start(f32[7,384]{1,0:T(8,128)S(1)} %reshape.344.rows_ref) | copy-start | bytes 32260
  36.9 5.2 %copy-start.7 = (bf16[1024,384]{1,0:T(8,128)(2,1)S(1)}, bf16[1024,384]{1,0:T(8,128)(2,1)}, u32[]{:S(2)}) copy-start(bf16[1024,384]{1,0:T(8,128)(2,1)} %tokens_ref.3) | copy-start | bytes 2359300
  38.2 14.4 %copy-start.27 = (f32[12,256]{1,0:T(8,128)}, f32[12,256]{1,0:T(8,128)S(1)}, u32[]{:S(2)}) copy-start(f32[12,256]{1,0:T(8,128)S(1)} %fusion.10.table_ref) | copy-start | bytes 36868
  42.1 23.5 %copy-start.31 = (f32[1,1920]{1,0:T(1,128)S(1)}, f32[1,1920]{1,0:T(1,128)}, u32[]{:S(2)}) copy-start(f32[1,1920]{1,0:T(1,128)} %param.37) | copy-start | bytes 23044
  52.6 1.2 copy-start.3
  53.8 0.9 copy-start.9
  62.1 29.6 %all-to-all-start.1 = ((bf16[32,40,384]{2,1,0:T(8,128)(2,1)}), bf16[32,40,384]{2,1,0:T(8,128)(2,1)}, u32[]{:S(2)}, u32[]{:S(2)}) async-start(bf16[32,40,384]{2,1,0:T(8,128)(2,1)} %bitcast.17), calls=%async_computation.1 | async-start | bytes 1966080 | tf_op jit(solution)/shard_map/all_to_all | solution.py:285
  66.3 3.0 %copy-start.19 = (f32[1,1536,384]{2,1,0:T(8,128)S(1)}, f32[1,1536,384]{2,1,0:T(8,128)}, u32[]{:S(2)}) copy-start(f32[1,1536,384]{2,1,0:T(8,128)} %param.34) | copy-start | bytes 7077892
  69.2 1.4 slice-start.1
  106.9 28.8 %all-to-all-start.2 = ((bf16[32,40,384]{2,1,0:T(8,128)(2,1)}), bf16[32,40,384]{2,1,0:T(8,128)(2,1)S(1)}, u32[]{:S(2)}, u32[]{:S(2)}) async-start(bf16[32,40,384]{2,1,0:T(8,128)(2,1)} %bitcast.78), calls=%async_computation.2 | async-start | bytes 1966080 | tf_op jit(solution)/shard_map/all_to_all | solution.py:285
  109.8 11.4 %copy-start.20 = (f32[1,1536,384]{2,1,0:T(8,128)S(1)}, f32[1,1536,384]{2,1,0:T(8,128)}, u32[]{:S(2)}) copy-start(f32[1,1536,384]{2,1,0:T(8,128)} %param.34) | copy-start | bytes 7077892
  109.8 11.4 %copy-start.35 = (f32[1,1536,384]{2,1,0:T(8,128)S(1)}, f32[1,1536,384]{2,1,0:T(8,128)}, u32[]{:S(2)}) copy-start(f32[1,1536,384]{2,1,0:T(8,128)} %param.35) | copy-start | bytes 7077892
  109.8 11.4 %copy-start.36 = (f32[1,1536,384]{2,1,0:T(8,128)S(1)}, f32[1,1536,384]{2,1,0:T(8,128)}, u32[]{:S(2)}) copy-start(f32[1,1536,384]{2,1,0:T(8,128)} %param.36) | copy-start | bytes 7077892
  109.9 11.4 %copy-start.37 = (bf16[1280,1536]{1,0:T(8,128)(2,1)S(1)}, bf16[1280,1536]{1,0:T(8,128)(2,1)}, u32[]{:S(2)}) copy-start(bf16[1280,1536]{1,0:T(8,128)(2,1)} %get-tuple-element.84) | copy-start | bytes 11796484
  109.9 11.4 %copy-start.38 = (bf16[1280,384]{1,0:T(8,128)(2,1)S(1)}, bf16[1280,384]{1,0:T(8,128)(2,1)}, u32[]{:S(2)}) copy-start(bf16[1280,384]{1,0:T(8,128)(2,1)} %get-tuple-element.85) | copy-start | bytes 2949124
  135.8 3.8 %copy-start.18 = (bf16[32,40,384]{2,1,0:T(8,128)(2,1)}, bf16[32,40,384]{2,1,0:T(8,128)(2,1)S(1)}, u32[]{:S(2)}) copy-start(bf16[32,40,384]{2,1,0:T(8,128)(2,1)S(1)} %all-to-all-done.2) | copy-start | bytes 2949124
  135.8 31.3 %all-to-all-start.3 = ((bf16[32,40,384]{2,1,0:T(8,128)(2,1)}), bf16[32,40,384]{2,1,0:T(8,128)(2,1)S(1)}, u32[]{:S(2)}, u32[]{:S(2)}) async-start(bf16[32,40,384]{2,1,0:T(8,128)(2,1)} %bitcast.77), calls=%async_computation.3 | async-start | bytes 1966080 | tf_op jit(solution)/shard_map/all_to_all | solution.py:285
  139.5 15.9 %copy-start.8 = (bf16[1024,384]{1,0:T(8,128)(2,1)S(1)}, bf16[1024,384]{1,0:T(8,128)(2,1)}, u32[]{:S(2)}) copy-start(bf16[1024,384]{1,0:T(8,128)(2,1)} %tokens_ref.3) | copy-start | bytes 2359300
  139.5 15.9 %copy-start.12 = (f32[8,384]{1,0:T(8,128)S(1)}, f32[8,384]{1,0:T(8,128)}, u32[]{:S(2)}) copy-start(f32[8,384]{1,0:T(8,128)} %get-tuple-element.91.expert_ref) | copy-start | bytes 36868
  155.5 1.1 copy-start.10
  156.6 1.1 copy-start.11
  157.7 3.6 %copy-start.28 = (f32[32,512]{1,0:T(8,128)S(1)}, f32[32,512]{1,0:T(8,128)}, u32[]{:S(2)}) copy-start(f32[32,512]{1,0:T(8,128)} %get-tuple-element.96) | copy-start | bytes 196612
  157.8 4.0 %copy-start.1 = (bf16[2,2,4,24,1568]{4,3,2,1,0:T(8,128)(2,1)S(1)}, bf16[2,2,4,24,1568]{4,3,2,1,0:T(8,128)(2,1)}, u32[]{:S(2)}) copy-start(bf16[2,2,4,24,1568]{4,3,2,1,0:T(8,128)(2,1)} %copy-done) | copy-start | bytes 3612676
  157.8 4.0 %copy-start.2 = (bf16[1024,1152]{1,0:T(8,128)(2,1)S(1)}, bf16[1024,1152]{1,0:T(8,128)(2,1)}, u32[]{:S(2)}) copy-start(bf16[1024,1152]{1,0:T(8,128)(2,1)} %get-tuple-element.93.projected_ref) | copy-start | bytes 7077892
  161.2 4.9 %collective-permute-start.6 = (bf16[16,24,896]{2,1,0:T(8,128)(2,1)S(1)}, bf16[16,24,896]{2,1,0:T(8,128)(2,1)S(1)}, u32[]{:S(2)}, u32[]{:S(2)}) collective-permute-start(bf16[16,24,896]{2,1,0:T(8,128)(2,1)S(1)} %get-tuple-element.95), channel_id=1, source_target_pairs={{0,8},{8,0},{16,24},{24,16},{1,9},{9,1},{17,25},{25,17},{2,10},{10... | collective-permute-start | bytes 2064392 | tf_op jit(solution)/shard_map/ppermute | solution.py:298
  161.3 4.8 %collective-permute-start.7 = (f32[32,512]{1,0:T(8,128)S(1)}, f32[32,512]{1,0:T(8,128)S(1)}, u32[]{:S(2)}, u32[]{:S(2)}) collective-permute-start(f32[32,512]{1,0:T(8,128)S(1)} %copy-done.28), channel_id=1, source_target_pairs={{0,8},{1,9},{2,10},{3,11},{4,12},{5,13},{6,14},{7,15},{8,0},{9,1},... | collective-permute-start | bytes 196616 | tf_op jit(solution)/shard_map/ppermute | solution.py:379
  161.8 1.4 copy-start.5
  166.1 15.7 %copy-start.32 = (f32[1,1920]{1,0:T(1,128)S(1)}, f32[1,1920]{1,0:T(1,128)}, u32[]{:S(2)}) copy-start(f32[1,1920]{1,0:T(1,128)} %param.38) | copy-start | bytes 23044
  166.1 15.7 %copy-start.33 = (f32[1,1920]{1,0:T(1,128)S(1)}, f32[1,1920]{1,0:T(1,128)}, u32[]{:S(2)}) copy-start(f32[1,1920]{1,0:T(1,128)} %param.39) | copy-start | bytes 23044
  166.1 15.7 %copy-start.34 = (f32[1,1536]{1,0:T(1,128)S(1)}, f32[1,1536]{1,0:T(1,128)}, u32[]{:S(2)}) copy-start(f32[1,1536]{1,0:T(1,128)} %get-tuple-element.112) | copy-start | bytes 18436
  166.1 16.4 %copy-start.15 = (s32[1,1024]{1,0:T(1,128)S(1)}, s32[1,1024]{1,0:T(1,128)}, u32[]{:S(2)}) copy-start(s32[1,1024]{1,0:T(1,128)} %copy-done.14) | copy-start | bytes 12292
  167.1 11.0 %collective-permute-start.10 = (f32[32,512]{1,0:T(8,128)S(1)}, f32[32,512]{1,0:T(8,128)S(1)}, u32[]{:S(2)}, u32[]{:S(2)}) collective-permute-start(f32[32,512]{1,0:T(8,128)S(1)} %add.206), channel_id=1, source_target_pairs={{0,6},{1,7},{2,4},{3,5},{4,2},{5,3},{6,0},{7,1},{8,14},{9,15},{10,... | collective-permute-start | bytes 196616 | tf_op jit(solution)/shard_map/ppermute | solution.py:379
  170.5 7.6 %collective-permute-start.9 = (f32[32,512]{1,0:T(8,128)S(1)}, f32[32,512]{1,0:T(8,128)S(1)}, u32[]{:S(2)}, u32[]{:S(2)}) collective-permute-start(f32[32,512]{1,0:T(8,128)S(1)} %add.206), channel_id=1, source_target_pairs={{0,4},{1,5},{2,6},{3,7},{4,0},{5,1},{6,2},{7,3},{8,12},{9,13},{10,... | collective-permute-start | bytes 196616 | tf_op jit(solution)/shard_map/ppermute | solution.py:379
  170.5 7.6 %collective-permute-start.8 = (f32[32,512]{1,0:T(8,128)S(1)}, f32[32,512]{1,0:T(8,128)S(1)}, u32[]{:S(2)}, u32[]{:S(2)}) collective-permute-start(f32[32,512]{1,0:T(8,128)S(1)} %add.206), channel_id=1, source_target_pairs={{0,2},{1,3},{2,0},{3,1},{4,6},{5,7},{6,4},{7,5},{8,10},{9,11},{10,... | collective-permute-start | bytes 196616 | tf_op jit(solution)/shard_map/ppermute | solution.py:379
  171.5 24.4 %all-to-all-start.4 = ((bf16[16,24,896]{2,1,0:T(8,128)(2,1)}), bf16[16,24,896]{2,1,0:T(8,128)(2,1)S(1)}, u32[]{:S(2)}, u32[]{:S(2)}) async-start(bf16[16,24,896]{2,1,0:T(8,128)(2,1)} %add_convert_fusion), calls=%async_computation.4 | async-start | bytes 1376256 | tf_op jit(solution)/shard_map/all_to_all | solution.py:396
  178.2 10.8 %copy-start.30 = (f32[10380]{0:T(1024)S(1)}, f32[10380]{0:T(1024)}, u32[]{:S(2)}) copy-start(f32[10380]{0:T(1024)} %param.30) | copy-start | bytes 124564
  178.2 10.8 %copy-start.29 = (f32[10380]{0:T(1024)S(1)}, f32[10380]{0:T(1024)}, u32[]{:S(2)}) copy-start(f32[10380]{0:T(1024)} %param.29) | copy-start | bytes 124564
  178.2 8.8 %collective-permute-start.13 = (f32[32,512]{1,0:T(8,128)S(1)}, f32[32,512]{1,0:T(8,128)S(1)}, u32[]{:S(2)}, u32[]{:S(2)}) collective-permute-start(f32[32,512]{1,0:T(8,128)S(1)} %add_add_fusion.1), channel_id=1, source_target_pairs={{0,17},{1,16},{2,19},{3,18},{4,21},{5,20},{6,23},{7,22},{8,25},{9,... | collective-permute-start | bytes 196616 | tf_op jit(solution)/shard_map/ppermute | solution.py:379
  181.1 7.2 %collective-permute-start.12 = (f32[32,512]{1,0:T(8,128)S(1)}, f32[32,512]{1,0:T(8,128)S(1)}, u32[]{:S(2)}, u32[]{:S(2)}) collective-permute-start(f32[32,512]{1,0:T(8,128)S(1)} %add_add_fusion.1), channel_id=1, source_target_pairs={{0,16},{1,17},{2,18},{3,19},{4,20},{5,21},{6,22},{7,23},{8,24},{9,... | collective-permute-start | bytes 196616 | tf_op jit(solution)/shard_map/ppermute | solution.py:379
  181.7 6.6 %collective-permute-start.11 = (f32[32,512]{1,0:T(8,128)S(1)}, f32[32,512]{1,0:T(8,128)S(1)}, u32[]{:S(2)}, u32[]{:S(2)}) collective-permute-start(f32[32,512]{1,0:T(8,128)S(1)} %add_add_fusion.1), channel_id=1, source_target_pairs={{0,1},{1,0},{2,3},{3,2},{4,5},{5,4},{6,7},{7,6},{8,9},{9,8},{10,11... | collective-permute-start | bytes 196616 | tf_op jit(solution)/shard_map/ppermute | solution.py:379
  182.4 1.4 copy-start.4
  183.8 12.2 %copy-start.21 = (f32[12,1568]{1,0:T(8,128)S(1)}, f32[12,1568]{1,0:T(8,128)}, u32[]{:S(2)}) copy-start(f32[12,1568]{1,0:T(8,128)} %param.25) | copy-start | bytes 225796
  183.8 12.2 %copy-start.25 = (f32[12,1568]{1,0:T(8,128)S(1)}, f32[12,1568]{1,0:T(8,128)}, u32[]{:S(2)}) copy-start(f32[12,1568]{1,0:T(8,128)} %param.26) | copy-start | bytes 225796
  183.9 12.2 %copy-start.26 = (f32[12,1568]{1,0:T(8,128)S(1)}, f32[12,1568]{1,0:T(8,128)}, u32[]{:S(2)}) copy-start(f32[12,1568]{1,0:T(8,128)} %param.27) | copy-start | bytes 225796

commit v3 on v2

--- a/solution.py
+++ b/solution.py
@@ -1325,16 +1325,15 @@
     share = dense_weight.astype(jnp.bfloat16)
     across, *deep = axis_bits("narrow")
     held = join_quad(share, deep)
+    held = join(held, across, -2)
     held, route_ids, cot = lax.optimization_barrier((held, routes, cotangent))
     dest, placed_cot = call_assign(images, route_ids, cot, capacity)
-    held = join(held, across, -2)
-    held, placed_cot, dest = lax.optimization_barrier((held, placed_cot, dest))
+    cot_rows = trade(placed_cot)
     core, *rest = axis_bits("wide")
     for step in rest:
         held = join(held, step)
+    held, params = lax.optimization_barrier((held, small_params))
     gathered = join(held, core, len(rest)).reshape(-1, share.shape[-1])
-    gathered, placed_cot, params = lax.optimization_barrier((gathered, placed_cot, small_params))
-    cot_rows = trade(placed_cot)
     table = bias_table(params)
     net_pieces = pieces(params)
     net = jnp.concatenate([net_pieces[10].T, net_pieces[8][None, :], net_pieces[9]])
@@ -1393,9 +1392,7 @@
     held = sum_chip(send, keep)
     narrow = lax.axis_size("narrow")
     sums = sums + swap_flat(sums, narrow)
-    held, sums, branch_rows, grad_inputs = lax.optimization_barrier(
-        (held, sums, branch_rows, grad_inputs)
-    )
+    held, sums, branch_rows = lax.optimization_barrier((held, sums, branch_rows))
     grad_dense = sum_shares(held)
     sums = sum_quads(sum_quads(sums, 2, 4), 1, 2 * narrow)
     layer_out = call_layer(images, dest, branch_rows, section)

time: 198 us -> 188 us (0.949)
  waiting for transfers between devices: 55.7 us -> 48.6 us
  local copies, waits for them, and re-layouts: 14.4 us -> 12.2 us
    ppermute x7, waiting for transfers between devices: 12.8 us -> 8.72 us  [swap(): lax.ppermute(value, axis, [(i, i ^ offset) for i in range(lax.axis_size(a...]
    all_to_all x1, waiting for transfers between devices: 6.26 us -> 2.99 us  [sum_shares(): lax.all_to_all(held, ('wide', 'narrow'), 0, 0, axis_index_groups=groups,...]
  transfers between devices with their start and end apart: 19 -> 19, of which waited for: 10 -> 10; matrix products, arithmetic and copies ran while one was open for 18% -> 19% of each run, Pallas kernels for 20% -> 21%
where the time goes in v3:
time: 188 us; the launch traced here: 187 us
  Pallas kernels  53.8 us (29%)
  waiting for transfers between devices  48.6 us (26%)
  starting transfers between devices  36.6 us (19%)
  matrix products  21.1 us (11%)
  other arithmetic  12.9 us (7%)
  local copies, waits for them, and re-layouts  12.2 us (6%)
  between operations  1.96 us (1%)
    all_to_all x4, waiting for transfers between devices, trade_rows(): lax.all_to_all(payload, ('wide', 'narrow'), split_axis=0, concat_axis=0,...  35.2 us
    dot_general x2, matrix products, dot_rows(): lax.dot_general(left, right, contract_rows, preferred_element_type=jnp.fl...  18.4 us
    pallas_call x1, Pallas kernels, call_back(): pl.pallas_call(back_kernel, grid=(count // block,), out_shape=(jax.ShapeD...  15.9 us
    pallas_call x1, Pallas kernels, call_expert(): pl.pallas_call(expert_kernel, grid=(count // block,), out_shape=(jax.Shap...  15.3 us
    all_to_all x4, starting transfers between devices, trade_rows(): lax.all_to_all(payload, ('wide', 'narrow'), split_axis=0, concat_axis=0,...  12.8 us
    pallas_call x1, Pallas kernels, call_front(): pl.pallas_call(front_kernel, grid=(count // block,), out_shape=(jax.Shape...  10.5 us
    unnamed x78, local copies, waits for them, and re-layouts  9.37 us
    ppermute x7, starting transfers between devices, swap(): lax.ppermute(value, axis, [(i, i ^ offset) for i in range(lax.axis_size(a...  8.94 us
  transfers between devices with their start and end apart: 19, of which 10 were waited for; matrix products, arithmetic and copies ran while one was open for 19% of the time, Pallas kernels for 21%

profile of v3, /device:TPU:0, one launch (start us, length us, event | category | flops | bytes accessed | tf_op | source)
XLA Modules:
  0.0 187.2 jit_solution(2196294612836140521)
XLA Ops:
  0.7 0.9 convert_element_type.30
  1.6 4.0 %collective-permute-start.2 = (bf16[12,1568]{1,0:T(8,128)(2,1)S(1)}, bf16[12,1568]{1,0:T(8,128)(2,1)S(1)}, u32[]{:S(2)}, u32[]{:S(2)}) collective-permute-start(bf16[12,1568]{1,0:T(8,128)(2,1)S(1)} %convert_element_type.30), channel_id=1, source_target_pairs={{0,4},{1,5},{2,6},{3,7},{4,0},{5,1},{6,2},{7,3},{8,12},{9,13},{10,... | collective-permute-start | bytes 112904 | tf_op jit(solution)/shard_map/ppermute | solution.py:298
  5.6 1.6 collective-permute-start.1
  7.2 1.2 collective-permute-done.2
  8.4 0.9 select_bitcast_fusion.2
  9.3 0.4 collective-permute-done.1
  9.7 3.4 %collective-permute-done = bf16[12,1568]{1,0:T(8,128)(2,1)S(1)} collective-permute-done((bf16[12,1568]{1,0:T(8,128)(2,1)S(1)}, bf16[12,1568]{1,0:T(8,128)(2,1)S(1)}, u32[]{:S(2)}, u32[]{:S(2)}) %collective-permute-start) | collective-permute-done | bytes 37664 | tf_op jit(solution)/shard_map/ppermute | solution.py:298
  13.2 1.6 collective-permute-start.3
  15.4 3.7 %collective-permute-done.3 = bf16[4,12,1568]{2,1,0:T(8,128)(2,1)S(1)} collective-permute-done((bf16[4,12,1568]{2,1,0:T(8,128)(2,1)S(1)}, bf16[4,12,1568]{2,1,0:T(8,128)(2,1)S(1)}, u32[]{:S(2)}, u32[]{:S(2)}) %collective-permute-start.3) | collective-permute-done | bytes 150560 | tf_op jit(solution)/shard_map/ppermute | solution.py:298
  19.1 0.2 maximum_select_fusion.2
  19.3 1.6 collective-permute-start.4
  20.9 1.1 copy-done.6
  22.0 0.7 copy-done.17
  22.7 2.8 %assign.1 = (s32[1,1024]{1,0:T(1,128)S(1)}, bf16[1280,384]{1,0:T(8,128)(2,1)}) custom-call(s32[1]{0:T(128)S(6)} %copy.48.count_ref, s32[1,1024]{1,0:T(1,128)S(1)} %bitcast.69, bf16[1024,384]{1,0:T(8,128)(2,1)S(1)} %copy-done.6), custom_call_target="tpu_custom_call" | custom-call | flops 1006632960 | bytes 4000000 | tf_op jit(solution)/shard_map/assign/pallas_call | solution.py:498
  25.5 3.5 %all-to-all-start = ((bf16[32,40,384]{2,1,0:T(8,128)(2,1)}), bf16[32,40,384]{2,1,0:T(8,128)(2,1)}, u32[]{:S(2)}, u32[]{:S(2)}) async-start(bf16[32,40,384]{2,1,0:T(8,128)(2,1)} %bitcast.14), calls=%async_computation | async-start | bytes 1966080 | tf_op jit(solution)/shard_map/all_to_all | solution.py:285
  29.8 0.3 reshape.286
  30.2 0.7 fusion.17
  31.0 0.6 fusion.10.table_ref
  31.5 1.4 fusion
  32.9 0.2 reshape.288
  33.1 0.3 copy.47
  33.4 0.3 reshape.289.bias_ref
  33.7 1.6 maximum_select_fusion
  35.4 10.5 %front.1 = (bf16[1280,384]{1,0:T(8,128)(2,1)}, f32[1024,384]{1,0:T(8,128)S(1)}, f32[1024,384]{1,0:T(8,128)}, bf16[1024,384]{1,0:T(8,128)(2,1)S(1)}, f32[1024,768...) custom-call(s32[1,1024]{1,0:T(1,128)S(1)} %get-tuple-element.63.dest_ref, ...), custom_call_target="tpu_custom_call" | custom-call | flops 2415919104 | bytes 20000000 | tf_op jit(solution)/shard_map/front/pallas_call | solution.py:609
  45.9 1.2 copy-done.3
  47.1 0.9 copy-done.9
  48.0 7.1 %all-to-all-done = bf16[32,40,384]{2,1,0:T(8,128)(2,1)} async-done(((bf16[32,40,384]{2,1,0:T(8,128)(2,1)}), bf16[32,40,384]{2,1,0:T(8,128)(2,1)}, u32[]{:S(2)}, u32[]{:S(2)}) %all-to-all-start) | async-done | bytes 983072 | tf_op jit(solution)/shard_map/all_to_all | solution.py:285
  55.1 3.6 %all-to-all-start.1 = ((bf16[32,40,384]{2,1,0:T(8,128)(2,1)}), bf16[32,40,384]{2,1,0:T(8,128)(2,1)}, u32[]{:S(2)}, u32[]{:S(2)}) async-start(bf16[32,40,384]{2,1,0:T(8,128)(2,1)} %bitcast.16), calls=%async_computation.1 | async-start | bytes 1966080 | tf_op jit(solution)/shard_map/all_to_all | solution.py:285
  58.7 0.6 slice.76.bias_one_ref
  59.3 3.0 %convert_bitcast_fusion.1.first_ref = bf16[384,1536]{1,0:T(8,128)(2,1)} fusion(f32[1,384,1536]{2,1,0:T(8,128)} %param.31), kind=kLoop, calls=%fused_computation.19 | loop fusion | flops 589824 | bytes 3538944 | tf_op jit(solution)/shard_map/convert_element_type | solution.py:1349
  62.3 1.1 convert_bitcast_fusion.second_ref
  63.4 0.2 convert_reduce_fusion.1
  63.6 0.6 pad_maximum_fusion.3.vecs_ref
  64.2 20.4 %all-to-all-done.1 = bf16[32,40,384]{2,1,0:T(8,128)(2,1)} async-done(((bf16[32,40,384]{2,1,0:T(8,128)(2,1)}), bf16[32,40,384]{2,1,0:T(8,128)(2,1)}, u32[]{:S(2)}, u32[]{:S(2)}) %all-to-all-start.1) | async-done | bytes 983072 | tf_op jit(solution)/shard_map/all_to_all | solution.py:285
  84.7 15.3 %expert.1 = (bf16[1280,384]{1,0:T(8,128)(2,1)}, bf16[1280,384]{1,0:T(8,128)(2,1)}, bf16[1280,1536]{1,0:T(8,128)(2,1)}, bf16[1280,1536]{1,0:T(8,128)(2,1)}, bf16[...) custom-call(bf16[1280,384]{1,0:T(8,128)(2,1)} %bitcast.17.rows_ref, bf16[1280,384]{1,0:T(8,128)(2,1)} %bitcast.15.cot_ref, ...), custom_call_target="tpu_custom_call" | custom-call | flops 6039797760 | bytes 16000000 | tf_op jit(solution)/shard_map/expert/pallas_call | solution.py:1062
  100.0 2.9 %all-to-all-start.2 = ((bf16[32,40,384]{2,1,0:T(8,128)(2,1)}), bf16[32,40,384]{2,1,0:T(8,128)(2,1)S(1)}, u32[]{:S(2)}, u32[]{:S(2)}) async-start(bf16[32,40,384]{2,1,0:T(8,128)(2,1)} %bitcast.75), calls=%async_computation.2 | async-start | bytes 1966080 | tf_op jit(solution)/shard_map/all_to_all | solution.py:285
  102.9 11.3 %fusion.29 = (bf16[1,384,1536]{2,1,0:T(8,128)(2,1)}, f32[1,384,1536]{2,1,0:T(8,128)}, f32[1,384,1536]{2,1,0:T(8,128)}, f32[1,384,1536]{2,1,0:T(8,128)}) fusion(f32[1,384,1536]{2,1,0:T(8,128)} %param.31, f32[1,384,1536]{2,1,0:T(8,128)} %param.32, f32[1,384,1536]{2,1,0:T(8,128)} %param.33, bf16[1280,384]{1,0:T(8,128)(2,1)} %bitcast.17.rows_ref, ...), kind=kOutput, calls=%fused_computation.74 | convolution fusion | flops 1519386624 | bytes 20250624 | tf_op jit(solution)/shard_map/dot_general | solution.py:414
  114.3 7.1 %fusion.27 = (bf16[1,1536,384]{2,1,0:T(8,128)(2,1)}, f32[1,1536,384]{2,1,0:T(8,128)}, f32[1,1536,384]{2,1,0:T(8,128)}, f32[1,1536,384]{2,1,0:T(8,128)}) fusion(f32[1,1536,384]{2,1,0:T(8,128)S(1)} %copy-done.20, f32[1,1536,384]{2,1,0:T(8,128)S(1)} %copy-done.35, f32[1,1536,384]{2,1,0:T(8,128)S(1)} %copy-done.36, bf16[1280,1536]{1,0:T(8,128)(2,1)S(1)} %copy-done.37, ...), kind=kOutput, calls=%fused_computation.73 | convolution fusion | flops 1519386624 | bytes 20250624 | tf_op jit(solution)/shard_map/dot_general | solution.py:414
  121.4 7.4 %all-to-all-done.2 = bf16[32,40,384]{2,1,0:T(8,128)(2,1)S(1)} async-done(((bf16[32,40,384]{2,1,0:T(8,128)(2,1)}), bf16[32,40,384]{2,1,0:T(8,128)(2,1)S(1)}, u32[]{:S(2)}, u32[]{:S(2)}) %all-to-all-start.2) | async-done | bytes 983072 | tf_op jit(solution)/shard_map/all_to_all | solution.py:285
  128.8 2.9 %all-to-all-start.3 = ((bf16[32,40,384]{2,1,0:T(8,128)(2,1)}), bf16[32,40,384]{2,1,0:T(8,128)(2,1)S(1)}, u32[]{:S(2)}, u32[]{:S(2)}) async-start(bf16[32,40,384]{2,1,0:T(8,128)(2,1)} %bitcast.74), calls=%async_computation.3 | async-start | bytes 1966080 | tf_op jit(solution)/shard_map/all_to_all | solution.py:285
  132.0 0.6 pad_maximum_fusion.1.net_ref
  132.6 15.9 %back.1 = (f32[1024,384]{1,0:T(8,128)}, bf16[1024,384]{1,0:T(8,128)(2,1)}, bf16[1024,1152]{1,0:T(8,128)(2,1)}, f32[32,512]{1,0:T(8,128)}) custom-call(s32[1]{0:T(128)S(6)} %copy.48.count_ref, s32[1,1024]{1,0:T(1,128)} %copy-done.14, bf16[1280,384]{1,0:T(8,128)(2,1)} %bitcast.70, bf16[1024,384]{1,0:T(8,128)(2,1)} %cot_ref.2, bf16[384,1568]{1,0:T(8,128)(2,1)} %bitcast.66, ...), custom_call_target="tpu_custom_call" | custom-call | flops 3019898880 | bytes 20000000 | tf_op jit(solution)/shard_map/back/pallas_call | solution.py:821
  148.6 1.1 copy-done.10
  149.7 1.1 copy-done.11
  150.8 3.3 %dense.1 = (bf16[16,24,896]{2,1,0:T(8,128)(2,1)S(1)}, f32[16,24,896]{2,1,0:T(8,128)S(1)}) custom-call(s32[2]{0:T(128)S(1)} %pad_add_fusion.place_ref, bf16[1024,384]{1,0:T(8,128)(2,1)S(1)} %copy-done.8, bf16[1024,384]{1,0:T(8,128)(2,1)S(1)} %copy-done.10, bf16[1024,384]{1,0:T(8,128)(2,1)S(1)} %copy-done.11, ...), custom_call_target="tpu_custom_call" | custom-call | flops 1207959552 | bytes 7000000 | tf_op jit(solution)/shard_map/dense/pallas_call | solution.py:911
  154.3 0.5 collective-permute-start.7
  154.8 1.7 collective-permute-done.7
  156.5 1.0 add_convert_fusion
  157.5 0.2 all-to-all-done.3
  157.7 3.2 %collective-permute-start.10 = (f32[32,512]{1,0:T(8,128)S(1)}, f32[32,512]{1,0:T(8,128)S(1)}, u32[]{:S(2)}, u32[]{:S(2)}) collective-permute-start(f32[32,512]{1,0:T(8,128)S(1)} %add.206), channel_id=1, source_target_pairs={{0,6},{1,7},{2,4},{3,5},{4,2},{5,3},{6,0},{7,1},{8,14},{9,15},{10,... | collective-permute-start | bytes 196616 | tf_op jit(solution)/shard_map/ppermute | solution.py:379
  160.9 1.2 collective-permute-start.8
  162.1 6.4 %all-to-all-start.4 = ((bf16[16,24,896]{2,1,0:T(8,128)(2,1)}), bf16[16,24,896]{2,1,0:T(8,128)(2,1)S(1)}, u32[]{:S(2)}, u32[]{:S(2)}) async-start(bf16[16,24,896]{2,1,0:T(8,128)(2,1)} %add_convert_fusion), calls=%async_computation.4 | async-start | bytes 1376256 | tf_op jit(solution)/shard_map/all_to_all | solution.py:396
  168.6 2.9 %collective-permute-start.13 = (f32[32,512]{1,0:T(8,128)S(1)}, f32[32,512]{1,0:T(8,128)S(1)}, u32[]{:S(2)}, u32[]{:S(2)}) collective-permute-start(f32[32,512]{1,0:T(8,128)S(1)} %add_add_fusion.1), channel_id=1, source_target_pairs={{0,17},{1,16},{2,19},{3,18},{4,21},{5,20},{6,23},{7,22},{8,25},{9,... | collective-permute-start | bytes 196616 | tf_op jit(solution)/shard_map/ppermute | solution.py:379
  171.5 0.6 collective-permute-start.12
  172.1 0.7 multiply_subtract_fusion.4
  172.8 1.7 copy-done.2
  174.5 1.4 copy-done.5
  175.9 2.8 %inputs.1 = bf16[1024,384]{1,0:T(8,128)(2,1)} custom-call(f32[1024,384]{1,0:T(8,128)S(1)} %copy-done.5, bf16[1024,1152]{1,0:T(8,128)(2,1)S(1)} %copy-done.2, bf16[384,1568]{1,0:T(8,128)(2,1)S(1)} %bitcast.67), custom_call_target="tpu_custom_call" | custom-call | tf_op jit(solution)/shard_map/inputs/pallas_call | solution.py:938
  178.8 3.1 %layer.1 = bf16[1024,384]{1,0:T(8,128)(2,1)} custom-call(s32[1]{0:T(128)S(6)} %copy.48.count_ref, s32[1,1024]{1,0:T(1,128)S(1)} %copy-done.15, bf16[1280,384]{1,0:T(8,128)(2,1)S(1)} %bitcast.68, f32[1024,384]{1,0:T(8,128)S(1)} %copy-done.4), custom_call_target="tpu_custom_call" | custom-call | tf_op jit(solution)/shard_map/layer/pallas_call | solution.py:967
  182.1 0.1 copy.45
  182.2 0.2 reshape.303
  182.7 0.7 multiply_subtract_fusion.3
  183.3 3.0 %all-to-all-done.4 = bf16[16,24,896]{2,1,0:T(8,128)(2,1)S(1)} async-done(((bf16[16,24,896]{2,1,0:T(8,128)(2,1)}), bf16[16,24,896]{2,1,0:T(8,128)(2,1)S(1)}, u32[]{:S(2)}, u32[]{:S(2)}) %all-to-all-start.4) | async-done | bytes 688160 | tf_op jit(solution)/shard_map/all_to_all | solution.py:396
  186.5 0.8 multiply_subtract_fusion.2
  (126 shorter events, 2.1 us)
Async XLA Ops:
  1.6 6.8 %collective-permute-start.2 = (bf16[12,1568]{1,0:T(8,128)(2,1)S(1)}, bf16[12,1568]{1,0:T(8,128)(2,1)S(1)}, u32[]{:S(2)}, u32[]{:S(2)}) collective-permute-start(bf16[12,1568]{1,0:T(8,128)(2,1)S(1)} %convert_element_type.30), channel_id=1, source_target_pairs={{0,4},{1,5},{2,6},{3,7},{4,0},{5,1},{6,2},{7,3},{8,12},{9,13},{10,... | collective-permute-start | bytes 112904 | tf_op jit(solution)/shard_map/ppermute | solution.py:298
  5.6 4.1 %collective-permute-start.1 = (bf16[12,1568]{1,0:T(8,128)(2,1)S(1)}, bf16[12,1568]{1,0:T(8,128)(2,1)S(1)}, u32[]{:S(2)}, u32[]{:S(2)}) collective-permute-start(bf16[12,1568]{1,0:T(8,128)(2,1)S(1)} %convert_element_type.30), channel_id=1, source_target_pairs={{0,2},{1,3},{2,0},{3,1},{4,6},{5,7},{6,4},{7,5},{8,10},{9,11},{10,... | collective-permute-start | bytes 112904 | tf_op jit(solution)/shard_map/ppermute | solution.py:298
  7.2 5.9 %collective-permute-start = (bf16[12,1568]{1,0:T(8,128)(2,1)S(1)}, bf16[12,1568]{1,0:T(8,128)(2,1)S(1)}, u32[]{:S(2)}, u32[]{:S(2)}) collective-permute-start(bf16[12,1568]{1,0:T(8,128)(2,1)S(1)} %convert_element_type.30), channel_id=1, source_target_pairs={{0,6},{1,7},{2,4},{3,5},{4,2},{5,3},{6,0},{7,1},{8,14},{9,15},{10,... | collective-permute-start | bytes 112904 | tf_op jit(solution)/shard_map/ppermute | solution.py:298
  13.2 5.9 %collective-permute-start.3 = (bf16[4,12,1568]{2,1,0:T(8,128)(2,1)S(1)}, bf16[4,12,1568]{2,1,0:T(8,128)(2,1)S(1)}, u32[]{:S(2)}, u32[]{:S(2)}) collective-permute-start(bf16[4,12,1568]{2,1,0:T(8,128)(2,1)S(1)} %maximum_select_fusion.3), channel_id=1, source_target_pairs={{0,1},{1,0},{2,3},{3,2},{4,5},{5,4},{6,7},{7,6},{8,9},{9,8},{10,11... | collective-permute-start | bytes 451592 | tf_op jit(solution)/shard_map/ppermute | solution.py:298
  19.3 9.9 %collective-permute-start.4 = (bf16[4,24,1568]{2,1,0:T(8,128)(2,1)S(1)}, bf16[4,24,1568]{2,1,0:T(8,128)(2,1)S(1)}, u32[]{:S(2)}, u32[]{:S(2)}) collective-permute-start(bf16[4,24,1568]{2,1,0:T(8,128)(2,1)S(1)} %maximum_select_fusion.2), channel_id=1, source_target_pairs={{0,16},{8,24},{16,0},{24,8},{1,17},{9,25},{17,1},{25,9},{2,18},{10... | collective-permute-start | bytes 903176 | tf_op jit(solution)/shard_map/ppermute | solution.py:298
  20.9 1.1 copy-start.6
  22.0 0.7 copy-start.17
  25.4 9.9 %copy-start.14 = (s32[1,1024]{1,0:T(1,128)}, s32[1,1024]{1,0:T(1,128)S(1)}, u32[]{:S(2)}) copy-start(s32[1,1024]{1,0:T(1,128)S(1)} %get-tuple-element.63.dest_ref) | copy-start | bytes 12292
  25.4 3.8 %copy-start.22 = (f32[10380]{0:T(1024)S(1)}, f32[10380]{0:T(1024)}, u32[]{:S(2)}) copy-start(f32[10380]{0:T(1024)} %param.28) | copy-start | bytes 124564
  25.4 4.3 %slice-start = ((f32[10380]{0:T(1024)}), f32[2688]{0:T(1024)S(1)}, s32[]{:S(2)}) async-start(f32[10380]{0:T(1024)} %param.28), calls=%async_computation.5 | async-start | bytes 24576 | tf_op jit(solution)/shard_map/slice | solution.py:1340
  25.4 4.8 %copy-start.23 = (f32[256,2]{1,0:T(8,128)S(1)}, f32[256,2]{1,0:T(8,128)}, u32[]{:S(2)}) copy-start(f32[256,2]{1,0:T(8,128)} %constant.144.clone.coords_ref) | copy-start | bytes 6148
  25.5 29.7 %all-to-all-start = ((bf16[32,40,384]{2,1,0:T(8,128)(2,1)}), bf16[32,40,384]{2,1,0:T(8,128)(2,1)}, u32[]{:S(2)}, u32[]{:S(2)}) async-start(bf16[32,40,384]{2,1,0:T(8,128)(2,1)} %bitcast.14), calls=%async_computation | async-start | bytes 1966080 | tf_op jit(solution)/shard_map/all_to_all | solution.py:285
  29.8 5.6 %copy-start.16 = (f32[3,1,256]{2,1,0:T(1,128)}, f32[3,1,256]{2,1,0:T(1,128)S(1)}, u32[]{:S(2)}) copy-start(f32[3,1,256]{2,1,0:T(1,128)S(1)} %broadcast_in_dim.7.scale_ref) | copy-start | bytes 9220
  29.8 5.6 %copy-start.13 = (f32[7,384]{1,0:T(8,128)}, f32[7,384]{1,0:T(8,128)S(1)}, u32[]{:S(2)}) copy-start(f32[7,384]{1,0:T(8,128)S(1)} %reshape.285.rows_ref) | copy-start | bytes 32260
  30.1 3.6 %collective-permute-start.5 = (bf16[2,4,24,1568]{3,2,1,0:T(8,128)(2,1)S(1)}, bf16[2,4,24,1568]{3,2,1,0:T(8,128)(2,1)}, u32[]{:S(2)}, u32[]{:S(2)}) collective-permute-start(bf16[2,4,24,1568]{3,2,1,0:T(8,128)(2,1)S(1)} %maximum_select_fusion.1), channel_id=1, source_target_pairs={{0,8},{8,0},{16,24},{24,16},{1,9},{9,1},{17,25},{25,17},{2,10},{10... | collective-permute-start | bytes 1806344 | tf_op jit(solution)/shard_map/ppermute | solution.py:298
  31.5 3.7 %copy-start.26 = (f32[12,256]{1,0:T(8,128)}, f32[12,256]{1,0:T(8,128)S(1)}, u32[]{:S(2)}) copy-start(f32[12,256]{1,0:T(8,128)S(1)} %fusion.10.table_ref) | copy-start | bytes 36868
  33.6 1.8 copy-start.7
  35.4 28.1 %copy-start = (bf16[2,2,4,24,1568]{4,3,2,1,0:T(8,128)(2,1)}, bf16[2,2,4,24,1568]{4,3,2,1,0:T(8,128)(2,1)S(1)}, u32[]{:S(2)}) copy-start(bf16[2,2,4,24,1568]{4,3,2,1,0:T(8,128)(2,1)S(1)} %copy.42) | copy-start | bytes 3612676
  35.4 23.3 %copy-start.30 = (f32[1,1920]{1,0:T(1,128)S(1)}, f32[1,1920]{1,0:T(1,128)}, u32[]{:S(2)}) copy-start(f32[1,1920]{1,0:T(1,128)} %param.37) | copy-start | bytes 23044
  45.9 1.2 copy-start.3
  47.1 0.9 copy-start.9
  55.1 29.6 %all-to-all-start.1 = ((bf16[32,40,384]{2,1,0:T(8,128)(2,1)}), bf16[32,40,384]{2,1,0:T(8,128)(2,1)}, u32[]{:S(2)}, u32[]{:S(2)}) async-start(bf16[32,40,384]{2,1,0:T(8,128)(2,1)} %bitcast.16), calls=%async_computation.1 | async-start | bytes 1966080 | tf_op jit(solution)/shard_map/all_to_all | solution.py:285
  59.3 3.0 %copy-start.19 = (f32[1,1536,384]{2,1,0:T(8,128)S(1)}, f32[1,1536,384]{2,1,0:T(8,128)}, u32[]{:S(2)}) copy-start(f32[1,1536,384]{2,1,0:T(8,128)} %param.34) | copy-start | bytes 7077892
  62.3 1.4 slice-start.1
  100.0 28.8 %all-to-all-start.2 = ((bf16[32,40,384]{2,1,0:T(8,128)(2,1)}), bf16[32,40,384]{2,1,0:T(8,128)(2,1)S(1)}, u32[]{:S(2)}, u32[]{:S(2)}) async-start(bf16[32,40,384]{2,1,0:T(8,128)(2,1)} %bitcast.75), calls=%async_computation.2 | async-start | bytes 1966080 | tf_op jit(solution)/shard_map/all_to_all | solution.py:285
  102.9 11.4 %copy-start.20 = (f32[1,1536,384]{2,1,0:T(8,128)S(1)}, f32[1,1536,384]{2,1,0:T(8,128)}, u32[]{:S(2)}) copy-start(f32[1,1536,384]{2,1,0:T(8,128)} %param.34) | copy-start | bytes 7077892
  102.9 11.4 %copy-start.35 = (f32[1,1536,384]{2,1,0:T(8,128)S(1)}, f32[1,1536,384]{2,1,0:T(8,128)}, u32[]{:S(2)}) copy-start(f32[1,1536,384]{2,1,0:T(8,128)} %param.35) | copy-start | bytes 7077892
  102.9 11.4 %copy-start.36 = (f32[1,1536,384]{2,1,0:T(8,128)S(1)}, f32[1,1536,384]{2,1,0:T(8,128)}, u32[]{:S(2)}) copy-start(f32[1,1536,384]{2,1,0:T(8,128)} %param.36) | copy-start | bytes 7077892
  102.9 11.4 %copy-start.37 = (bf16[1280,1536]{1,0:T(8,128)(2,1)S(1)}, bf16[1280,1536]{1,0:T(8,128)(2,1)}, u32[]{:S(2)}) copy-start(bf16[1280,1536]{1,0:T(8,128)(2,1)} %get-tuple-element.75) | copy-start | bytes 11796484
  102.9 11.4 %copy-start.38 = (bf16[1280,384]{1,0:T(8,128)(2,1)S(1)}, bf16[1280,384]{1,0:T(8,128)(2,1)}, u32[]{:S(2)}) copy-start(bf16[1280,384]{1,0:T(8,128)(2,1)} %get-tuple-element.76) | copy-start | bytes 2949124
  128.8 3.8 %copy-start.18 = (bf16[32,40,384]{2,1,0:T(8,128)(2,1)}, bf16[32,40,384]{2,1,0:T(8,128)(2,1)S(1)}, u32[]{:S(2)}) copy-start(bf16[32,40,384]{2,1,0:T(8,128)(2,1)S(1)} %all-to-all-done.2) | copy-start | bytes 2949124
  128.8 28.8 %all-to-all-start.3 = ((bf16[32,40,384]{2,1,0:T(8,128)(2,1)}), bf16[32,40,384]{2,1,0:T(8,128)(2,1)S(1)}, u32[]{:S(2)}, u32[]{:S(2)}) async-start(bf16[32,40,384]{2,1,0:T(8,128)(2,1)} %bitcast.74), calls=%async_computation.3 | async-start | bytes 1966080 | tf_op jit(solution)/shard_map/all_to_all | solution.py:285
  132.6 15.9 %copy-start.8 = (bf16[1024,384]{1,0:T(8,128)(2,1)S(1)}, bf16[1024,384]{1,0:T(8,128)(2,1)}, u32[]{:S(2)}) copy-start(bf16[1024,384]{1,0:T(8,128)(2,1)} %tokens_ref.3) | copy-start | bytes 2359300
  132.6 15.9 %copy-start.12 = (f32[8,384]{1,0:T(8,128)S(1)}, f32[8,384]{1,0:T(8,128)}, u32[]{:S(2)}) copy-start(f32[8,384]{1,0:T(8,128)} %get-tuple-element.82.expert_ref) | copy-start | bytes 36868
  148.5 1.1 copy-start.10
  149.7 1.1 copy-start.11
  150.8 3.5 %copy-start.27 = (f32[32,512]{1,0:T(8,128)S(1)}, f32[32,512]{1,0:T(8,128)}, u32[]{:S(2)}) copy-start(f32[32,512]{1,0:T(8,128)} %get-tuple-element.87) | copy-start | bytes 196612
  154.2 18.0 %copy-start.31 = (f32[1,1920]{1,0:T(1,128)S(1)}, f32[1,1920]{1,0:T(1,128)}, u32[]{:S(2)}) copy-start(f32[1,1920]{1,0:T(1,128)} %param.37) | copy-start | bytes 23044
  154.2 18.0 %copy-start.32 = (f32[1,1920]{1,0:T(1,128)S(1)}, f32[1,1920]{1,0:T(1,128)}, u32[]{:S(2)}) copy-start(f32[1,1920]{1,0:T(1,128)} %param.38) | copy-start | bytes 23044
  154.2 18.0 %copy-start.33 = (f32[1,1920]{1,0:T(1,128)S(1)}, f32[1,1920]{1,0:T(1,128)}, u32[]{:S(2)}) copy-start(f32[1,1920]{1,0:T(1,128)} %param.39) | copy-start | bytes 23044
  154.2 17.9 %copy-start.34 = (f32[1,1536]{1,0:T(1,128)S(1)}, f32[1,1536]{1,0:T(1,128)}, u32[]{:S(2)}) copy-start(f32[1,1536]{1,0:T(1,128)} %get-tuple-element.102) | copy-start | bytes 18436
  154.2 2.3 %collective-permute-start.6 = (bf16[16,24,896]{2,1,0:T(8,128)(2,1)S(1)}, bf16[16,24,896]{2,1,0:T(8,128)(2,1)S(1)}, u32[]{:S(2)}, u32[]{:S(2)}) collective-permute-start(bf16[16,24,896]{2,1,0:T(8,128)(2,1)S(1)} %get-tuple-element.86), channel_id=1, source_target_pairs={{0,8},{8,0},{16,24},{24,16},{1,9},{9,1},{17,25},{25,17},{2,10},{10... | collective-permute-start | bytes 2064392 | tf_op jit(solution)/shard_map/ppermute | solution.py:298
  154.3 18.5 %copy-start.1 = (bf16[2,2,4,24,1568]{4,3,2,1,0:T(8,128)(2,1)S(1)}, bf16[2,2,4,24,1568]{4,3,2,1,0:T(8,128)(2,1)}, u32[]{:S(2)}) copy-start(bf16[2,2,4,24,1568]{4,3,2,1,0:T(8,128)(2,1)} %copy-done) | copy-start | bytes 3612676
  154.3 2.2 %collective-permute-start.7 = (f32[32,512]{1,0:T(8,128)S(1)}, f32[32,512]{1,0:T(8,128)S(1)}, u32[]{:S(2)}, u32[]{:S(2)}) collective-permute-start(f32[32,512]{1,0:T(8,128)S(1)} %copy-done.27), channel_id=1, source_target_pairs={{0,8},{1,9},{2,10},{3,11},{4,12},{5,13},{6,14},{7,15},{8,0},{9,1},... | collective-permute-start | bytes 196616 | tf_op jit(solution)/shard_map/ppermute | solution.py:379
  157.7 10.8 %collective-permute-start.10 = (f32[32,512]{1,0:T(8,128)S(1)}, f32[32,512]{1,0:T(8,128)S(1)}, u32[]{:S(2)}, u32[]{:S(2)}) collective-permute-start(f32[32,512]{1,0:T(8,128)S(1)} %add.206), channel_id=1, source_target_pairs={{0,6},{1,7},{2,4},{3,5},{4,2},{5,3},{6,0},{7,1},{8,14},{9,15},{10,... | collective-permute-start | bytes 196616 | tf_op jit(solution)/shard_map/ppermute | solution.py:379
  160.9 7.6 %collective-permute-start.9 = (f32[32,512]{1,0:T(8,128)S(1)}, f32[32,512]{1,0:T(8,128)S(1)}, u32[]{:S(2)}, u32[]{:S(2)}) collective-permute-start(f32[32,512]{1,0:T(8,128)S(1)} %add.206), channel_id=1, source_target_pairs={{0,4},{1,5},{2,6},{3,7},{4,0},{5,1},{6,2},{7,3},{8,12},{9,13},{10,... | collective-permute-start | bytes 196616 | tf_op jit(solution)/shard_map/ppermute | solution.py:379
  160.9 7.6 %collective-permute-start.8 = (f32[32,512]{1,0:T(8,128)S(1)}, f32[32,512]{1,0:T(8,128)S(1)}, u32[]{:S(2)}, u32[]{:S(2)}) collective-permute-start(f32[32,512]{1,0:T(8,128)S(1)} %add.206), channel_id=1, source_target_pairs={{0,2},{1,3},{2,0},{3,1},{4,6},{5,7},{6,4},{7,5},{8,10},{9,11},{10,... | collective-permute-start | bytes 196616 | tf_op jit(solution)/shard_map/ppermute | solution.py:379
  162.1 24.2 %all-to-all-start.4 = ((bf16[16,24,896]{2,1,0:T(8,128)(2,1)}), bf16[16,24,896]{2,1,0:T(8,128)(2,1)S(1)}, u32[]{:S(2)}, u32[]{:S(2)}) async-start(bf16[16,24,896]{2,1,0:T(8,128)(2,1)} %add_convert_fusion), calls=%async_computation.4 | async-start | bytes 1376256 | tf_op jit(solution)/shard_map/all_to_all | solution.py:396
  168.6 13.4 %collective-permute-start.13 = (f32[32,512]{1,0:T(8,128)S(1)}, f32[32,512]{1,0:T(8,128)S(1)}, u32[]{:S(2)}, u32[]{:S(2)}) collective-permute-start(f32[32,512]{1,0:T(8,128)S(1)} %add_add_fusion.1), channel_id=1, source_target_pairs={{0,17},{1,16},{2,19},{3,18},{4,21},{5,20},{6,23},{7,22},{8,25},{9,... | collective-permute-start | bytes 196616 | tf_op jit(solution)/shard_map/ppermute | solution.py:379
  171.5 10.5 %collective-permute-start.12 = (f32[32,512]{1,0:T(8,128)S(1)}, f32[32,512]{1,0:T(8,128)S(1)}, u32[]{:S(2)}, u32[]{:S(2)}) collective-permute-start(f32[32,512]{1,0:T(8,128)S(1)} %add_add_fusion.1), channel_id=1, source_target_pairs={{0,16},{1,17},{2,18},{3,19},{4,20},{5,21},{6,22},{7,23},{8,24},{9,... | collective-permute-start | bytes 196616 | tf_op jit(solution)/shard_map/ppermute | solution.py:379
  172.0 9.9 %collective-permute-start.11 = (f32[32,512]{1,0:T(8,128)S(1)}, f32[32,512]{1,0:T(8,128)S(1)}, u32[]{:S(2)}, u32[]{:S(2)}) collective-permute-start(f32[32,512]{1,0:T(8,128)S(1)} %add_add_fusion.1), channel_id=1, source_target_pairs={{0,1},{1,0},{2,3},{3,2},{4,5},{5,4},{6,7},{7,6},{8,9},{9,8},{10,11... | collective-permute-start | bytes 196616 | tf_op jit(solution)/shard_map/ppermute | solution.py:379
  172.8 1.7 copy-start.2
  174.5 1.4 copy-start.5
  175.9 2.9 %copy-start.4 = (f32[1024,384]{1,0:T(8,128)S(1)}, f32[1024,384]{1,0:T(8,128)}, u32[]{:S(2)}) copy-start(f32[1024,384]{1,0:T(8,128)} %copy-done.3) | copy-start | bytes 4718596
  175.9 2.9 %copy-start.15 = (s32[1,1024]{1,0:T(1,128)S(1)}, s32[1,1024]{1,0:T(1,128)}, u32[]{:S(2)}) copy-start(s32[1,1024]{1,0:T(1,128)} %copy-done.14) | copy-start | bytes 12292
  178.7 3.9 %copy-start.28 = (f32[10380]{0:T(1024)S(1)}, f32[10380]{0:T(1024)}, u32[]{:S(2)}) copy-start(f32[10380]{0:T(1024)} %param.29) | copy-start | bytes 124564
  178.7 3.9 %copy-start.29 = (f32[10380]{0:T(1024)S(1)}, f32[10380]{0:T(1024)}, u32[]{:S(2)}) copy-start(f32[10380]{0:T(1024)} %param.30) | copy-start | bytes 124564
  178.7 7.7 %copy-start.21 = (f32[12,1568]{1,0:T(8,128)S(1)}, f32[12,1568]{1,0:T(8,128)}, u32[]{:S(2)}) copy-start(f32[12,1568]{1,0:T(8,128)} %param.25) | copy-start | bytes 225796
  178.8 7.7 %copy-start.24 = (f32[12,1568]{1,0:T(8,128)S(1)}, f32[12,1568]{1,0:T(8,128)}, u32[]{:S(2)}) copy-start(f32[12,1568]{1,0:T(8,128)} %param.26) | copy-start | bytes 225796
  178.8 7.7 %copy-start.25 = (f32[12,1568]{1,0:T(8,128)S(1)}, f32[12,1568]{1,0:T(8,128)}, u32[]{:S(2)}) copy-start(f32[12,1568]{1,0:T(8,128)} %param.27) | copy-start | bytes 225796

commit v4 on v3

--- a/solution.py
+++ b/solution.py
@@ -589,7 +589,7 @@
 
 
 def token_block(tok_rows):
-    return math.gcd(tok_rows, 256)
+    return math.gcd(tok_rows, 512)
 
 
 def whole(shape):

time: 188 us -> 188 us (level)
  waiting for transfers between devices: 48.6 us -> 50.6 us
  transfers between devices with their start and end apart: 19 -> 19, of which waited for: 10 -> 10; matrix products, arithmetic and copies ran while one was open for 19% -> 19% of each run, Pallas kernels for 21% -> 20%
where the time goes in v4:
time: 188 us; the launch traced here: 187 us
  Pallas kernels  52.1 us (28%)
  waiting for transfers between devices  50.6 us (27%)
  starting transfers between devices  36.3 us (19%)
  matrix products  21.1 us (11%)
  other arithmetic  12.9 us (7%)
  local copies, waits for them, and re-layouts  12.2 us (6%)
  between operations  1.96 us (1%)
    all_to_all x4, waiting for transfers between devices, trade_rows(): lax.all_to_all(payload, ('wide', 'narrow'), split_axis=0, concat_axis=0,...  36.2 us
    dot_general x2, matrix products, dot_rows(): lax.dot_general(left, right, contract_rows, preferred_element_type=jnp.fl...  18.4 us
    pallas_call x1, Pallas kernels, call_back(): pl.pallas_call(back_kernel, grid=(count // block,), out_shape=(jax.ShapeD...  15.8 us
    pallas_call x1, Pallas kernels, call_expert(): pl.pallas_call(expert_kernel, grid=(count // block,), out_shape=(jax.Shap...  15.3 us
    all_to_all x4, starting transfers between devices, trade_rows(): lax.all_to_all(payload, ('wide', 'narrow'), split_axis=0, concat_axis=0,...  12.6 us
    pallas_call x1, Pallas kernels, call_front(): pl.pallas_call(front_kernel, grid=(count // block,), out_shape=(jax.Shape...  9.88 us
    unnamed x78, local copies, waits for them, and re-layouts  9.37 us
    ppermute x7, starting transfers between devices, swap(): lax.ppermute(value, axis, [(i, i ^ offset) for i in range(lax.axis_size(a...  8.94 us
  transfers between devices with their start and end apart: 19, of which 10 were waited for; matrix products, arithmetic and copies ran while one was open for 19% of the time, Pallas kernels for 20%

profile of v4, /device:TPU:0, one launch (start us, length us, event | category | flops | bytes accessed | tf_op | source)
XLA Modules:
  0.0 187.2 jit_solution(15156478304396821344)
XLA Ops:
  0.7 0.9 convert_element_type.30
  1.6 4.0 %collective-permute-start.2 = (bf16[12,1568]{1,0:T(8,128)(2,1)S(1)}, bf16[12,1568]{1,0:T(8,128)(2,1)S(1)}, u32[]{:S(2)}, u32[]{:S(2)}) collective-permute-start(bf16[12,1568]{1,0:T(8,128)(2,1)S(1)} %convert_element_type.30), channel_id=1, source_target_pairs={{0,4},{1,5},{2,6},{3,7},{4,0},{5,1},{6,2},{7,3},{8,12},{9,13},{10,... | collective-permute-start | bytes 112904 | tf_op jit(solution)/shard_map/ppermute | solution.py:298
  5.6 1.6 collective-permute-start.1
  7.2 1.2 collective-permute-done.2
  8.4 0.9 select_bitcast_fusion.2
  9.3 0.4 collective-permute-done.1
  9.7 3.4 %collective-permute-done = bf16[12,1568]{1,0:T(8,128)(2,1)S(1)} collective-permute-done((bf16[12,1568]{1,0:T(8,128)(2,1)S(1)}, bf16[12,1568]{1,0:T(8,128)(2,1)S(1)}, u32[]{:S(2)}, u32[]{:S(2)}) %collective-permute-start) | collective-permute-done | bytes 37664 | tf_op jit(solution)/shard_map/ppermute | solution.py:298
  13.2 1.6 collective-permute-start.3
  15.4 3.7 %collective-permute-done.3 = bf16[4,12,1568]{2,1,0:T(8,128)(2,1)S(1)} collective-permute-done((bf16[4,12,1568]{2,1,0:T(8,128)(2,1)S(1)}, bf16[4,12,1568]{2,1,0:T(8,128)(2,1)S(1)}, u32[]{:S(2)}, u32[]{:S(2)}) %collective-permute-start.3) | collective-permute-done | bytes 150560 | tf_op jit(solution)/shard_map/ppermute | solution.py:298
  19.1 0.2 maximum_select_fusion.2
  19.3 1.6 collective-permute-start.4
  20.9 1.1 copy-done.6
  22.0 0.7 copy-done.17
  22.7 2.8 %assign.1 = (s32[1,1024]{1,0:T(1,128)S(1)}, bf16[1280,384]{1,0:T(8,128)(2,1)}) custom-call(s32[1]{0:T(128)S(6)} %copy.48.count_ref, s32[1,1024]{1,0:T(1,128)S(1)} %bitcast.69, bf16[1024,384]{1,0:T(8,128)(2,1)S(1)} %copy-done.6), custom_call_target="tpu_custom_call" | custom-call | flops 1006632960 | bytes 4000000 | tf_op jit(solution)/shard_map/assign/pallas_call | solution.py:498
  25.5 3.5 %all-to-all-start = ((bf16[32,40,384]{2,1,0:T(8,128)(2,1)}), bf16[32,40,384]{2,1,0:T(8,128)(2,1)}, u32[]{:S(2)}, u32[]{:S(2)}) async-start(bf16[32,40,384]{2,1,0:T(8,128)(2,1)} %bitcast.14), calls=%async_computation | async-start | bytes 1966080 | tf_op jit(solution)/shard_map/all_to_all | solution.py:285
  29.8 0.3 reshape.286
  30.2 0.7 fusion.17
  31.0 0.6 fusion.10.table_ref
  31.5 1.4 fusion
  32.9 0.2 reshape.288
  33.1 0.3 copy.47
  33.4 0.3 reshape.289.bias_ref
  33.7 1.6 maximum_select_fusion
  35.4 9.9 %front.1 = (bf16[1280,384]{1,0:T(8,128)(2,1)}, f32[1024,384]{1,0:T(8,128)S(1)}, f32[1024,384]{1,0:T(8,128)}, bf16[1024,384]{1,0:T(8,128)(2,1)S(1)}, f32[1024,768...) custom-call(s32[1,1024]{1,0:T(1,128)S(1)} %get-tuple-element.63.dest_ref, ...), custom_call_target="tpu_custom_call" | custom-call | flops 2415919104 | bytes 20000000 | tf_op jit(solution)/shard_map/front/pallas_call | solution.py:609
  45.3 1.2 copy-done.3
  46.5 0.9 copy-done.9
  47.4 7.8 %all-to-all-done = bf16[32,40,384]{2,1,0:T(8,128)(2,1)} async-done(((bf16[32,40,384]{2,1,0:T(8,128)(2,1)}), bf16[32,40,384]{2,1,0:T(8,128)(2,1)}, u32[]{:S(2)}, u32[]{:S(2)}) %all-to-all-start) | async-done | bytes 983072 | tf_op jit(solution)/shard_map/all_to_all | solution.py:285
  55.1 3.6 %all-to-all-start.1 = ((bf16[32,40,384]{2,1,0:T(8,128)(2,1)}), bf16[32,40,384]{2,1,0:T(8,128)(2,1)}, u32[]{:S(2)}, u32[]{:S(2)}) async-start(bf16[32,40,384]{2,1,0:T(8,128)(2,1)} %bitcast.16), calls=%async_computation.1 | async-start | bytes 1966080 | tf_op jit(solution)/shard_map/all_to_all | solution.py:285
  58.7 0.6 slice.76.bias_one_ref
  59.3 3.0 %convert_bitcast_fusion.1.first_ref = bf16[384,1536]{1,0:T(8,128)(2,1)} fusion(f32[1,384,1536]{2,1,0:T(8,128)} %param.31), kind=kLoop, calls=%fused_computation.19 | loop fusion | flops 589824 | bytes 3538944 | tf_op jit(solution)/shard_map/convert_element_type | solution.py:1349
  62.3 1.1 convert_bitcast_fusion.second_ref
  63.4 0.2 convert_reduce_fusion.1
  63.6 0.6 pad_maximum_fusion.3.vecs_ref
  64.2 20.4 %all-to-all-done.1 = bf16[32,40,384]{2,1,0:T(8,128)(2,1)} async-done(((bf16[32,40,384]{2,1,0:T(8,128)(2,1)}), bf16[32,40,384]{2,1,0:T(8,128)(2,1)}, u32[]{:S(2)}, u32[]{:S(2)}) %all-to-all-start.1) | async-done | bytes 983072 | tf_op jit(solution)/shard_map/all_to_all | solution.py:285
  84.7 15.3 %expert.1 = (bf16[1280,384]{1,0:T(8,128)(2,1)}, bf16[1280,384]{1,0:T(8,128)(2,1)}, bf16[1280,1536]{1,0:T(8,128)(2,1)}, bf16[1280,1536]{1,0:T(8,128)(2,1)}, bf16[...) custom-call(bf16[1280,384]{1,0:T(8,128)(2,1)} %bitcast.17.rows_ref, bf16[1280,384]{1,0:T(8,128)(2,1)} %bitcast.15.cot_ref, ...), custom_call_target="tpu_custom_call" | custom-call | flops 6039797760 | bytes 16000000 | tf_op jit(solution)/shard_map/expert/pallas_call | solution.py:1062
  100.0 2.7 %all-to-all-start.2 = ((bf16[32,40,384]{2,1,0:T(8,128)(2,1)}), bf16[32,40,384]{2,1,0:T(8,128)(2,1)S(1)}, u32[]{:S(2)}, u32[]{:S(2)}) async-start(bf16[32,40,384]{2,1,0:T(8,128)(2,1)} %bitcast.75), calls=%async_computation.2 | async-start | bytes 1966080 | tf_op jit(solution)/shard_map/all_to_all | solution.py:285
  102.7 11.3 %fusion.29 = (bf16[1,384,1536]{2,1,0:T(8,128)(2,1)}, f32[1,384,1536]{2,1,0:T(8,128)}, f32[1,384,1536]{2,1,0:T(8,128)}, f32[1,384,1536]{2,1,0:T(8,128)}) fusion(f32[1,384,1536]{2,1,0:T(8,128)} %param.31, f32[1,384,1536]{2,1,0:T(8,128)} %param.32, f32[1,384,1536]{2,1,0:T(8,128)} %param.33, bf16[1280,384]{1,0:T(8,128)(2,1)} %bitcast.17.rows_ref, ...), kind=kOutput, calls=%fused_computation.74 | convolution fusion | flops 1519386624 | bytes 20250624 | tf_op jit(solution)/shard_map/dot_general | solution.py:414
  114.1 7.1 %fusion.27 = (bf16[1,1536,384]{2,1,0:T(8,128)(2,1)}, f32[1,1536,384]{2,1,0:T(8,128)}, f32[1,1536,384]{2,1,0:T(8,128)}, f32[1,1536,384]{2,1,0:T(8,128)}) fusion(f32[1,1536,384]{2,1,0:T(8,128)S(1)} %copy-done.20, f32[1,1536,384]{2,1,0:T(8,128)S(1)} %copy-done.35, f32[1,1536,384]{2,1,0:T(8,128)S(1)} %copy-done.36, bf16[1280,1536]{1,0:T(8,128)(2,1)S(1)} %copy-done.37, ...), kind=kOutput, calls=%fused_computation.73 | convolution fusion | flops 1519386624 | bytes 20250624 | tf_op jit(solution)/shard_map/dot_general | solution.py:414
  121.2 7.7 %all-to-all-done.2 = bf16[32,40,384]{2,1,0:T(8,128)(2,1)S(1)} async-done(((bf16[32,40,384]{2,1,0:T(8,128)(2,1)}), bf16[32,40,384]{2,1,0:T(8,128)(2,1)S(1)}, u32[]{:S(2)}, u32[]{:S(2)}) %all-to-all-start.2) | async-done | bytes 983072 | tf_op jit(solution)/shard_map/all_to_all | solution.py:285
  128.8 2.9 %all-to-all-start.3 = ((bf16[32,40,384]{2,1,0:T(8,128)(2,1)}), bf16[32,40,384]{2,1,0:T(8,128)(2,1)S(1)}, u32[]{:S(2)}, u32[]{:S(2)}) async-start(bf16[32,40,384]{2,1,0:T(8,128)(2,1)} %bitcast.74), calls=%async_computation.3 | async-start | bytes 1966080 | tf_op jit(solution)/shard_map/all_to_all | solution.py:285
  131.9 0.6 pad_maximum_fusion.1.net_ref
  132.6 15.8 %back.1 = (f32[1024,384]{1,0:T(8,128)}, bf16[1024,384]{1,0:T(8,128)(2,1)}, bf16[1024,1152]{1,0:T(8,128)(2,1)}, f32[32,512]{1,0:T(8,128)}) custom-call(s32[1]{0:T(128)S(6)} %copy.48.count_ref, s32[1,1024]{1,0:T(1,128)} %copy-done.14, bf16[1280,384]{1,0:T(8,128)(2,1)} %bitcast.70, bf16[1024,384]{1,0:T(8,128)(2,1)} %cot_ref.2, bf16[384,1568]{1,0:T(8,128)(2,1)} %bitcast.66, ...), custom_call_target="tpu_custom_call" | custom-call | flops 3019898880 | bytes 20000000 | tf_op jit(solution)/shard_map/back/pallas_call | solution.py:821
  148.4 1.1 copy-done.10
  149.6 1.1 copy-done.11
  150.7 3.3 %dense.1 = (bf16[16,24,896]{2,1,0:T(8,128)(2,1)S(1)}, f32[16,24,896]{2,1,0:T(8,128)S(1)}) custom-call(s32[2]{0:T(128)S(1)} %pad_add_fusion.place_ref, bf16[1024,384]{1,0:T(8,128)(2,1)S(1)} %copy-done.8, bf16[1024,384]{1,0:T(8,128)(2,1)S(1)} %copy-done.10, bf16[1024,384]{1,0:T(8,128)(2,1)S(1)} %copy-done.11, ...), custom_call_target="tpu_custom_call" | custom-call | flops 1207959552 | bytes 7000000 | tf_op jit(solution)/shard_map/dense/pallas_call | solution.py:911
  154.2 0.5 collective-permute-start.7
  154.7 1.7 collective-permute-done.7
  156.4 1.0 add_convert_fusion
  157.4 0.3 all-to-all-done.3
  157.7 3.1 %collective-permute-start.10 = (f32[32,512]{1,0:T(8,128)S(1)}, f32[32,512]{1,0:T(8,128)S(1)}, u32[]{:S(2)}, u32[]{:S(2)}) collective-permute-start(f32[32,512]{1,0:T(8,128)S(1)} %add.206), channel_id=1, source_target_pairs={{0,6},{1,7},{2,4},{3,5},{4,2},{5,3},{6,0},{7,1},{8,14},{9,15},{10,... | collective-permute-start | bytes 196616 | tf_op jit(solution)/shard_map/ppermute | solution.py:379
  160.8 1.3 collective-permute-start.8
  162.1 6.4 %all-to-all-start.4 = ((bf16[16,24,896]{2,1,0:T(8,128)(2,1)}), bf16[16,24,896]{2,1,0:T(8,128)(2,1)S(1)}, u32[]{:S(2)}, u32[]{:S(2)}) async-start(bf16[16,24,896]{2,1,0:T(8,128)(2,1)} %add_convert_fusion), calls=%async_computation.4 | async-start | bytes 1376256 | tf_op jit(solution)/shard_map/all_to_all | solution.py:396
  168.5 2.9 %collective-permute-start.13 = (f32[32,512]{1,0:T(8,128)S(1)}, f32[32,512]{1,0:T(8,128)S(1)}, u32[]{:S(2)}, u32[]{:S(2)}) collective-permute-start(f32[32,512]{1,0:T(8,128)S(1)} %add_add_fusion.1), channel_id=1, source_target_pairs={{0,17},{1,16},{2,19},{3,18},{4,21},{5,20},{6,23},{7,22},{8,25},{9,... | collective-permute-start | bytes 196616 | tf_op jit(solution)/shard_map/ppermute | solution.py:379
  171.4 0.6 collective-permute-start.12
  172.1 0.7 multiply_subtract_fusion.4
  172.7 1.7 copy-done.2
  174.4 1.4 copy-done.5
  175.8 2.4 %inputs.1 = bf16[1024,384]{1,0:T(8,128)(2,1)} custom-call(f32[1024,384]{1,0:T(8,128)S(1)} %copy-done.5, bf16[1024,1152]{1,0:T(8,128)(2,1)S(1)} %copy-done.2, bf16[384,1568]{1,0:T(8,128)(2,1)S(1)} %bitcast.67), custom_call_target="tpu_custom_call" | custom-call | tf_op jit(solution)/shard_map/inputs/pallas_call | solution.py:938
  178.2 2.6 %layer.1 = bf16[1024,384]{1,0:T(8,128)(2,1)} custom-call(s32[1]{0:T(128)S(6)} %copy.48.count_ref, s32[1,1024]{1,0:T(1,128)S(1)} %copy-done.15, bf16[1280,384]{1,0:T(8,128)(2,1)S(1)} %bitcast.68, f32[1024,384]{1,0:T(8,128)S(1)} %copy-done.4), custom_call_target="tpu_custom_call" | custom-call | tf_op jit(solution)/shard_map/layer/pallas_call | solution.py:967
  181.0 0.1 copy.45
  181.1 0.2 reshape.303
  181.6 0.7 multiply_subtract_fusion.3
  182.2 4.0 %all-to-all-done.4 = bf16[16,24,896]{2,1,0:T(8,128)(2,1)S(1)} async-done(((bf16[16,24,896]{2,1,0:T(8,128)(2,1)}), bf16[16,24,896]{2,1,0:T(8,128)(2,1)S(1)}, u32[]{:S(2)}, u32[]{:S(2)}) %all-to-all-start.4) | async-done | bytes 688160 | tf_op jit(solution)/shard_map/all_to_all | solution.py:396
  186.4 0.8 multiply_subtract_fusion.2
  (126 shorter events, 2.1 us)
Async XLA Ops:
  1.6 6.8 %collective-permute-start.2 = (bf16[12,1568]{1,0:T(8,128)(2,1)S(1)}, bf16[12,1568]{1,0:T(8,128)(2,1)S(1)}, u32[]{:S(2)}, u32[]{:S(2)}) collective-permute-start(bf16[12,1568]{1,0:T(8,128)(2,1)S(1)} %convert_element_type.30), channel_id=1, source_target_pairs={{0,4},{1,5},{2,6},{3,7},{4,0},{5,1},{6,2},{7,3},{8,12},{9,13},{10,... | collective-permute-start | bytes 112904 | tf_op jit(solution)/shard_map/ppermute | solution.py:298
  5.6 4.1 %collective-permute-start.1 = (bf16[12,1568]{1,0:T(8,128)(2,1)S(1)}, bf16[12,1568]{1,0:T(8,128)(2,1)S(1)}, u32[]{:S(2)}, u32[]{:S(2)}) collective-permute-start(bf16[12,1568]{1,0:T(8,128)(2,1)S(1)} %convert_element_type.30), channel_id=1, source_target_pairs={{0,2},{1,3},{2,0},{3,1},{4,6},{5,7},{6,4},{7,5},{8,10},{9,11},{10,... | collective-permute-start | bytes 112904 | tf_op jit(solution)/shard_map/ppermute | solution.py:298
  7.2 5.9 %collective-permute-start = (bf16[12,1568]{1,0:T(8,128)(2,1)S(1)}, bf16[12,1568]{1,0:T(8,128)(2,1)S(1)}, u32[]{:S(2)}, u32[]{:S(2)}) collective-permute-start(bf16[12,1568]{1,0:T(8,128)(2,1)S(1)} %convert_element_type.30), channel_id=1, source_target_pairs={{0,6},{1,7},{2,4},{3,5},{4,2},{5,3},{6,0},{7,1},{8,14},{9,15},{10,... | collective-permute-start | bytes 112904 | tf_op jit(solution)/shard_map/ppermute | solution.py:298
  13.2 5.9 %collective-permute-start.3 = (bf16[4,12,1568]{2,1,0:T(8,128)(2,1)S(1)}, bf16[4,12,1568]{2,1,0:T(8,128)(2,1)S(1)}, u32[]{:S(2)}, u32[]{:S(2)}) collective-permute-start(bf16[4,12,1568]{2,1,0:T(8,128)(2,1)S(1)} %maximum_select_fusion.3), channel_id=1, source_target_pairs={{0,1},{1,0},{2,3},{3,2},{4,5},{5,4},{6,7},{7,6},{8,9},{9,8},{10,11... | collective-permute-start | bytes 451592 | tf_op jit(solution)/shard_map/ppermute | solution.py:298
  19.3 9.9 %collective-permute-start.4 = (bf16[4,24,1568]{2,1,0:T(8,128)(2,1)S(1)}, bf16[4,24,1568]{2,1,0:T(8,128)(2,1)S(1)}, u32[]{:S(2)}, u32[]{:S(2)}) collective-permute-start(bf16[4,24,1568]{2,1,0:T(8,128)(2,1)S(1)} %maximum_select_fusion.2), channel_id=1, source_target_pairs={{0,16},{8,24},{16,0},{24,8},{1,17},{9,25},{17,1},{25,9},{2,18},{10... | collective-permute-start | bytes 903176 | tf_op jit(solution)/shard_map/ppermute | solution.py:298
  20.9 1.1 copy-start.6
  22.0 0.7 copy-start.17
  25.4 9.9 %copy-start.14 = (s32[1,1024]{1,0:T(1,128)}, s32[1,1024]{1,0:T(1,128)S(1)}, u32[]{:S(2)}) copy-start(s32[1,1024]{1,0:T(1,128)S(1)} %get-tuple-element.63.dest_ref) | copy-start | bytes 12292
  25.4 3.8 %copy-start.22 = (f32[10380]{0:T(1024)S(1)}, f32[10380]{0:T(1024)}, u32[]{:S(2)}) copy-start(f32[10380]{0:T(1024)} %param.28) | copy-start | bytes 124564
  25.4 4.3 %slice-start = ((f32[10380]{0:T(1024)}), f32[2688]{0:T(1024)S(1)}, s32[]{:S(2)}) async-start(f32[10380]{0:T(1024)} %param.28), calls=%async_computation.5 | async-start | bytes 24576 | tf_op jit(solution)/shard_map/slice | solution.py:1340
  25.4 4.8 %copy-start.23 = (f32[256,2]{1,0:T(8,128)S(1)}, f32[256,2]{1,0:T(8,128)}, u32[]{:S(2)}) copy-start(f32[256,2]{1,0:T(8,128)} %constant.144.clone.coords_ref) | copy-start | bytes 6148
  25.5 29.7 %all-to-all-start = ((bf16[32,40,384]{2,1,0:T(8,128)(2,1)}), bf16[32,40,384]{2,1,0:T(8,128)(2,1)}, u32[]{:S(2)}, u32[]{:S(2)}) async-start(bf16[32,40,384]{2,1,0:T(8,128)(2,1)} %bitcast.14), calls=%async_computation | async-start | bytes 1966080 | tf_op jit(solution)/shard_map/all_to_all | solution.py:285
  29.8 5.6 %copy-start.16 = (f32[3,1,256]{2,1,0:T(1,128)}, f32[3,1,256]{2,1,0:T(1,128)S(1)}, u32[]{:S(2)}) copy-start(f32[3,1,256]{2,1,0:T(1,128)S(1)} %broadcast_in_dim.7.scale_ref) | copy-start | bytes 9220
  29.8 5.6 %copy-start.13 = (f32[7,384]{1,0:T(8,128)}, f32[7,384]{1,0:T(8,128)S(1)}, u32[]{:S(2)}) copy-start(f32[7,384]{1,0:T(8,128)S(1)} %reshape.285.rows_ref) | copy-start | bytes 32260
  30.1 3.6 %collective-permute-start.5 = (bf16[2,4,24,1568]{3,2,1,0:T(8,128)(2,1)S(1)}, bf16[2,4,24,1568]{3,2,1,0:T(8,128)(2,1)}, u32[]{:S(2)}, u32[]{:S(2)}) collective-permute-start(bf16[2,4,24,1568]{3,2,1,0:T(8,128)(2,1)S(1)} %maximum_select_fusion.1), channel_id=1, source_target_pairs={{0,8},{8,0},{16,24},{24,16},{1,9},{9,1},{17,25},{25,17},{2,10},{10... | collective-permute-start | bytes 1806344 | tf_op jit(solution)/shard_map/ppermute | solution.py:298
  31.5 3.7 %copy-start.26 = (f32[12,256]{1,0:T(8,128)}, f32[12,256]{1,0:T(8,128)S(1)}, u32[]{:S(2)}) copy-start(f32[12,256]{1,0:T(8,128)S(1)} %fusion.10.table_ref) | copy-start | bytes 36868
  33.6 1.8 copy-start.7
  35.4 28.1 %copy-start = (bf16[2,2,4,24,1568]{4,3,2,1,0:T(8,128)(2,1)}, bf16[2,2,4,24,1568]{4,3,2,1,0:T(8,128)(2,1)S(1)}, u32[]{:S(2)}) copy-start(bf16[2,2,4,24,1568]{4,3,2,1,0:T(8,128)(2,1)S(1)} %copy.42) | copy-start | bytes 3612676
  35.4 23.3 %copy-start.30 = (f32[1,1920]{1,0:T(1,128)S(1)}, f32[1,1920]{1,0:T(1,128)}, u32[]{:S(2)}) copy-start(f32[1,1920]{1,0:T(1,128)} %param.37) | copy-start | bytes 23044
  45.3 1.2 copy-start.3
  46.5 0.9 copy-start.9
  55.1 29.6 %all-to-all-start.1 = ((bf16[32,40,384]{2,1,0:T(8,128)(2,1)}), bf16[32,40,384]{2,1,0:T(8,128)(2,1)}, u32[]{:S(2)}, u32[]{:S(2)}) async-start(bf16[32,40,384]{2,1,0:T(8,128)(2,1)} %bitcast.16), calls=%async_computation.1 | async-start | bytes 1966080 | tf_op jit(solution)/shard_map/all_to_all | solution.py:285
  59.3 3.0 %copy-start.19 = (f32[1,1536,384]{2,1,0:T(8,128)S(1)}, f32[1,1536,384]{2,1,0:T(8,128)}, u32[]{:S(2)}) copy-start(f32[1,1536,384]{2,1,0:T(8,128)} %param.34) | copy-start | bytes 7077892
  62.3 1.4 slice-start.1
  100.0 28.8 %all-to-all-start.2 = ((bf16[32,40,384]{2,1,0:T(8,128)(2,1)}), bf16[32,40,384]{2,1,0:T(8,128)(2,1)S(1)}, u32[]{:S(2)}, u32[]{:S(2)}) async-start(bf16[32,40,384]{2,1,0:T(8,128)(2,1)} %bitcast.75), calls=%async_computation.2 | async-start | bytes 1966080 | tf_op jit(solution)/shard_map/all_to_all | solution.py:285
  102.7 11.4 %copy-start.20 = (f32[1,1536,384]{2,1,0:T(8,128)S(1)}, f32[1,1536,384]{2,1,0:T(8,128)}, u32[]{:S(2)}) copy-start(f32[1,1536,384]{2,1,0:T(8,128)} %param.34) | copy-start | bytes 7077892
  102.7 11.4 %copy-start.35 = (f32[1,1536,384]{2,1,0:T(8,128)S(1)}, f32[1,1536,384]{2,1,0:T(8,128)}, u32[]{:S(2)}) copy-start(f32[1,1536,384]{2,1,0:T(8,128)} %param.35) | copy-start | bytes 7077892
  102.7 11.4 %copy-start.36 = (f32[1,1536,384]{2,1,0:T(8,128)S(1)}, f32[1,1536,384]{2,1,0:T(8,128)}, u32[]{:S(2)}) copy-start(f32[1,1536,384]{2,1,0:T(8,128)} %param.36) | copy-start | bytes 7077892
  102.7 11.3 %copy-start.37 = (bf16[1280,1536]{1,0:T(8,128)(2,1)S(1)}, bf16[1280,1536]{1,0:T(8,128)(2,1)}, u32[]{:S(2)}) copy-start(bf16[1280,1536]{1,0:T(8,128)(2,1)} %get-tuple-element.75) | copy-start | bytes 11796484
  102.7 11.3 %copy-start.38 = (bf16[1280,384]{1,0:T(8,128)(2,1)S(1)}, bf16[1280,384]{1,0:T(8,128)(2,1)}, u32[]{:S(2)}) copy-start(bf16[1280,384]{1,0:T(8,128)(2,1)} %get-tuple-element.76) | copy-start | bytes 2949124
  128.8 3.7 %copy-start.18 = (bf16[32,40,384]{2,1,0:T(8,128)(2,1)}, bf16[32,40,384]{2,1,0:T(8,128)(2,1)S(1)}, u32[]{:S(2)}) copy-start(bf16[32,40,384]{2,1,0:T(8,128)(2,1)S(1)} %all-to-all-done.2) | copy-start | bytes 2949124
  128.8 28.8 %all-to-all-start.3 = ((bf16[32,40,384]{2,1,0:T(8,128)(2,1)}), bf16[32,40,384]{2,1,0:T(8,128)(2,1)S(1)}, u32[]{:S(2)}, u32[]{:S(2)}) async-start(bf16[32,40,384]{2,1,0:T(8,128)(2,1)} %bitcast.74), calls=%async_computation.3 | async-start | bytes 1966080 | tf_op jit(solution)/shard_map/all_to_all | solution.py:285
  132.6 15.8 %copy-start.8 = (bf16[1024,384]{1,0:T(8,128)(2,1)S(1)}, bf16[1024,384]{1,0:T(8,128)(2,1)}, u32[]{:S(2)}) copy-start(bf16[1024,384]{1,0:T(8,128)(2,1)} %tokens_ref.3) | copy-start | bytes 2359300
  132.6 15.8 %copy-start.12 = (f32[8,384]{1,0:T(8,128)S(1)}, f32[8,384]{1,0:T(8,128)}, u32[]{:S(2)}) copy-start(f32[8,384]{1,0:T(8,128)} %get-tuple-element.82.expert_ref) | copy-start | bytes 36868
  148.4 1.1 copy-start.10
  149.6 1.1 copy-start.11
  150.7 3.5 %copy-start.27 = (f32[32,512]{1,0:T(8,128)S(1)}, f32[32,512]{1,0:T(8,128)}, u32[]{:S(2)}) copy-start(f32[32,512]{1,0:T(8,128)} %get-tuple-element.87) | copy-start | bytes 196612
  154.0 18.0 %copy-start.31 = (f32[1,1920]{1,0:T(1,128)S(1)}, f32[1,1920]{1,0:T(1,128)}, u32[]{:S(2)}) copy-start(f32[1,1920]{1,0:T(1,128)} %param.37) | copy-start | bytes 23044
  154.0 18.0 %copy-start.32 = (f32[1,1920]{1,0:T(1,128)S(1)}, f32[1,1920]{1,0:T(1,128)}, u32[]{:S(2)}) copy-start(f32[1,1920]{1,0:T(1,128)} %param.38) | copy-start | bytes 23044
  154.1 18.0 %copy-start.33 = (f32[1,1920]{1,0:T(1,128)S(1)}, f32[1,1920]{1,0:T(1,128)}, u32[]{:S(2)}) copy-start(f32[1,1920]{1,0:T(1,128)} %param.39) | copy-start | bytes 23044
  154.1 18.0 %copy-start.34 = (f32[1,1536]{1,0:T(1,128)S(1)}, f32[1,1536]{1,0:T(1,128)}, u32[]{:S(2)}) copy-start(f32[1,1536]{1,0:T(1,128)} %get-tuple-element.102) | copy-start | bytes 18436
  154.1 2.3 %collective-permute-start.6 = (bf16[16,24,896]{2,1,0:T(8,128)(2,1)S(1)}, bf16[16,24,896]{2,1,0:T(8,128)(2,1)S(1)}, u32[]{:S(2)}, u32[]{:S(2)}) collective-permute-start(bf16[16,24,896]{2,1,0:T(8,128)(2,1)S(1)} %get-tuple-element.86), channel_id=1, source_target_pairs={{0,8},{8,0},{16,24},{24,16},{1,9},{9,1},{17,25},{25,17},{2,10},{10... | collective-permute-start | bytes 2064392 | tf_op jit(solution)/shard_map/ppermute | solution.py:298
  154.2 18.6 %copy-start.1 = (bf16[2,2,4,24,1568]{4,3,2,1,0:T(8,128)(2,1)S(1)}, bf16[2,2,4,24,1568]{4,3,2,1,0:T(8,128)(2,1)}, u32[]{:S(2)}) copy-start(bf16[2,2,4,24,1568]{4,3,2,1,0:T(8,128)(2,1)} %copy-done) | copy-start | bytes 3612676
  154.2 2.2 %collective-permute-start.7 = (f32[32,512]{1,0:T(8,128)S(1)}, f32[32,512]{1,0:T(8,128)S(1)}, u32[]{:S(2)}, u32[]{:S(2)}) collective-permute-start(f32[32,512]{1,0:T(8,128)S(1)} %copy-done.27), channel_id=1, source_target_pairs={{0,8},{1,9},{2,10},{3,11},{4,12},{5,13},{6,14},{7,15},{8,0},{9,1},... | collective-permute-start | bytes 196616 | tf_op jit(solution)/shard_map/ppermute | solution.py:379
  157.7 10.8 %collective-permute-start.10 = (f32[32,512]{1,0:T(8,128)S(1)}, f32[32,512]{1,0:T(8,128)S(1)}, u32[]{:S(2)}, u32[]{:S(2)}) collective-permute-start(f32[32,512]{1,0:T(8,128)S(1)} %add.206), channel_id=1, source_target_pairs={{0,6},{1,7},{2,4},{3,5},{4,2},{5,3},{6,0},{7,1},{8,14},{9,15},{10,... | collective-permute-start | bytes 196616 | tf_op jit(solution)/shard_map/ppermute | solution.py:379
  160.8 7.6 %collective-permute-start.9 = (f32[32,512]{1,0:T(8,128)S(1)}, f32[32,512]{1,0:T(8,128)S(1)}, u32[]{:S(2)}, u32[]{:S(2)}) collective-permute-start(f32[32,512]{1,0:T(8,128)S(1)} %add.206), channel_id=1, source_target_pairs={{0,4},{1,5},{2,6},{3,7},{4,0},{5,1},{6,2},{7,3},{8,12},{9,13},{10,... | collective-permute-start | bytes 196616 | tf_op jit(solution)/shard_map/ppermute | solution.py:379
  160.8 7.6 %collective-permute-start.8 = (f32[32,512]{1,0:T(8,128)S(1)}, f32[32,512]{1,0:T(8,128)S(1)}, u32[]{:S(2)}, u32[]{:S(2)}) collective-permute-start(f32[32,512]{1,0:T(8,128)S(1)} %add.206), channel_id=1, source_target_pairs={{0,2},{1,3},{2,0},{3,1},{4,6},{5,7},{6,4},{7,5},{8,10},{9,11},{10,... | collective-permute-start | bytes 196616 | tf_op jit(solution)/shard_map/ppermute | solution.py:379
  162.1 24.2 %all-to-all-start.4 = ((bf16[16,24,896]{2,1,0:T(8,128)(2,1)}), bf16[16,24,896]{2,1,0:T(8,128)(2,1)S(1)}, u32[]{:S(2)}, u32[]{:S(2)}) async-start(bf16[16,24,896]{2,1,0:T(8,128)(2,1)} %add_convert_fusion), calls=%async_computation.4 | async-start | bytes 1376256 | tf_op jit(solution)/shard_map/all_to_all | solution.py:396
  168.5 12.3 %collective-permute-start.13 = (f32[32,512]{1,0:T(8,128)S(1)}, f32[32,512]{1,0:T(8,128)S(1)}, u32[]{:S(2)}, u32[]{:S(2)}) collective-permute-start(f32[32,512]{1,0:T(8,128)S(1)} %add_add_fusion.1), channel_id=1, source_target_pairs={{0,17},{1,16},{2,19},{3,18},{4,21},{5,20},{6,23},{7,22},{8,25},{9,... | collective-permute-start | bytes 196616 | tf_op jit(solution)/shard_map/ppermute | solution.py:379
  171.4 9.4 %collective-permute-start.12 = (f32[32,512]{1,0:T(8,128)S(1)}, f32[32,512]{1,0:T(8,128)S(1)}, u32[]{:S(2)}, u32[]{:S(2)}) collective-permute-start(f32[32,512]{1,0:T(8,128)S(1)} %add_add_fusion.1), channel_id=1, source_target_pairs={{0,16},{1,17},{2,18},{3,19},{4,20},{5,21},{6,22},{7,23},{8,24},{9,... | collective-permute-start | bytes 196616 | tf_op jit(solution)/shard_map/ppermute | solution.py:379
  171.9 8.9 %collective-permute-start.11 = (f32[32,512]{1,0:T(8,128)S(1)}, f32[32,512]{1,0:T(8,128)S(1)}, u32[]{:S(2)}, u32[]{:S(2)}) collective-permute-start(f32[32,512]{1,0:T(8,128)S(1)} %add_add_fusion.1), channel_id=1, source_target_pairs={{0,1},{1,0},{2,3},{3,2},{4,5},{5,4},{6,7},{7,6},{8,9},{9,8},{10,11... | collective-permute-start | bytes 196616 | tf_op jit(solution)/shard_map/ppermute | solution.py:379
  172.7 1.7 copy-start.2
  174.4 1.4 copy-start.5
  175.8 2.4 %copy-start.4 = (f32[1024,384]{1,0:T(8,128)S(1)}, f32[1024,384]{1,0:T(8,128)}, u32[]{:S(2)}) copy-start(f32[1024,384]{1,0:T(8,128)} %copy-done.3) | copy-start | bytes 4718596
  175.8 2.4 %copy-start.15 = (s32[1,1024]{1,0:T(1,128)S(1)}, s32[1,1024]{1,0:T(1,128)}, u32[]{:S(2)}) copy-start(s32[1,1024]{1,0:T(1,128)} %copy-done.14) | copy-start | bytes 12292
  178.2 3.4 %copy-start.28 = (f32[10380]{0:T(1024)S(1)}, f32[10380]{0:T(1024)}, u32[]{:S(2)}) copy-start(f32[10380]{0:T(1024)} %param.29) | copy-start | bytes 124564
  178.2 3.4 %copy-start.29 = (f32[10380]{0:T(1024)S(1)}, f32[10380]{0:T(1024)}, u32[]{:S(2)}) copy-start(f32[10380]{0:T(1024)} %param.30) | copy-start | bytes 124564
  178.2 8.2 %copy-start.21 = (f32[12,1568]{1,0:T(8,128)S(1)}, f32[12,1568]{1,0:T(8,128)}, u32[]{:S(2)}) copy-start(f32[12,1568]{1,0:T(8,128)} %param.25) | copy-start | bytes 225796
  178.2 8.2 %copy-start.24 = (f32[12,1568]{1,0:T(8,128)S(1)}, f32[12,1568]{1,0:T(8,128)}, u32[]{:S(2)}) copy-start(f32[12,1568]{1,0:T(8,128)} %param.26) | copy-start | bytes 225796
  178.2 8.2 %copy-start.25 = (f32[12,1568]{1,0:T(8,128)S(1)}, f32[12,1568]{1,0:T(8,128)}, u32[]{:S(2)}) copy-start(f32[12,1568]{1,0:T(8,128)} %param.27) | copy-start | bytes 225796

commit v5 on v3

--- a/solution.py
+++ b/solution.py
@@ -1063,11 +1063,11 @@
         expert_kernel,
         grid=(count // block,),
         out_shape=(
-            jax.ShapeDtypeStruct((count, width), jnp.bfloat16),
-            jax.ShapeDtypeStruct((count, width), jnp.bfloat16),
-            jax.ShapeDtypeStruct((count, ff), jnp.bfloat16),
-            jax.ShapeDtypeStruct((count, ff), jnp.bfloat16),
-            jax.ShapeDtypeStruct((count, width), jnp.bfloat16),
+            pltpu.HBM((count, width), jnp.bfloat16),
+            pltpu.HBM((count, width), jnp.bfloat16),
+            pltpu.HBM((count, ff), jnp.bfloat16),
+            pltpu.HBM((count, ff), jnp.bfloat16),
+            pltpu.HBM((count, width), jnp.bfloat16),
             jax.ShapeDtypeStruct((8, width), jnp.float32),
             jax.ShapeDtypeStruct((1, ff), jnp.float32),
         ),
@@ -1091,9 +1091,16 @@
         cost_estimate=pl.CostEstimate(
             flops=8 * count * width * ff, bytes_accessed=16 * 10**6, transcendentals=count * ff
         ),
-        compiler_params=pltpu.CompilerParams(vmem_limit_bytes=VMEM_MOST),
+        compiler_params=pltpu.CompilerParams(vmem_limit_bytes=VMEM_BYTES),
         name="expert",
-    )(rows, cot, first, second, bias_one, vecs)
+    )(
+        pltpu.with_memory_space_constraint(rows, pltpu.HBM),
+        pltpu.with_memory_space_constraint(cot, pltpu.HBM),
+        first,
+        pltpu.with_memory_space_constraint(second, pltpu.HBM),
+        bias_one,
+        vecs,
+    )
 
 
 def offset_coords():

time: 188 us -> 188 us (level)
    unnamed x78 -> x76, local copies, waits for them, and re-layouts: 9.37 us -> 10.4 us
  transfers between devices with their start and end apart: 19 -> 19, of which waited for: 10 -> 10; matrix products, arithmetic and copies ran while one was open for 19% -> 17% of each run, Pallas kernels for 21% -> 21%
where the time goes in v5:
time: 188 us; the launch traced here: 187 us
  Pallas kernels  53.5 us (28%)
  waiting for transfers between devices  50.4 us (27%)
  starting transfers between devices  36.6 us (19%)
  matrix products  21.1 us (11%)
  local copies, waits for them, and re-layouts  12.6 us (7%)
  other arithmetic  11.3 us (6%)
  between operations  1.98 us (1%)
    all_to_all x4, waiting for transfers between devices, trade_rows(): lax.all_to_all(payload, ('wide', 'narrow'), split_axis=0, concat_axis=0,...  37 us
    dot_general x2, matrix products, dot_rows(): lax.dot_general(left, right, contract_rows, preferred_element_type=jnp.fl...  18.4 us
    pallas_call x1, Pallas kernels, call_back(): pl.pallas_call(back_kernel, grid=(count // block,), out_shape=(jax.ShapeD...  15.9 us
    pallas_call x1, Pallas kernels, call_expert(): pl.pallas_call(expert_kernel, grid=(count // block,), out_shape=(pltpu.HB...  15 us
    all_to_all x4, starting transfers between devices, trade_rows(): lax.all_to_all(payload, ('wide', 'narrow'), split_axis=0, concat_axis=0,...  12.8 us
    pallas_call x1, Pallas kernels, call_front(): pl.pallas_call(front_kernel, grid=(count // block,), out_shape=(jax.Shape...  10.5 us
    unnamed x76, local copies, waits for them, and re-layouts  10.4 us
    ppermute x7, starting transfers between devices, swap(): lax.ppermute(value, axis, [(i, i ^ offset) for i in range(lax.axis_size(a...  8.94 us
  transfers between devices with their start and end apart: 19, of which 10 were waited for; matrix products, arithmetic and copies ran while one was open for 17% of the time, Pallas kernels for 21%

profile of v5, /device:TPU:0, one launch (start us, length us, event | category | flops | bytes accessed | tf_op | source)
XLA Modules:
  0.0 187.5 jit_solution(5571453772024770571)
XLA Ops:
  0.7 0.9 convert_element_type.30
  1.6 4.0 %collective-permute-start.2 = (bf16[12,1568]{1,0:T(8,128)(2,1)S(1)}, bf16[12,1568]{1,0:T(8,128)(2,1)S(1)}, u32[]{:S(2)}, u32[]{:S(2)}) collective-permute-start(bf16[12,1568]{1,0:T(8,128)(2,1)S(1)} %convert_element_type.30), channel_id=1, source_target_pairs={{0,4},{1,5},{2,6},{3,7},{4,0},{5,1},{6,2},{7,3},{8,12},{9,13},{10,... | collective-permute-start | bytes 112904 | tf_op jit(solution)/shard_map/ppermute | solution.py:298
  5.6 1.6 collective-permute-start.1
  7.2 1.2 collective-permute-done.2
  8.4 0.9 select_bitcast_fusion.2
  9.3 0.4 collective-permute-done.1
  9.7 3.4 %collective-permute-done = bf16[12,1568]{1,0:T(8,128)(2,1)S(1)} collective-permute-done((bf16[12,1568]{1,0:T(8,128)(2,1)S(1)}, bf16[12,1568]{1,0:T(8,128)(2,1)S(1)}, u32[]{:S(2)}, u32[]{:S(2)}) %collective-permute-start) | collective-permute-done | bytes 37664 | tf_op jit(solution)/shard_map/ppermute | solution.py:298
  13.2 1.6 collective-permute-start.3
  15.4 3.7 %collective-permute-done.3 = bf16[4,12,1568]{2,1,0:T(8,128)(2,1)S(1)} collective-permute-done((bf16[4,12,1568]{2,1,0:T(8,128)(2,1)S(1)}, bf16[4,12,1568]{2,1,0:T(8,128)(2,1)S(1)}, u32[]{:S(2)}, u32[]{:S(2)}) %collective-permute-start.3) | collective-permute-done | bytes 150560 | tf_op jit(solution)/shard_map/ppermute | solution.py:298
  19.1 0.2 maximum_select_fusion.2
  19.3 1.6 collective-permute-start.4
  20.9 1.1 copy-done.6
  22.0 0.7 copy-done.18
  22.7 2.8 %assign.1 = (s32[1,1024]{1,0:T(1,128)S(1)}, bf16[1280,384]{1,0:T(8,128)(2,1)}) custom-call(s32[1]{0:T(128)S(6)} %copy.48.count_ref, s32[1,1024]{1,0:T(1,128)S(1)} %bitcast.69, bf16[1024,384]{1,0:T(8,128)(2,1)S(1)} %copy-done.6), custom_call_target="tpu_custom_call" | custom-call | flops 1006632960 | bytes 4000000 | tf_op jit(solution)/shard_map/assign/pallas_call | solution.py:498
  25.5 3.5 %all-to-all-start = ((bf16[32,40,384]{2,1,0:T(8,128)(2,1)}), bf16[32,40,384]{2,1,0:T(8,128)(2,1)}, u32[]{:S(2)}, u32[]{:S(2)}) async-start(bf16[32,40,384]{2,1,0:T(8,128)(2,1)} %bitcast.14), calls=%async_computation | async-start | bytes 1966080 | tf_op jit(solution)/shard_map/all_to_all | solution.py:285
  29.8 0.3 reshape.286
  30.2 0.7 fusion.17
  31.0 0.6 fusion.10.table_ref
  31.5 1.4 fusion
  32.9 0.2 reshape.288
  33.1 0.3 copy.47
  33.4 0.3 reshape.289.bias_ref
  33.7 1.6 maximum_select_fusion
  35.4 10.5 %front.1 = (bf16[1280,384]{1,0:T(8,128)(2,1)}, f32[1024,384]{1,0:T(8,128)S(1)}, f32[1024,384]{1,0:T(8,128)}, bf16[1024,384]{1,0:T(8,128)(2,1)S(1)}, f32[1024,768...) custom-call(s32[1,1024]{1,0:T(1,128)S(1)} %get-tuple-element.63.dest_ref, ...), custom_call_target="tpu_custom_call" | custom-call | flops 2415919104 | bytes 20000000 | tf_op jit(solution)/shard_map/front/pallas_call | solution.py:609
  45.9 1.2 copy-done.3
  47.1 0.9 copy-done.9
  48.0 7.2 %all-to-all-done = bf16[32,40,384]{2,1,0:T(8,128)(2,1)} async-done(((bf16[32,40,384]{2,1,0:T(8,128)(2,1)}), bf16[32,40,384]{2,1,0:T(8,128)(2,1)}, u32[]{:S(2)}, u32[]{:S(2)}) %all-to-all-start) | async-done | bytes 983072 | tf_op jit(solution)/shard_map/all_to_all | solution.py:285
  55.1 3.5 %all-to-all-start.1 = ((bf16[32,40,384]{2,1,0:T(8,128)(2,1)}), bf16[32,40,384]{2,1,0:T(8,128)(2,1)}, u32[]{:S(2)}, u32[]{:S(2)}) async-start(bf16[32,40,384]{2,1,0:T(8,128)(2,1)} %bitcast.16), calls=%async_computation.1 | async-start | bytes 1966080 | tf_op jit(solution)/shard_map/all_to_all | solution.py:285
  58.7 1.9 %convert_bitcast_fusion.1.first_ref = bf16[384,1536]{1,0:T(8,128)(2,1)S(1)} fusion(f32[1,384,1536]{2,1,0:T(8,128)} %param.31), kind=kLoop, calls=%fused_computation.19 | loop fusion | flops 589824 | bytes 3538944 | tf_op jit(solution)/shard_map/convert_element_type | solution.py:1356
  60.7 0.4 copy-done.20
  61.1 1.1 convert_bitcast_fusion.second_ref
  62.3 0.2 convert_reduce_fusion.1
  62.5 22.2 %all-to-all-done.1 = bf16[32,40,384]{2,1,0:T(8,128)(2,1)} async-done(((bf16[32,40,384]{2,1,0:T(8,128)(2,1)}), bf16[32,40,384]{2,1,0:T(8,128)(2,1)}, u32[]{:S(2)}, u32[]{:S(2)}) %all-to-all-start.1) | async-done | bytes 983072 | tf_op jit(solution)/shard_map/all_to_all | solution.py:285
  84.7 15.0 %expert.1 = (bf16[1280,384]{1,0:T(8,128)(2,1)}, bf16[1280,384]{1,0:T(8,128)(2,1)}, bf16[1280,1536]{1,0:T(8,128)(2,1)}, bf16[1280,1536]{1,0:T(8,128)(2,1)}, bf16[...) custom-call(bf16[1280,384]{1,0:T(8,128)(2,1)} %bitcast.17.rows_ref, ...), custom_call_target="tpu_custom_call" | custom-call | flops 6039797760 | bytes 16000000 | tf_op jit(solution)/shard_map/expert/pallas_call | solution.py:1062
  99.7 0.6 copy-done.12
  100.3 2.9 %all-to-all-start.2 = ((bf16[32,40,384]{2,1,0:T(8,128)(2,1)}), bf16[32,40,384]{2,1,0:T(8,128)(2,1)S(1)}, u32[]{:S(2)}, u32[]{:S(2)}) async-start(bf16[32,40,384]{2,1,0:T(8,128)(2,1)} %bitcast.75), calls=%async_computation.2 | async-start | bytes 1966080 | tf_op jit(solution)/shard_map/all_to_all | solution.py:285
  103.2 11.3 %fusion.29 = (bf16[1,384,1536]{2,1,0:T(8,128)(2,1)}, f32[1,384,1536]{2,1,0:T(8,128)}, f32[1,384,1536]{2,1,0:T(8,128)}, f32[1,384,1536]{2,1,0:T(8,128)}) fusion(f32[1,384,1536]{2,1,0:T(8,128)} %param.31, f32[1,384,1536]{2,1,0:T(8,128)} %param.32, f32[1,384,1536]{2,1,0:T(8,128)} %param.33, bf16[1280,384]{1,0:T(8,128)(2,1)} %bitcast.17.rows_ref, ...), kind=kOutput, calls=%fused_computation.74 | convolution fusion | flops 1519386624 | bytes 20250624 | tf_op jit(solution)/shard_map/dot_general | solution.py:414
  114.6 7.1 %fusion.27 = (bf16[1,1536,384]{2,1,0:T(8,128)(2,1)}, f32[1,1536,384]{2,1,0:T(8,128)}, f32[1,1536,384]{2,1,0:T(8,128)}, f32[1,1536,384]{2,1,0:T(8,128)}) fusion(f32[1,1536,384]{2,1,0:T(8,128)S(1)} %copy-done.21, f32[1,1536,384]{2,1,0:T(8,128)S(1)} %copy-done.34, f32[1,1536,384]{2,1,0:T(8,128)S(1)} %copy-done.35, bf16[1280,1536]{1,0:T(8,128)(2,1)S(1)} %copy-done.36, ...), kind=kOutput, calls=%fused_computation.73 | convolution fusion | flops 1519386624 | bytes 20250624 | tf_op jit(solution)/shard_map/dot_general | solution.py:414
  121.7 7.4 %all-to-all-done.2 = bf16[32,40,384]{2,1,0:T(8,128)(2,1)S(1)} async-done(((bf16[32,40,384]{2,1,0:T(8,128)(2,1)}), bf16[32,40,384]{2,1,0:T(8,128)(2,1)S(1)}, u32[]{:S(2)}, u32[]{:S(2)}) %all-to-all-start.2) | async-done | bytes 983072 | tf_op jit(solution)/shard_map/all_to_all | solution.py:285
  129.1 2.9 %all-to-all-start.3 = ((bf16[32,40,384]{2,1,0:T(8,128)(2,1)}), bf16[32,40,384]{2,1,0:T(8,128)(2,1)S(1)}, u32[]{:S(2)}, u32[]{:S(2)}) async-start(bf16[32,40,384]{2,1,0:T(8,128)(2,1)} %bitcast.74), calls=%async_computation.3 | async-start | bytes 1966080 | tf_op jit(solution)/shard_map/all_to_all | solution.py:285
  132.2 0.6 pad_maximum_fusion.1.net_ref
  132.9 15.9 %back.1 = (f32[1024,384]{1,0:T(8,128)}, bf16[1024,384]{1,0:T(8,128)(2,1)}, bf16[1024,1152]{1,0:T(8,128)(2,1)}, f32[32,512]{1,0:T(8,128)}) custom-call(s32[1]{0:T(128)S(6)} %copy.48.count_ref, s32[1,1024]{1,0:T(1,128)} %copy-done.15, bf16[1280,384]{1,0:T(8,128)(2,1)} %bitcast.70, bf16[1024,384]{1,0:T(8,128)(2,1)} %cot_ref.2, bf16[384,1568]{1,0:T(8,128)(2,1)} %bitcast.66, ...), custom_call_target="tpu_custom_call" | custom-call | flops 3019898880 | bytes 20000000 | tf_op jit(solution)/shard_map/back/pallas_call | solution.py:821
  148.8 1.1 copy-done.10
  149.9 1.1 copy-done.11
  151.1 3.3 %dense.1 = (bf16[16,24,896]{2,1,0:T(8,128)(2,1)S(1)}, f32[16,24,896]{2,1,0:T(8,128)S(1)}) custom-call(s32[2]{0:T(128)S(1)} %pad_add_fusion.place_ref, bf16[1024,384]{1,0:T(8,128)(2,1)S(1)} %copy-done.8, bf16[1024,384]{1,0:T(8,128)(2,1)S(1)} %copy-done.10, bf16[1024,384]{1,0:T(8,128)(2,1)S(1)} %copy-done.11, ...), custom_call_target="tpu_custom_call" | custom-call | flops 1207959552 | bytes 7000000 | tf_op jit(solution)/shard_map/dense/pallas_call | solution.py:911
  154.5 0.5 collective-permute-start.7
  155.0 1.7 collective-permute-done.7
  156.8 1.0 add_convert_fusion
  157.8 0.2 all-to-all-done.3
  157.9 3.2 %collective-permute-start.10 = (f32[32,512]{1,0:T(8,128)S(1)}, f32[32,512]{1,0:T(8,128)S(1)}, u32[]{:S(2)}, u32[]{:S(2)}) collective-permute-start(f32[32,512]{1,0:T(8,128)S(1)} %add.206), channel_id=1, source_target_pairs={{0,6},{1,7},{2,4},{3,5},{4,2},{5,3},{6,0},{7,1},{8,14},{9,15},{10,... | collective-permute-start | bytes 196616 | tf_op jit(solution)/shard_map/ppermute | solution.py:379
  161.1 1.2 collective-permute-start.8
  162.3 6.4 %all-to-all-start.4 = ((bf16[16,24,896]{2,1,0:T(8,128)(2,1)}), bf16[16,24,896]{2,1,0:T(8,128)(2,1)S(1)}, u32[]{:S(2)}, u32[]{:S(2)}) async-start(bf16[16,24,896]{2,1,0:T(8,128)(2,1)} %add_convert_fusion), calls=%async_computation.4 | async-start | bytes 1376256 | tf_op jit(solution)/shard_map/all_to_all | solution.py:396
  168.8 2.9 %collective-permute-start.13 = (f32[32,512]{1,0:T(8,128)S(1)}, f32[32,512]{1,0:T(8,128)S(1)}, u32[]{:S(2)}, u32[]{:S(2)}) collective-permute-start(f32[32,512]{1,0:T(8,128)S(1)} %add_add_fusion.1), channel_id=1, source_target_pairs={{0,17},{1,16},{2,19},{3,18},{4,21},{5,20},{6,23},{7,22},{8,25},{9,... | collective-permute-start | bytes 196616 | tf_op jit(solution)/shard_map/ppermute | solution.py:379
  171.7 0.6 collective-permute-start.12
  172.4 0.7 multiply_subtract_fusion.4
  173.1 1.7 copy-done.2
  174.7 1.4 copy-done.5
  176.1 2.8 %inputs.1 = bf16[1024,384]{1,0:T(8,128)(2,1)} custom-call(f32[1024,384]{1,0:T(8,128)S(1)} %copy-done.5, bf16[1024,1152]{1,0:T(8,128)(2,1)S(1)} %copy-done.2, bf16[384,1568]{1,0:T(8,128)(2,1)S(1)} %bitcast.67), custom_call_target="tpu_custom_call" | custom-call | tf_op jit(solution)/shard_map/inputs/pallas_call | solution.py:938
  179.0 3.1 %layer.1 = bf16[1024,384]{1,0:T(8,128)(2,1)} custom-call(s32[1]{0:T(128)S(6)} %copy.48.count_ref, s32[1,1024]{1,0:T(1,128)S(1)} %copy-done.16, bf16[1280,384]{1,0:T(8,128)(2,1)S(1)} %bitcast.68, f32[1024,384]{1,0:T(8,128)S(1)} %copy-done.4), custom_call_target="tpu_custom_call" | custom-call | tf_op jit(solution)/shard_map/layer/pallas_call | solution.py:967
  182.3 0.1 copy.45
  182.5 0.2 reshape.303
  182.9 0.7 multiply_subtract_fusion.3
  183.6 3.0 %all-to-all-done.4 = bf16[16,24,896]{2,1,0:T(8,128)(2,1)S(1)} async-done(((bf16[16,24,896]{2,1,0:T(8,128)(2,1)}), bf16[16,24,896]{2,1,0:T(8,128)(2,1)S(1)}, u32[]{:S(2)}, u32[]{:S(2)}) %all-to-all-start.4) | async-done | bytes 688160 | tf_op jit(solution)/shard_map/all_to_all | solution.py:396
  186.7 0.8 multiply_subtract_fusion.2
  (124 shorter events, 2.1 us)
Async XLA Ops:
  1.6 6.8 %collective-permute-start.2 = (bf16[12,1568]{1,0:T(8,128)(2,1)S(1)}, bf16[12,1568]{1,0:T(8,128)(2,1)S(1)}, u32[]{:S(2)}, u32[]{:S(2)}) collective-permute-start(bf16[12,1568]{1,0:T(8,128)(2,1)S(1)} %convert_element_type.30), channel_id=1, source_target_pairs={{0,4},{1,5},{2,6},{3,7},{4,0},{5,1},{6,2},{7,3},{8,12},{9,13},{10,... | collective-permute-start | bytes 112904 | tf_op jit(solution)/shard_map/ppermute | solution.py:298
  5.6 4.1 %collective-permute-start.1 = (bf16[12,1568]{1,0:T(8,128)(2,1)S(1)}, bf16[12,1568]{1,0:T(8,128)(2,1)S(1)}, u32[]{:S(2)}, u32[]{:S(2)}) collective-permute-start(bf16[12,1568]{1,0:T(8,128)(2,1)S(1)} %convert_element_type.30), channel_id=1, source_target_pairs={{0,2},{1,3},{2,0},{3,1},{4,6},{5,7},{6,4},{7,5},{8,10},{9,11},{10,... | collective-permute-start | bytes 112904 | tf_op jit(solution)/shard_map/ppermute | solution.py:298
  7.2 5.9 %collective-permute-start = (bf16[12,1568]{1,0:T(8,128)(2,1)S(1)}, bf16[12,1568]{1,0:T(8,128)(2,1)S(1)}, u32[]{:S(2)}, u32[]{:S(2)}) collective-permute-start(bf16[12,1568]{1,0:T(8,128)(2,1)S(1)} %convert_element_type.30), channel_id=1, source_target_pairs={{0,6},{1,7},{2,4},{3,5},{4,2},{5,3},{6,0},{7,1},{8,14},{9,15},{10,... | collective-permute-start | bytes 112904 | tf_op jit(solution)/shard_map/ppermute | solution.py:298
  13.2 5.9 %collective-permute-start.3 = (bf16[4,12,1568]{2,1,0:T(8,128)(2,1)S(1)}, bf16[4,12,1568]{2,1,0:T(8,128)(2,1)S(1)}, u32[]{:S(2)}, u32[]{:S(2)}) collective-permute-start(bf16[4,12,1568]{2,1,0:T(8,128)(2,1)S(1)} %maximum_select_fusion.3), channel_id=1, source_target_pairs={{0,1},{1,0},{2,3},{3,2},{4,5},{5,4},{6,7},{7,6},{8,9},{9,8},{10,11... | collective-permute-start | bytes 451592 | tf_op jit(solution)/shard_map/ppermute | solution.py:298
  19.3 9.9 %collective-permute-start.4 = (bf16[4,24,1568]{2,1,0:T(8,128)(2,1)S(1)}, bf16[4,24,1568]{2,1,0:T(8,128)(2,1)S(1)}, u32[]{:S(2)}, u32[]{:S(2)}) collective-permute-start(bf16[4,24,1568]{2,1,0:T(8,128)(2,1)S(1)} %maximum_select_fusion.2), channel_id=1, source_target_pairs={{0,16},{8,24},{16,0},{24,8},{1,17},{9,25},{17,1},{25,9},{2,18},{10... | collective-permute-start | bytes 903176 | tf_op jit(solution)/shard_map/ppermute | solution.py:298
  20.9 1.1 copy-start.6
  22.0 0.7 copy-start.18
  25.4 9.9 %copy-start.15 = (s32[1,1024]{1,0:T(1,128)}, s32[1,1024]{1,0:T(1,128)S(1)}, u32[]{:S(2)}) copy-start(s32[1,1024]{1,0:T(1,128)S(1)} %get-tuple-element.63.dest_ref) | copy-start | bytes 12292
  25.4 3.8 %copy-start.23 = (f32[10380]{0:T(1024)S(1)}, f32[10380]{0:T(1024)}, u32[]{:S(2)}) copy-start(f32[10380]{0:T(1024)} %param.28) | copy-start | bytes 124564
  25.4 4.3 %slice-start = ((f32[10380]{0:T(1024)}), f32[2688]{0:T(1024)S(1)}, s32[]{:S(2)}) async-start(f32[10380]{0:T(1024)} %param.28), calls=%async_computation.5 | async-start | bytes 24576 | tf_op jit(solution)/shard_map/slice | solution.py:1347
  25.4 4.8 %copy-start.24 = (f32[256,2]{1,0:T(8,128)S(1)}, f32[256,2]{1,0:T(8,128)}, u32[]{:S(2)}) copy-start(f32[256,2]{1,0:T(8,128)} %constant.144.clone.coords_ref) | copy-start | bytes 6148
  25.5 29.7 %all-to-all-start = ((bf16[32,40,384]{2,1,0:T(8,128)(2,1)}), bf16[32,40,384]{2,1,0:T(8,128)(2,1)}, u32[]{:S(2)}, u32[]{:S(2)}) async-start(bf16[32,40,384]{2,1,0:T(8,128)(2,1)} %bitcast.14), calls=%async_computation | async-start | bytes 1966080 | tf_op jit(solution)/shard_map/all_to_all | solution.py:285
  29.8 5.6 %copy-start.17 = (f32[3,1,256]{2,1,0:T(1,128)}, f32[3,1,256]{2,1,0:T(1,128)S(1)}, u32[]{:S(2)}) copy-start(f32[3,1,256]{2,1,0:T(1,128)S(1)} %broadcast_in_dim.7.scale_ref) | copy-start | bytes 9220
  29.8 5.6 %copy-start.14 = (f32[7,384]{1,0:T(8,128)}, f32[7,384]{1,0:T(8,128)S(1)}, u32[]{:S(2)}) copy-start(f32[7,384]{1,0:T(8,128)S(1)} %reshape.285.rows_ref) | copy-start | bytes 32260
  30.1 3.6 %collective-permute-start.5 = (bf16[2,4,24,1568]{3,2,1,0:T(8,128)(2,1)S(1)}, bf16[2,4,24,1568]{3,2,1,0:T(8,128)(2,1)}, u32[]{:S(2)}, u32[]{:S(2)}) collective-permute-start(bf16[2,4,24,1568]{3,2,1,0:T(8,128)(2,1)S(1)} %maximum_select_fusion.1), channel_id=1, source_target_pairs={{0,8},{8,0},{16,24},{24,16},{1,9},{9,1},{17,25},{25,17},{2,10},{10... | collective-permute-start | bytes 1806344 | tf_op jit(solution)/shard_map/ppermute | solution.py:298
  31.5 3.7 %copy-start.27 = (f32[12,256]{1,0:T(8,128)}, f32[12,256]{1,0:T(8,128)S(1)}, u32[]{:S(2)}) copy-start(f32[12,256]{1,0:T(8,128)S(1)} %fusion.10.table_ref) | copy-start | bytes 36868
  33.6 1.8 copy-start.7
  35.4 26.9 %copy-start = (bf16[2,2,4,24,1568]{4,3,2,1,0:T(8,128)(2,1)}, bf16[2,2,4,24,1568]{4,3,2,1,0:T(8,128)(2,1)S(1)}, u32[]{:S(2)}) copy-start(bf16[2,2,4,24,1568]{4,3,2,1,0:T(8,128)(2,1)S(1)} %copy.42) | copy-start | bytes 3612676
  35.4 23.3 %copy-start.31 = (f32[1,1920]{1,0:T(1,128)S(1)}, f32[1,1920]{1,0:T(1,128)}, u32[]{:S(2)}) copy-start(f32[1,1920]{1,0:T(1,128)} %param.37) | copy-start | bytes 23044
  45.9 1.2 copy-start.3
  47.1 0.9 copy-start.9
  55.1 29.5 %all-to-all-start.1 = ((bf16[32,40,384]{2,1,0:T(8,128)(2,1)}), bf16[32,40,384]{2,1,0:T(8,128)(2,1)}, u32[]{:S(2)}, u32[]{:S(2)}) async-start(bf16[32,40,384]{2,1,0:T(8,128)(2,1)} %bitcast.16), calls=%async_computation.1 | async-start | bytes 1966080 | tf_op jit(solution)/shard_map/all_to_all | solution.py:285
  58.7 2.4 %copy-start.20 = (f32[1,1536,384]{2,1,0:T(8,128)S(1)}, f32[1,1536,384]{2,1,0:T(8,128)}, u32[]{:S(2)}) copy-start(f32[1,1536,384]{2,1,0:T(8,128)} %param.34) | copy-start | bytes 7077892
  61.1 1.4 slice-start.1
  99.7 0.6 copy-start.12
  100.3 28.8 %all-to-all-start.2 = ((bf16[32,40,384]{2,1,0:T(8,128)(2,1)}), bf16[32,40,384]{2,1,0:T(8,128)(2,1)S(1)}, u32[]{:S(2)}, u32[]{:S(2)}) async-start(bf16[32,40,384]{2,1,0:T(8,128)(2,1)} %bitcast.75), calls=%async_computation.2 | async-start | bytes 1966080 | tf_op jit(solution)/shard_map/all_to_all | solution.py:285
  103.1 11.4 %copy-start.21 = (f32[1,1536,384]{2,1,0:T(8,128)S(1)}, f32[1,1536,384]{2,1,0:T(8,128)}, u32[]{:S(2)}) copy-start(f32[1,1536,384]{2,1,0:T(8,128)} %param.34) | copy-start | bytes 7077892
  103.2 11.4 %copy-start.34 = (f32[1,1536,384]{2,1,0:T(8,128)S(1)}, f32[1,1536,384]{2,1,0:T(8,128)}, u32[]{:S(2)}) copy-start(f32[1,1536,384]{2,1,0:T(8,128)} %param.35) | copy-start | bytes 7077892
  103.2 11.4 %copy-start.35 = (f32[1,1536,384]{2,1,0:T(8,128)S(1)}, f32[1,1536,384]{2,1,0:T(8,128)}, u32[]{:S(2)}) copy-start(f32[1,1536,384]{2,1,0:T(8,128)} %param.36) | copy-start | bytes 7077892
  103.2 11.4 %copy-start.36 = (bf16[1280,1536]{1,0:T(8,128)(2,1)S(1)}, bf16[1280,1536]{1,0:T(8,128)(2,1)}, u32[]{:S(2)}) copy-start(bf16[1280,1536]{1,0:T(8,128)(2,1)} %get-tuple-element.75) | copy-start | bytes 11796484
  103.2 11.4 %copy-start.37 = (bf16[1280,384]{1,0:T(8,128)(2,1)S(1)}, bf16[1280,384]{1,0:T(8,128)(2,1)}, u32[]{:S(2)}) copy-start(bf16[1280,384]{1,0:T(8,128)(2,1)} %get-tuple-element.76) | copy-start | bytes 2949124
  129.1 3.8 %copy-start.19 = (bf16[32,40,384]{2,1,0:T(8,128)(2,1)}, bf16[32,40,384]{2,1,0:T(8,128)(2,1)S(1)}, u32[]{:S(2)}) copy-start(bf16[32,40,384]{2,1,0:T(8,128)(2,1)S(1)} %all-to-all-done.2) | copy-start | bytes 2949124
  129.1 28.8 %all-to-all-start.3 = ((bf16[32,40,384]{2,1,0:T(8,128)(2,1)}), bf16[32,40,384]{2,1,0:T(8,128)(2,1)S(1)}, u32[]{:S(2)}, u32[]{:S(2)}) async-start(bf16[32,40,384]{2,1,0:T(8,128)(2,1)} %bitcast.74), calls=%async_computation.3 | async-start | bytes 1966080 | tf_op jit(solution)/shard_map/all_to_all | solution.py:285
  132.9 15.9 %copy-start.8 = (bf16[1024,384]{1,0:T(8,128)(2,1)S(1)}, bf16[1024,384]{1,0:T(8,128)(2,1)}, u32[]{:S(2)}) copy-start(bf16[1024,384]{1,0:T(8,128)(2,1)} %tokens_ref.3) | copy-start | bytes 2359300
  132.9 15.9 %copy-start.13 = (f32[8,384]{1,0:T(8,128)S(1)}, f32[8,384]{1,0:T(8,128)}, u32[]{:S(2)}) copy-start(f32[8,384]{1,0:T(8,128)} %copy-done.12) | copy-start | bytes 36868
  148.8 1.1 copy-start.10
  149.9 1.1 copy-start.11
  151.1 3.5 %copy-start.28 = (f32[32,512]{1,0:T(8,128)S(1)}, f32[32,512]{1,0:T(8,128)}, u32[]{:S(2)}) copy-start(f32[32,512]{1,0:T(8,128)} %get-tuple-element.87) | copy-start | bytes 196612
  154.4 18.0 %copy-start.32 = (f32[1,1920]{1,0:T(1,128)S(1)}, f32[1,1920]{1,0:T(1,128)}, u32[]{:S(2)}) copy-start(f32[1,1920]{1,0:T(1,128)} %param.38) | copy-start | bytes 23044
  154.4 18.0 %copy-start.33 = (f32[1,1920]{1,0:T(1,128)S(1)}, f32[1,1920]{1,0:T(1,128)}, u32[]{:S(2)}) copy-start(f32[1,1920]{1,0:T(1,128)} %param.39) | copy-start | bytes 23044
  154.4 2.3 %collective-permute-start.6 = (bf16[16,24,896]{2,1,0:T(8,128)(2,1)S(1)}, bf16[16,24,896]{2,1,0:T(8,128)(2,1)S(1)}, u32[]{:S(2)}, u32[]{:S(2)}) collective-permute-start(bf16[16,24,896]{2,1,0:T(8,128)(2,1)S(1)} %get-tuple-element.86), channel_id=1, source_target_pairs={{0,8},{8,0},{16,24},{24,16},{1,9},{9,1},{17,25},{25,17},{2,10},{10... | collective-permute-start | bytes 2064392 | tf_op jit(solution)/shard_map/ppermute | solution.py:298
  154.5 18.5 %copy-start.1 = (bf16[2,2,4,24,1568]{4,3,2,1,0:T(8,128)(2,1)S(1)}, bf16[2,2,4,24,1568]{4,3,2,1,0:T(8,128)(2,1)}, u32[]{:S(2)}) copy-start(bf16[2,2,4,24,1568]{4,3,2,1,0:T(8,128)(2,1)} %copy-done) | copy-start | bytes 3612676
  154.5 2.2 %collective-permute-start.7 = (f32[32,512]{1,0:T(8,128)S(1)}, f32[32,512]{1,0:T(8,128)S(1)}, u32[]{:S(2)}, u32[]{:S(2)}) collective-permute-start(f32[32,512]{1,0:T(8,128)S(1)} %copy-done.28), channel_id=1, source_target_pairs={{0,8},{1,9},{2,10},{3,11},{4,12},{5,13},{6,14},{7,15},{8,0},{9,1},... | collective-permute-start | bytes 196616 | tf_op jit(solution)/shard_map/ppermute | solution.py:379
  157.9 10.8 %collective-permute-start.10 = (f32[32,512]{1,0:T(8,128)S(1)}, f32[32,512]{1,0:T(8,128)S(1)}, u32[]{:S(2)}, u32[]{:S(2)}) collective-permute-start(f32[32,512]{1,0:T(8,128)S(1)} %add.206), channel_id=1, source_target_pairs={{0,6},{1,7},{2,4},{3,5},{4,2},{5,3},{6,0},{7,1},{8,14},{9,15},{10,... | collective-permute-start | bytes 196616 | tf_op jit(solution)/shard_map/ppermute | solution.py:379
  161.1 7.6 %collective-permute-start.9 = (f32[32,512]{1,0:T(8,128)S(1)}, f32[32,512]{1,0:T(8,128)S(1)}, u32[]{:S(2)}, u32[]{:S(2)}) collective-permute-start(f32[32,512]{1,0:T(8,128)S(1)} %add.206), channel_id=1, source_target_pairs={{0,4},{1,5},{2,6},{3,7},{4,0},{5,1},{6,2},{7,3},{8,12},{9,13},{10,... | collective-permute-start | bytes 196616 | tf_op jit(solution)/shard_map/ppermute | solution.py:379
  161.1 7.7 %collective-permute-start.8 = (f32[32,512]{1,0:T(8,128)S(1)}, f32[32,512]{1,0:T(8,128)S(1)}, u32[]{:S(2)}, u32[]{:S(2)}) collective-permute-start(f32[32,512]{1,0:T(8,128)S(1)} %add.206), channel_id=1, source_target_pairs={{0,2},{1,3},{2,0},{3,1},{4,6},{5,7},{6,4},{7,5},{8,10},{9,11},{10,... | collective-permute-start | bytes 196616 | tf_op jit(solution)/shard_map/ppermute | solution.py:379
  162.3 24.2 %all-to-all-start.4 = ((bf16[16,24,896]{2,1,0:T(8,128)(2,1)}), bf16[16,24,896]{2,1,0:T(8,128)(2,1)S(1)}, u32[]{:S(2)}, u32[]{:S(2)}) async-start(bf16[16,24,896]{2,1,0:T(8,128)(2,1)} %add_convert_fusion), calls=%async_computation.4 | async-start | bytes 1376256 | tf_op jit(solution)/shard_map/all_to_all | solution.py:396
  168.8 13.3 %collective-permute-start.13 = (f32[32,512]{1,0:T(8,128)S(1)}, f32[32,512]{1,0:T(8,128)S(1)}, u32[]{:S(2)}, u32[]{:S(2)}) collective-permute-start(f32[32,512]{1,0:T(8,128)S(1)} %add_add_fusion.1), channel_id=1, source_target_pairs={{0,17},{1,16},{2,19},{3,18},{4,21},{5,20},{6,23},{7,22},{8,25},{9,... | collective-permute-start | bytes 196616 | tf_op jit(solution)/shard_map/ppermute | solution.py:379
  171.7 10.5 %collective-permute-start.12 = (f32[32,512]{1,0:T(8,128)S(1)}, f32[32,512]{1,0:T(8,128)S(1)}, u32[]{:S(2)}, u32[]{:S(2)}) collective-permute-start(f32[32,512]{1,0:T(8,128)S(1)} %add_add_fusion.1), channel_id=1, source_target_pairs={{0,16},{1,17},{2,18},{3,19},{4,20},{5,21},{6,22},{7,23},{8,24},{9,... | collective-permute-start | bytes 196616 | tf_op jit(solution)/shard_map/ppermute | solution.py:379
  172.3 9.9 %collective-permute-start.11 = (f32[32,512]{1,0:T(8,128)S(1)}, f32[32,512]{1,0:T(8,128)S(1)}, u32[]{:S(2)}, u32[]{:S(2)}) collective-permute-start(f32[32,512]{1,0:T(8,128)S(1)} %add_add_fusion.1), channel_id=1, source_target_pairs={{0,1},{1,0},{2,3},{3,2},{4,5},{5,4},{6,7},{7,6},{8,9},{9,8},{10,11... | collective-permute-start | bytes 196616 | tf_op jit(solution)/shard_map/ppermute | solution.py:379
  173.0 1.7 copy-start.2
  174.7 1.4 copy-start.5
  176.1 2.9 %copy-start.4 = (f32[1024,384]{1,0:T(8,128)S(1)}, f32[1024,384]{1,0:T(8,128)}, u32[]{:S(2)}) copy-start(f32[1024,384]{1,0:T(8,128)} %copy-done.3) | copy-start | bytes 4718596
  176.1 2.9 %copy-start.16 = (s32[1,1024]{1,0:T(1,128)S(1)}, s32[1,1024]{1,0:T(1,128)}, u32[]{:S(2)}) copy-start(s32[1,1024]{1,0:T(1,128)} %copy-done.15) | copy-start | bytes 12292
  179.0 3.9 %copy-start.29 = (f32[10380]{0:T(1024)S(1)}, f32[10380]{0:T(1024)}, u32[]{:S(2)}) copy-start(f32[10380]{0:T(1024)} %param.29) | copy-start | bytes 124564
  179.0 3.9 %copy-start.30 = (f32[10380]{0:T(1024)S(1)}, f32[10380]{0:T(1024)}, u32[]{:S(2)}) copy-start(f32[10380]{0:T(1024)} %param.30) | copy-start | bytes 124564
  179.0 7.7 %copy-start.22 = (f32[12,1568]{1,0:T(8,128)S(1)}, f32[12,1568]{1,0:T(8,128)}, u32[]{:S(2)}) copy-start(f32[12,1568]{1,0:T(8,128)} %param.25) | copy-start | bytes 225796
  179.0 7.7 %copy-start.25 = (f32[12,1568]{1,0:T(8,128)S(1)}, f32[12,1568]{1,0:T(8,128)}, u32[]{:S(2)}) copy-start(f32[12,1568]{1,0:T(8,128)} %param.26) | copy-start | bytes 225796
  179.0 7.7 %copy-start.26 = (f32[12,1568]{1,0:T(8,128)S(1)}, f32[12,1568]{1,0:T(8,128)}, u32[]{:S(2)}) copy-start(f32[12,1568]{1,0:T(8,128)} %param.27) | copy-start | bytes 225796
